TPU v7x, 512 devices: a whole 4x8x8 slice. The times are simulated.
512 devices in a mesh: blk: 64 (over y, z_hi, core), head: 8 (over z_lo, x).
Axes of the slice: x: 4, y: 8, z: 8 (z_hi: 4, z_lo: 2; z = z_hi * 2 + z_lo), core: 2. Of those that a mesh axis runs over, the one named last changes fastest.
Arguments:
- query_nope: bfloat16 [4096, 8192], P('blk', 'head'), may hold values from -140 to 140
- query_rope: bfloat16 [4096, 4096], P('blk', 'head'), may hold values from -6 to 6
- compressed: bfloat16 [4096, 576], P(('blk', 'head')), may hold values from -6 to 6
- latent_gain: float32 [512], replicated, may hold values from 0.1 to 1.9
- key_up: bfloat16 [64, 128, 512], P('head'), may hold values from -0.5 to 0.5
- value_up: bfloat16 [64, 512, 128], P('head'), may hold values from -1.5 to 1.5
- span_order: int32 [128], replicated, may hold values from 0 to 127, each once
Outputs:
- attended: bfloat16 [4096, 8192], P('blk', 'head')
Inputs may be any that keep to these rules, and one draw needn't show every extreme that they name: Every number appears once; device index i of blk holds the blocks span_order[2 i] and span_order[2 i + 1].
All inputs are finite; a program needn't handle non-finite values.
Results may differ from a plain program's by a relative error of at most 0.0075.
The roundings to bfloat16 on the way count: a program that leaves them out, or rounds other values in their place, can miss the bound.
Values may be sent and summed in bfloat16 or wider, within the bound.
No kernel may reach another device: no remote copies, remote signals or barrier semaphores. Data moves between devices by JAX's collectives and lax.ppermute only.
A program may use at most 64 MiB of HBM per device.

v0:
```python
import jax
import jax.numpy as jnp
from jax import lax
from jax.sharding import Mesh
from jax.sharding import PartitionSpec as P

BLK = ("blk_0", "blk_1", "blk_2")
BLK_HEAD = ("blk_0", "blk_1", "blk_2", "head")


norm_epsilon = 1e-06
rope_base = 10000.0
masked_score = -1e30


def joined_along(parts, dim):
    parts = jnp.moveaxis(parts, 0, dim)
    dims = parts.shape
    return parts.reshape(*dims[:dim], dims[dim] * dims[dim + 1], *dims[dim + 2 :])


def from_everyone(value, axis):
    size = lax.axis_size(axis)
    return lax.all_to_all(
        jnp.broadcast_to(value[None], (size, *value.shape)), axis, 0, 0, tiled=True
    )


def collect(value, axis, dim):
    return joined_along(from_everyone(value, axis), dim)


def stacked_from(value, axes, order):
    parts = value[None]
    for k in order:
        parts = lax.all_gather(parts, axes[k], axis=0, tiled=True)
    block = [lax.axis_size(axes[k]) for k in reversed(order)]
    parts = parts.reshape(*block, *value.shape)
    turned = sorted(range(len(order)), key=lambda place: order[len(order) - 1 - place])
    return parts.transpose(*turned, *range(len(order), parts.ndim)).reshape(-1, *value.shape)


def whole_of(value, axes, order, dim):
    return joined_along(stacked_from(value, axes, order), dim)


def lookup(entries, index_array):
    slots = jnp.arange(entries.shape[0], dtype=jnp.int32)
    matches = index_array[..., None] == slots
    return jnp.sum(jnp.where(matches, entries, 0), axis=-1)


def rotate(values, positions):
    half_width = values.shape[-1] // 2
    frequency = rope_base ** (-jnp.arange(half_width, dtype=jnp.float32) / half_width)
    angles = positions.astype(jnp.float32)[..., None] * frequency
    cosine = jnp.cos(angles)
    sine_value = jnp.sin(angles)
    leading = values[..., :half_width]
    trailing = values[..., half_width:]
    return jnp.concatenate(
        [leading * cosine - trailing * sine_value, leading * sine_value + trailing * cosine],
        axis=-1,
    )


def shards(query_nope, query_rope, compressed, latent_gain, key_up, value_up, span_order):
    tokens_here = query_nope.shape[0]
    heads_here = key_up.shape[0]
    nope_width = key_up.shape[1]
    latent_width = key_up.shape[2]
    rope_width = query_rope.shape[1] // heads_here
    value_width = value_up.shape[2]
    half_block = tokens_here // 2
    slice_count = compressed.shape[0]
    block_id = lax.axis_index(BLK)
    head_id = lax.axis_index("head")

    def positions_of(row_ids):
        return lookup(span_order, row_ids // half_block) * half_block + row_ids % half_block

    query_pos = positions_of(block_id * tokens_here + jnp.arange(tokens_here, dtype=jnp.int32))
    own_rows = (
        block_id * tokens_here + head_id * slice_count + jnp.arange(slice_count, dtype=jnp.int32)
    )
    own_pos = positions_of(own_rows)
    latent = compressed[:, :latent_width].astype(jnp.float32)
    latent = (
        latent
        * lax.rsqrt(jnp.mean(latent * latent, axis=1, keepdims=True) + norm_epsilon)
        * latent_gain
    )
    latent = latent.astype(jnp.bfloat16)
    key_rot = rotate(compressed[:, latent_width:].astype(jnp.float32), own_pos).astype(jnp.bfloat16)
    key_rows = jnp.concatenate([latent, key_rot], axis=1)
    nope_parts = query_nope.reshape(tokens_here, heads_here, nope_width)
    query_lat = jnp.einsum(
        "thn,hnl->thl", nope_parts, key_up, preferred_element_type=jnp.float32
    ).astype(jnp.bfloat16)
    query_rot = rotate(
        query_rope.reshape(tokens_here, heads_here, rope_width).astype(jnp.float32),
        query_pos[:, None],
    ).astype(jnp.bfloat16)
    row_count = tokens_here * heads_here
    queries = jnp.concatenate([query_lat, query_rot], axis=2).reshape(
        row_count, latent_width + rope_width
    )
    query_rows_pos = jnp.repeat(query_pos, heads_here)
    score_scale = (nope_width + rope_width) ** (-0.5)
    block_keys = collect(key_rows, "head", 0)
    shard_keys = whole_of(block_keys, BLK, (1, 0, 2), 0)
    row_ids = jnp.arange(shard_keys.shape[0], dtype=jnp.int32)
    run_max = jnp.full((row_count,), masked_score, jnp.float32)
    scores = (
        jnp.einsum("qd,kd->qk", queries, shard_keys, preferred_element_type=jnp.float32)
        * score_scale
    )
    visible = positions_of(row_ids)[None, :] <= query_rows_pos[:, None]
    scores = jnp.where(visible, scores, masked_score)
    new_max = jnp.maximum(run_max, jnp.max(scores, axis=1))
    weight = jnp.where(visible, jnp.exp(scores - new_max[:, None]), 0.0)
    new_sum = jnp.sum(weight, axis=1)
    product = jnp.dot(
        weight.astype(jnp.bfloat16),
        shard_keys[:, :latent_width],
        preferred_element_type=jnp.float32,
    )
    folded = (new_max, new_sum, product)
    run_max, run_sum, run_acc = folded
    lat_out = (
        (run_acc / run_sum[:, None])
        .astype(jnp.bfloat16)
        .reshape(tokens_here, heads_here, latent_width)
    )
    attended = jnp.einsum(
        "thl,hlv->thv", lat_out, value_up, preferred_element_type=jnp.float32
    ).astype(jnp.bfloat16)
    return attended.reshape(tokens_here, heads_here * value_width)


def solution(mesh):
    split = Mesh(
        mesh.devices.reshape(8, 4, 2, mesh.shape["head"]), ("blk_0", "blk_1", "blk_2", "head")
    )
    placed = (
        P(BLK, "head"),
        P(BLK, "head"),
        P(BLK_HEAD, None),
        P(),
        P("head", None, None),
        P("head", None, None),
        P(),
    )
    return jax.shard_map(
        shards, mesh=split, in_specs=placed, out_specs=P(BLK, "head"), check_vma=False
    )
```

profile of v0, /device:TPU:1, one launch (start us, length us, event | category | flops | bytes accessed | tf_op | source)
XLA Modules:
  0.0 131.8 jit_solution(17058499181964433245)
XLA Ops:
  6.6 0.9 fusion.34
  7.5 0.7 slice_convert_fusion
  8.2 0.8 select_reduce_fusion.2
  9.0 0.8 fusion.36
  9.8 0.1 fusion.44
  10.0 11.7 %all_to_all.5 = bf16[8,8,576]{2,1,0:T(8,128)(2,1)S(1)} all-to-all(bf16[8,8,576]{2,1,0:T(8,128)(2,1)S(1)} %broadcast_in_dim.66), channel_id=1, replica_groups=mesh['blk_0'=8,'blk_1'=4,'blk_2'=2,'head'=8] {'head'}, dimensions={0} | all-to-all | bytes 147456 | tf_op jit(solution)/shard_map/all_to_all | solution.py:24
  21.7 18.8 %all_gather.9 = bf16[4,64,576]{2,1,0:T(8,128)(2,1)} all-gather(bf16[1,64,576]{2,1,0:T(8,128)(2,1)S(1)} %bitcast.33), channel_id=1, replica_groups=mesh['blk_0'=8,'blk_1'=4,'blk_2'=2,'head'=8] {'blk_1'}, dimensions={0}, use_global_device_ids=true | all-gather | bytes 368640 | tf_op jit(solution)/shard_map/all_gather | solution.py:36
  40.6 42.2 %all-gather.3.cloned.1.call-done = bf16[32,64,576]{2,1,0:T(8,128)(2,1)} async-done(((bf16[4,64,576]{2,1,0:T(8,128)(2,1)}), bf16[32,64,576]{2,1,0:T(8,128)(2,1)}) %all-gather.3.cloned.1.call-update) | async-done | bytes 2359312 | tf_op jit(solution)/shard_map/all_gather | solution.py:36
  82.8 0.8 select_reduce_fusion.1
  83.8 0.1 le.16
  83.9 1.0 reshape.213
  84.9 0.2 multiply_cosine_fusion
  85.1 0.1 fusion.55
  85.2 0.1 subtract_convert_fusion
  85.3 1.2 fusion.11
  86.5 0.1 pad_maximum_fusion
  86.7 1.3 select_reduce_fusion
  88.0 23.6 %all-gather.5.cloned.1.call-done = bf16[64,64,576]{2,1,0:T(8,128)(2,1)} async-done(((bf16[32,64,576]{2,1,0:T(8,128)(2,1)}), bf16[64,64,576]{2,1,0:T(8,128)(2,1)}) %all-gather.5.cloned.1.call-update) | async-done | bytes 4718608 | tf_op jit(solution)/shard_map/all_gather | solution.py:36
  111.6 3.0 %copy.34 = bf16[8,4,2,64,576]{4,3,2,1,0:T(8,128)(2,1)S(1)} copy(bf16[8,4,2,64,576]{4,3,1,0,2:T(8,128)(2,1)} %bitcast.30) | data formatting | bytes 9437184 | tf_op jit(solution)/shard_map/transpose | solution.py:40
  114.7 4.0 %fusion = (f32[512]{0:T(512)S(1)}, f32[512,4096]{1,0:T(8,128)S(1)}) fusion(s32[4096]{0:T(1024)S(1)} %fusion.37, s32[512]{0:T(512)S(1)} %le.16, bf16[4096,576]{1,0:T(8,128)(2,1)S(1)} %bitcast.31, bf16[64,8,576]{2,0,1:T(8,128)(2,1)S(1)} %pad_maximum_fusion), kind=kOutput, calls=%fused_computation.2 | convolution fusion | flops 2424307200 | bytes 13717504 | tf_op jit(solution)/shard_map/qd,kd->qk/dot_general | solution.py:115
  118.7 2.6 %fusion.1 = f32[512]{0:T(512)S(1)} fusion(f32[512,4096]{1,0:T(8,128)S(1)} %get-tuple-element.16, f32[512]{0:T(512)S(1)} %broadcast_maximum_fusion, s32[4096]{0:T(1024)S(1)} %fusion.37, s32[512]{0:T(512)S(1)} %le.16), kind=kLoop, calls=%fused_computation.3 | loop fusion | flops 12582400 | bytes 8411136 | tf_op jit(solution)/shard_map/reduce_sum | solution.py:122
  121.3 2.6 %fusion.17 = bf16[64,8,512]{2,1,0:T(8,128)(2,1)S(1)} fusion(bf16[4096,576]{1,0:T(8,128)(2,1)S(1)} %bitcast.32, f32[512,4096]{1,0:T(8,128)S(1)} %get-tuple-element.16, f32[512]{0:T(512)S(1)} %broadcast_maximum_fusion, s32[4096]{0:T(1024)S(1)} %fusion.37, s32[512]{0:T(512)S(1)} %le.16, f32[512]{0:T(512)S(1)} %fusion.1), kind=kOutput, calls=%fused_computation.19 | convolution fusion | flops 2160590848 | bytes 13129728 | tf_op jit(solution)/shard_map/dot_general | solution.py:123
  123.9 0.4 fusion.12
  124.3 0.7 copy.58
  (22 shorter events, 0.3 us)
Async XLA Ops:
  6.5 78.8 %copy-start = (bf16[8,128,512]{2,1,0:T(8,128)(2,1)S(1)}, bf16[8,128,512]{2,1,0:T(8,128)(2,1)}, u32[]{:S(2)}) copy-start(bf16[8,128,512]{2,1,0:T(8,128)(2,1)} %param.11) | copy-start | bytes 3145732
  6.5 80.1 %copy-start.2 = (s32[128]{0:T(128)S(1)}, s32[128]{0:T(128)}, u32[]{:S(2)}) copy-start(s32[128]{0:T(128)} %param.13) | copy-start | bytes 1540
  6.5 76.3 %all-gather.3.cloned.1.call-start = ((), (), s32[]{:S(2)}) async-start(), calls=%async_computation.1 | async-start | bytes 2949120 | tf_op jit(solution)/shard_map/all_gather | solution.py:36
  40.5 71.1 %all-gather.5.cloned.1.call-start = ((), (), s32[]{:S(2)}) async-start(), calls=%async_computation.2 | async-start | bytes 7864320 | tf_op jit(solution)/shard_map/all_gather | solution.py:36
  121.3 2.6 %copy-start.1 = (bf16[8,512,128]{2,1,0:T(8,128)(2,1)S(1)}, bf16[8,512,128]{2,1,0:T(8,128)(2,1)}, u32[]{:S(2)}) copy-start(bf16[8,512,128]{2,1,0:T(8,128)(2,1)} %param.12) | copy-start | bytes 3145732
Sparse Core Ops, SparseCore 0:
  40.6 42.1 all-gather.2
  84.9 26.6 all-gather.4
where the time goes:
time: 132 us
  waiting for transfers between devices  65.9 us (50%)
  blocking collectives  30.5 us (23%)
  between operations  13.5 us (10%)
  other arithmetic  8.63 us (7%)
  matrix products  8.16 us (6%)
  local copies, waits for them, and re-layouts  5.02 us (4%)
    all_gather x2, waiting for transfers between devices, stacked_from(): parts = lax.all_gather(parts, axes[k], axis=0, tiled=True)  65.9 us
    all_gather x1, blocking collectives, stacked_from(): parts = lax.all_gather(parts, axes[k], axis=0, tiled=True)  18.8 us
    all_to_all x1, blocking collectives, from_everyone(): lax.all_to_all(jnp.broadcast_to(value[None], (size, *value.shape)), axis,...  11.7 us
    dot_general x1, matrix products, shards(): jnp.einsum('qd,kd->qk', queries, shard_keys, preferred_element_type=jnp.f...  4.03 us
    transpose x1, local copies, waits for them, and re-layouts, stacked_from(): parts.transpose(*turned, *range(len(order), parts.ndim))  3.05 us
    reduce_sum x3, other arithmetic, lookup(): return jnp.sum(jnp.where(matches, entries, 0), axis=-1)  2.95 us
  transfers between devices with their start and end apart: 2, of which 2 were waited for; matrix products, arithmetic and copies ran while one was open for 4% of the time, Pallas kernels for 0%

commit v1 on v0

v1 whole, which is shorter than its diff:
```python
import functools

import jax
import jax.numpy as jnp
import numpy as np
from jax import lax
from jax.experimental import pallas as pl
from jax.experimental.pallas import tpu as pltpu
from jax.sharding import Mesh
from jax.sharding import PartitionSpec as P

AXES = ("y", "zh", "c", "zl", "x")
BLK = ("y", "zh", "c")
HEAD = ("zl", "x")
PLANE = ("y", "zh", "zl")
NY, NZH, NC, NZL, NX = 8, 4, 2, 2, 4

LATENT = 512
ROPE = 64
NOPE = 128
VDIM = 128
HEADS_HERE = 8
TOK = 64
HALF = 32
WIDE = 640
ROWS = TOK * HEADS_HERE
CHUNK = 256

norm_epsilon = 1e-06
rope_base = 10000.0
masked_score = -1e30
score_scale = (NOPE + ROPE) ** (-0.5)
log2e = 1.4426950408889634

FREQUENCY = np.tile(
    np.float32(rope_base) ** (-np.arange(ROPE // 2, dtype=np.float32) / np.float32(ROPE // 2)),
    128 // (ROPE // 2),
).astype(np.float32)[None]

VMEM = pl.BlockSpec(memory_space=pltpu.VMEM)
SMEM = pl.BlockSpec(memory_space=pltpu.SMEM)


def lanes_of(shape):
    return lax.broadcasted_iota(jnp.int32, shape, 1)


def rotated(values, positions, frequency):
    lane = lanes_of(values.shape)
    leading = lane % ROPE < ROPE // 2
    angles = positions * frequency
    cosine = jnp.cos(angles)
    sine_value = jnp.where(leading, -jnp.sin(angles), jnp.sin(angles))
    return cosine, sine_value, leading


def apply_rotation(values, cosine, sine_value, leading):
    swapped = jnp.where(
        leading,
        pltpu.roll(values, 128 - ROPE // 2, 1),
        pltpu.roll(values, ROPE // 2, 1),
    )
    return values * cosine + swapped * sine_value


def block_index():
    return (lax.axis_index("y") * NZH + lax.axis_index("zh")) * NC + lax.axis_index("c")


def prep_kernel(span_ref, compressed_ref, gain_ref, frequency_ref, out_ref):
    rows = compressed_ref.shape[0]
    block = block_index()
    x = lax.axis_index("x")
    span = span_ref[block * 2 + lax.axis_index("zl")]
    offset = x * rows + lax.broadcasted_iota(jnp.int32, (rows, 128), 0)
    latent = compressed_ref[:, :LATENT].astype(jnp.float32)
    scale = lax.rsqrt(jnp.mean(latent * latent, axis=1, keepdims=True) + norm_epsilon)
    latent = (latent * scale * gain_ref[...]).astype(jnp.bfloat16)
    rope = compressed_ref[:, LATENT:].astype(jnp.float32)
    rope = jnp.concatenate([rope, jnp.zeros_like(rope)], axis=1)
    positions = (span * HALF + offset).astype(jnp.float32)
    cosine, sine_value, leading = rotated(rope, positions, frequency_ref[...])
    turned = apply_rotation(rope, cosine, sine_value, leading)
    lane = lanes_of((rows, 128))
    tail = jnp.where(
        lane < ROPE,
        turned,
        jnp.where(
            lane == ROPE,
            span.astype(jnp.float32),
            jnp.where(lane == ROPE + 1, offset.astype(jnp.float32), 0.0),
        ),
    ).astype(jnp.bfloat16)
    row = jnp.concatenate([latent, tail], axis=1)
    out_ref[...] = jnp.broadcast_to(row[None], out_ref.shape)


def key_positions(keys):
    lane = lanes_of((16, WIDE))
    pick = jnp.where(
        lane == LATENT + ROPE, float(HALF), jnp.where(lane == LATENT + ROPE + 1, 1.0, 0.0)
    ).astype(jnp.bfloat16)
    found = lax.dot_general(
        pick, keys, (((1,), (1,)), ((), ())), preferred_element_type=jnp.float32
    )
    return found[:1]


def query_positions(span_ref, start, count):
    block = block_index()
    other = start // ROWS
    block = block + other * (1 - 2 * lax.axis_index("c"))
    row = lax.broadcasted_iota(jnp.int32, (count, 1), 0)
    first = span_ref[block * 2] * HALF
    second = span_ref[block * 2 + 1] * HALF
    token = row % TOK
    return jnp.where(token < HALF, first + token, second + token - HALF).astype(jnp.float32)


def attend(span_ref, query_ref, key_refs, carry, finish):
    keys = [ref[...] for ref in key_refs]
    places = [key_positions(block) for block in keys]
    for start in range(0, 2 * ROWS, CHUNK):
        queries = query_ref[start : start + CHUNK, :]
        here = query_positions(span_ref, start, CHUNK)
        scores = []
        for block, place in zip(keys, places):
            raw = lax.dot_general(
                queries, block, (((1,), (1,)), ((), ())), preferred_element_type=jnp.float32
            )
            scores.append(jnp.where(place <= here, raw * (score_scale * log2e), masked_score))
        tops = [jnp.max(score, axis=1, keepdims=True) for score in scores]
        top = functools.reduce(jnp.maximum, tops)
        if carry is not None:
            old_acc, old_top, old_sum = carry
            before = old_top[start : start + CHUNK, :1]
            top = jnp.maximum(top, before)
        product = None
        total = None
        for block, score in zip(keys, scores):
            weight = jnp.exp2(score - top)
            for at in range(0, weight.shape[1], 128):
                part = weight[:, at : at + 128]
                total = part if total is None else total + part
            term = jnp.dot(
                weight.astype(jnp.bfloat16), block[:, :LATENT], preferred_element_type=jnp.float32
            )
            product = term if product is None else product + term
        if carry is not None:
            shrink = jnp.exp2(before - top)
            product = product + old_acc[start : start + CHUNK, :] * shrink
            total = total + old_sum[start : start + CHUNK, :] * shrink
        finish(start, product, top, total)


def first_kernel(
    span_ref,
    frequency_ref,
    nope_ref,
    rope_ref,
    sibling_ref,
    key_up_ref,
    keys_ref,
    query_ref,
    acc_ref,
    top_ref,
    sum_ref,
):
    for other in range(2):
        if other == 0:
            nope = nope_ref[...]
            rope = rope_ref[...]
        else:
            nope = sibling_ref[:, : HEADS_HERE * NOPE]
            rope = sibling_ref[:, HEADS_HERE * NOPE :]
        base = other * ROWS
        positions = jnp.broadcast_to(query_positions(span_ref, base, TOK), (TOK, 128))
        cosine, sine_value, leading = rotated(positions, positions, frequency_ref[...])
        lane = lanes_of((TOK, 128))
        for head in range(HEADS_HERE):
            at = base + head * TOK
            query_ref[at : at + TOK, :LATENT] = jnp.dot(
                nope[:, head * NOPE : (head + 1) * NOPE],
                key_up_ref[head],
                preferred_element_type=jnp.float32,
            ).astype(jnp.bfloat16)
        for pair in range(HEADS_HERE // 2):
            turned = apply_rotation(
                rope[:, pair * 128 : (pair + 1) * 128].astype(jnp.float32),
                cosine,
                sine_value,
                leading,
            )
            for side in range(2):
                at = base + (pair * 2 + side) * TOK
                shifted = turned if side == 0 else pltpu.roll(turned, ROPE, 1)
                query_ref[at : at + TOK, LATENT:] = jnp.where(lane < ROPE, shifted, 0.0).astype(
                    jnp.bfloat16
                )

    def finish(start, product, top, total):
        acc_ref[start : start + CHUNK, :] = product
        top_ref[start : start + CHUNK, :] = jnp.broadcast_to(top, (CHUNK, 128))
        sum_ref[start : start + CHUNK, :] = total

    attend(span_ref, query_ref, [keys_ref], None, finish)


def middle_kernel(
    span_ref,
    query_ref,
    one_ref,
    two_ref,
    old_acc_ref,
    old_top_ref,
    old_sum_ref,
    acc_ref,
    top_ref,
    sum_ref,
):
    def finish(start, product, top, total):
        acc_ref[start : start + CHUNK, :] = product
        top_ref[start : start + CHUNK, :] = jnp.broadcast_to(top, (CHUNK, 128))
        sum_ref[start : start + CHUNK, :] = total

    attend(
        span_ref,
        query_ref,
        [one_ref, two_ref],
        (old_acc_ref, old_top_ref, old_sum_ref),
        finish,
    )


def last_kernel(
    span_ref, query_ref, keys_ref, old_acc_ref, old_top_ref, old_sum_ref, own_ref, send_ref
):
    def finish(start, product, top, total):
        ref = own_ref if start < ROWS else send_ref
        at = start % ROWS
        whole = jnp.sum(total, axis=1, keepdims=True)
        lane = lanes_of((CHUNK, 128))
        ref[at : at + CHUNK, :LATENT] = product
        ref[at : at + CHUNK, LATENT:] = jnp.where(lane < 64, top, whole)

    attend(span_ref, query_ref, [keys_ref], (old_acc_ref, old_top_ref, old_sum_ref), finish)


def merge_kernel(own_ref, got_ref, value_up_ref, out_ref):
    for head in range(HEADS_HERE):
        at = slice(head * TOK, (head + 1) * TOK)
        one_top = own_ref[at, LATENT : LATENT + 1]
        two_top = got_ref[at, LATENT : LATENT + 1]
        one_sum = own_ref[at, LATENT + 64 : LATENT + 65]
        two_sum = got_ref[at, LATENT + 64 : LATENT + 65]
        top = jnp.maximum(one_top, two_top)
        one = jnp.exp2(one_top - top)
        two = jnp.exp2(two_top - top)
        total = one_sum * one + two_sum * two
        latent = (own_ref[at, :LATENT] * one + got_ref[at, :LATENT] * two) / total
        out_ref[:, head * VDIM : (head + 1) * VDIM] = jnp.dot(
            latent.astype(jnp.bfloat16), value_up_ref[head], preferred_element_type=jnp.float32
        ).astype(jnp.bfloat16)


def call(kernel, specs, out_shape, name, vmem=32):
    out_specs = jax.tree.map(lambda _: VMEM, out_shape)
    return pl.pallas_call(
        kernel,
        in_specs=specs,
        out_specs=out_specs,
        out_shape=out_shape,
        name=name,
        compiler_params=pltpu.CompilerParams(vmem_limit_bytes=vmem * 1024 * 1024),
    )


def device_at(y, z, x, c):
    y, z, x = y % NY, z % (NZH * NZL), x % NX
    return (((y * NZH + z // NZL) * NC + c) * NZL + z % NZL) * NX + x


def pairs(target):
    return [
        (device_at(y, z, x, c), device_at(*target(y, z, x, c)))
        for y in range(NY)
        for z in range(NZH * NZL)
        for x in range(NX)
        for c in range(NC)
    ]


def shards(query_nope, query_rope, compressed, latent_gain, key_up, value_up, span_order):
    f32 = jnp.float32
    bf16 = jnp.bfloat16
    shape = jax.ShapeDtypeStruct
    frequency = jnp.asarray(FREQUENCY)
    toward = pairs(lambda y, z, x, c: (y, z, x - 1 + 2 * c, c))
    away = pairs(lambda y, z, x, c: (y, z, x + 1 - 2 * c, c))
    across = pairs(lambda y, z, x, c: (y, z, x, 1 - c))

    sent = call(
        prep_kernel, [SMEM, VMEM, VMEM, VMEM], shape((64, 8, WIDE), bf16), "prep", 8
    )(span_order, compressed, latent_gain[None], frequency)
    own_keys = lax.all_to_all(sent, PLANE, 0, 0, tiled=True).reshape(512, WIDE)
    one = lax.ppermute(own_keys, AXES, toward)
    two = lax.ppermute(own_keys, AXES, away)
    sibling = lax.ppermute(jnp.concatenate([query_nope, query_rope], axis=1), AXES, across)
    three = lax.ppermute(one, AXES, toward)
    state = (
        shape((2 * ROWS, LATENT), f32),
        shape((2 * ROWS, 128), f32),
        shape((2 * ROWS, 128), f32),
    )
    queries, *carry = call(
        first_kernel,
        [SMEM] + [VMEM] * 6,
        (shape((2 * ROWS, WIDE), bf16), *state),
        "first",
    )(span_order, frequency, query_nope, query_rope, sibling, key_up, own_keys)
    carry = call(middle_kernel, [SMEM] + [VMEM] * 6, state, "middle")(
        span_order, queries, one, two, *carry
    )
    packet = shape((ROWS, WIDE), f32)
    own, send = call(last_kernel, [SMEM] + [VMEM] * 5, (packet, packet), "last")(
        span_order, queries, three, *carry
    )
    got = lax.ppermute(send, AXES, across)
    return call(
        merge_kernel, [VMEM] * 3, shape((TOK, HEADS_HERE * VDIM), bf16), "merge", 16
    )(own, got, value_up)


def solution(mesh):
    split = Mesh(mesh.devices.reshape(NY, NZH, NC, NZL, NX), AXES)
    placed = (
        P(BLK, HEAD),
        P(BLK, HEAD),
        P(AXES, None),
        P(),
        P(HEAD, None, None),
        P(HEAD, None, None),
        P(),
    )
    return jax.shard_map(
        shards, mesh=split, in_specs=placed, out_specs=P(BLK, HEAD), check_vma=False
    )
```

time: 132 us -> 89.1 us (0.67)
  waiting for transfers between devices: 65.9 us -> 9.72 us
  starting transfers between devices: 0.04 us -> 25.2 us
  Pallas kernels: 0 us -> 15 us
  between operations: 13.5 us -> 0.14 us
  other arithmetic: 8.63 us -> 0.02 us
  matrix products: 8.16 us -> 0 us
  blocking collectives: 30.5 us -> 35.5 us
  local copies, waits for them, and re-layouts: 5.02 us -> 2.81 us
    all_gather x2 -> x0, waiting for transfers between devices: 65.9 us -> none  [stacked_from(): parts = lax.all_gather(parts, axes[k], axis=0, tiled=True)]
    ppermute x0 -> x5, starting transfers between devices: none -> 25.2 us  [the longest x1 14.2 us: shards(): lax.ppermute(jnp.concatenate([query_nope, query_rope], axis=1), AXES, acr...]
    all_to_all x1, blocking collectives: 11.7 us -> 35.5 us  [shards(): own_keys = lax.all_to_all(sent, PLANE, 0, 0, tiled=True).reshape(512, WIDE)]
    all_gather x1 -> x0, blocking collectives: 18.8 us -> none  [stacked_from(): parts = lax.all_gather(parts, axes[k], axis=0, tiled=True)]
    pallas_call x0 -> x5, Pallas kernels: none -> 15 us  [the longest x1 5.58 us: shards(): call(middle_kernel, [SMEM] + [VMEM] * 6, state, 'middle')]
    ppermute x0 -> x5, waiting for transfers between devices: none -> 9.72 us  [the longest x1 6.03 us: shards(): one = lax.ppermute(own_keys, AXES, toward)]
    dot_general x4 -> x0, matrix products: 8.16 us -> none  [the longest x1 4.03 us: shards(): jnp.einsum('qd,kd->qk', queries, shard_keys, preferred_element_type=jnp.f...]
    reduce_sum x5 -> x0, other arithmetic: 6.47 us -> none  [the longest x3 2.95 us: lookup(): return jnp.sum(jnp.where(matches, entries, 0), axis=-1)]
  transfers between devices with their start and end apart: 2 -> 5, of which waited for: 2 -> 3; matrix products, arithmetic and copies ran while one was open for 4% -> 0% of each run, Pallas kernels for 0% -> 10%
where the time goes in v1:
time: 89.1 us; the launch traced here: 88.3 us
  blocking collectives  35.5 us (40%)
  starting transfers between devices  25.2 us (28%)
  Pallas kernels  15 us (17%)
  waiting for transfers between devices  9.72 us (11%)
  local copies, waits for them, and re-layouts  2.81 us (3%)
    all_to_all x1, blocking collectives, shards(): own_keys = lax.all_to_all(sent, PLANE, 0, 0, tiled=True).reshape(512, WIDE)  35.5 us
    ppermute x1, starting transfers between devices, shards(): lax.ppermute(jnp.concatenate([query_nope, query_rope], axis=1), AXES, acr...  14.2 us
    ppermute x1, waiting for transfers between devices, shards(): one = lax.ppermute(own_keys, AXES, toward)  6.03 us
    pallas_call x1, Pallas kernels, shards(): call(middle_kernel, [SMEM] + [VMEM] * 6, state, 'middle')  5.58 us
    pallas_call x1, Pallas kernels, shards(): call(last_kernel, [SMEM] + [VMEM] * 5, (packet, packet), 'last')  3.78 us
    pallas_call x1, Pallas kernels, shards(): call(first_kernel, [SMEM] + [VMEM] * 6, (shape((2 * ROWS, WIDE), bf16), *...  3.48 us
    ppermute x1, starting transfers between devices, shards(): two = lax.ppermute(own_keys, AXES, away)  3.37 us
    ppermute x1, starting transfers between devices, shards(): one = lax.ppermute(own_keys, AXES, toward)  3.11 us
  transfers between devices with their start and end apart: 5, of which 3 were waited for; matrix products, arithmetic and copies ran while one was open for 0% of the time, Pallas kernels for 10%

profile of v1, /device:TPU:1, one launch (start us, length us, event | category | flops | bytes accessed | tf_op | source)
XLA Modules:
  0.0 88.3 jit_solution(17096469091962807331)
XLA Ops:
  0.0 0.8 copy-done.4
  0.8 0.7 copy-done.5
  1.5 0.7 copy-done.7
  2.2 0.7 copy-done.8
  2.8 0.7 prep.1
  3.5 35.5 %all_to_all.5 = bf16[64,8,640]{2,1,0:T(8,128)(2,1)S(1)} all-to-all(bf16[64,8,640]{2,1,0:T(8,128)(2,1)S(1)} %prep.1), channel_id=1, replica_groups=mesh['y'=8,'zh'=4,'c'=2,'zl'=2,'x'=4] {'y','zh','zl'}, dimensions={0} | all-to-all | bytes 1310720 | tf_op jit(solution)/shard_map/all_to_all | solution.py:305
  39.0 3.1 %collective-permute-start.1 = (bf16[512,640]{1,0:T(8,128)(2,1)S(1)}, bf16[512,640]{1,0:T(8,128)(2,1)S(1)}, u32[]{:S(2)}, u32[]{:S(2)}) collective-permute-start(bf16[512,640]{1,0:T(8,128)(2,1)S(1)} %bitcast.2), channel_id=1, source_target_pairs={{0,3},{8,9},{1,0},{9,10},{2,1},{10,11},{3,2},{11,8},{4,7},{12,13},... | collective-permute-start | bytes 1966088 | tf_op jit(solution)/shard_map/ppermute | solution.py:306
  42.1 3.4 %collective-permute-start.3 = (bf16[512,640]{1,0:T(8,128)(2,1)S(1)}, bf16[512,640]{1,0:T(8,128)(2,1)S(1)}, u32[]{:S(2)}, u32[]{:S(2)}) collective-permute-start(bf16[512,640]{1,0:T(8,128)(2,1)S(1)} %bitcast.3), channel_id=1, source_target_pairs={{0,1},{8,11},{1,2},{9,8},{2,3},{10,9},{3,0},{11,10},{4,5},{12,15},... | collective-permute-start | bytes 1966088 | tf_op jit(solution)/shard_map/ppermute | solution.py:307
  45.5 6.0 %collective-permute-done.1.one_ref = bf16[512,640]{1,0:T(8,128)(2,1)S(1)} collective-permute-done((bf16[512,640]{1,0:T(8,128)(2,1)S(1)}, bf16[512,640]{1,0:T(8,128)(2,1)S(1)}, u32[]{:S(2)}, u32[]{:S(2)}) %collective-permute-start.1) | collective-permute-done | bytes 655392 | tf_op jit(solution)/shard_map/ppermute | solution.py:306
  51.5 2.2 %collective-permute-start.2 = (bf16[512,640]{1,0:T(8,128)(2,1)S(1)}, bf16[512,640]{1,0:T(8,128)(2,1)S(1)}, u32[]{:S(2)}, u32[]{:S(2)}) collective-permute-start(bf16[512,640]{1,0:T(8,128)(2,1)S(1)} %collective-permute-done.1.one_ref), channel_id=1, source_target_pairs={{0,3},{8,9},{1,0},{9,10},{2,1},{10,11},{3,2},{11,8},{4,7},{12,13},... | collective-permute-start | bytes 1966088 | tf_op jit(solution)/shard_map/ppermute | solution.py:309
  53.7 0.0 copy-done.2
  53.7 0.0 copy-done.3
  53.7 14.2 %collective-permute-start = (bf16[64,1536]{1,0:T(8,128)(2,1)S(1)}, bf16[64,1536]{1,0:T(8,128)(2,1)S(1)}, u32[]{:S(2)}, u32[]{:S(2)}) collective-permute-start(bf16[64,1536]{1,0:T(8,128)(2,1)S(1)} %pad_maximum_fusion), channel_id=1, source_target_pairs={{0,8},{8,0},{1,9},{9,1},{2,10},{10,2},{3,11},{11,3},{4,12},{12,4},... | collective-permute-start | bytes 589832 | tf_op jit(solution)/shard_map/ppermute | solution.py:308
  67.9 1.0 %collective-permute-done.sibling_ref = bf16[64,1536]{1,0:T(8,128)(2,1)S(1)} collective-permute-done((bf16[64,1536]{1,0:T(8,128)(2,1)S(1)}, bf16[64,1536]{1,0:T(8,128)(2,1)S(1)}, u32[]{:S(2)}, u32[]{:S(2)}) %collective-permute-start) | collective-permute-done | bytes 196640 | tf_op jit(solution)/shard_map/ppermute | solution.py:308
  69.0 0.0 copy-done.6
  69.0 3.5 %first.1 = (bf16[1024,640]{1,0:T(8,128)(2,1)S(1)}, f32[1024,512]{1,0:T(8,128)S(1)}, f32[1024,128]{1,0:T(8,128)S(1)}, f32[1024,128]{1,0:T(8,128)S(1)}) custom-call(s32[128]{0:T(128)S(1)} %copy-done.6, f32[1,128]{1,0:T(1,128)S(1)} %copy-done.9, bf16[64,1024]{1,0:T(8,128)(2,1)S(1)} %copy-done.2, bf16[64,512]{1,0:T(8,128)(2,1)S(1)} %copy-done.3, ...), custom_call_target="tpu_custom_call" | custom-call | tf_op jit(solution)/shard_map/first/pallas_call | solution.py:315
  72.5 0.0 collective-permute-done.3.two_ref
  72.5 5.6 %middle.1 = (f32[1024,512]{1,0:T(8,128)S(1)}, f32[1024,128]{1,0:T(8,128)S(1)}, f32[1024,128]{1,0:T(8,128)S(1)}) custom-call(s32[128]{0:T(128)S(1)} %copy-done.6, bf16[1024,640]{1,0:T(8,128)(2,1)S(1)} %get-tuple-element.14.query_ref, bf16[512,640]{1,0:T(8,128)(2,1)S(1)} %collective-permute-done.1.one_ref, ...), custom_call_target="tpu_custom_call" | custom-call | tf_op jit(solution)/shard_map/middle/pallas_call | solution.py:321
  78.1 0.0 collective-permute-done.2.keys_ref
  78.1 0.0 copy-start.1
  78.1 3.8 %last.1 = (f32[512,640]{1,0:T(8,128)S(1)}, f32[512,640]{1,0:T(8,128)S(1)}) custom-call(s32[128]{0:T(128)S(1)} %copy-done.6, bf16[1024,640]{1,0:T(8,128)(2,1)S(1)} %get-tuple-element.14.query_ref, bf16[512,640]{1,0:T(8,128)(2,1)S(1)} %collective-permute-done.2.keys_ref, f32[1024,512]{1,0:T(8,128)S(1)} %get-tuple-element.18.old_acc_ref, ...), custom_call_target="tpu_custom_call" | custom-call | tf_op jit(solution)/shard_map/last/pallas_call | solution.py:325
  81.9 2.3 %collective-permute-start.4 = (f32[512,640]{1,0:T(8,128)S(1)}, f32[512,640]{1,0:T(8,128)S(1)}, u32[]{:S(2)}, u32[]{:S(2)}) collective-permute-start(f32[512,640]{1,0:T(8,128)S(1)} %get-tuple-element.22), channel_id=1, source_target_pairs={{0,8},{8,0},{1,9},{9,1},{2,10},{10,2},{3,11},{11,3},{4,12},{12,4},... | collective-permute-start | bytes 3932168 | tf_op jit(solution)/shard_map/ppermute | solution.py:328
  84.2 2.6 %collective-permute-done.4.got_ref = f32[512,640]{1,0:T(8,128)S(1)} collective-permute-done((f32[512,640]{1,0:T(8,128)S(1)}, f32[512,640]{1,0:T(8,128)S(1)}, u32[]{:S(2)}, u32[]{:S(2)}) %collective-permute-start.4) | collective-permute-done | bytes 1310752 | tf_op jit(solution)/shard_map/ppermute | solution.py:328
  86.8 1.5 %merge.1 = bf16[64,1024]{1,0:T(8,128)(2,1)} custom-call(f32[512,640]{1,0:T(8,128)S(1)} %get-tuple-element.21.own_ref, f32[512,640]{1,0:T(8,128)S(1)} %collective-permute-done.4.got_ref, bf16[8,512,128]{2,1,0:T(8,128)(2,1)S(1)} %copy-done.1), custom_call_target="tpu_custom_call" | custom-call | tf_op jit(solution)/shard_map/merge/pallas_call | solution.py:329
  (13 shorter events, 0.0 us)
Async XLA Ops:
  0.0 53.7 %copy-start.2 = (bf16[64,1024]{1,0:T(8,128)(2,1)S(1)}, bf16[64,1024]{1,0:T(8,128)(2,1)}, u32[]{:S(2)}) copy-start(bf16[64,1024]{1,0:T(8,128)(2,1)} %nope_ref.1) | copy-start | bytes 393220
  0.0 53.7 %copy-start.3 = (bf16[64,512]{1,0:T(8,128)(2,1)S(1)}, bf16[64,512]{1,0:T(8,128)(2,1)}, u32[]{:S(2)}) copy-start(bf16[64,512]{1,0:T(8,128)(2,1)} %rope_ref.1) | copy-start | bytes 196612
  0.0 69.0 %copy-start = (bf16[8,128,512]{2,1,0:T(8,128)(2,1)S(1)}, bf16[8,128,512]{2,1,0:T(8,128)(2,1)}, u32[]{:S(2)}) copy-start(bf16[8,128,512]{2,1,0:T(8,128)(2,1)} %key_up_ref.1) | copy-start | bytes 3145732
  0.0 0.8 copy-start.4
  0.8 0.7 copy-start.5
  1.5 0.7 copy-start.7
  2.2 0.7 copy-start.8
  2.8 66.2 %copy-start.6 = (s32[128]{0:T(128)S(1)}, s32[128]{0:T(128)}, u32[]{:S(2)}) copy-start(s32[128]{0:T(128)} %span_ref.7) | copy-start | bytes 1540
  2.8 66.2 %copy-start.9 = (f32[1,128]{1,0:T(1,128)S(1)}, f32[1,128]{1,0:T(1,128)}, u32[]{:S(2)}) copy-start(f32[1,128]{1,0:T(1,128)} %constant.2.clone.frequency_ref) | copy-start | bytes 1540
  39.0 12.5 %collective-permute-start.1 = (bf16[512,640]{1,0:T(8,128)(2,1)S(1)}, bf16[512,640]{1,0:T(8,128)(2,1)S(1)}, u32[]{:S(2)}, u32[]{:S(2)}) collective-permute-start(bf16[512,640]{1,0:T(8,128)(2,1)S(1)} %bitcast.2), channel_id=1, source_target_pairs={{0,3},{8,9},{1,0},{9,10},{2,1},{10,11},{3,2},{11,8},{4,7},{12,13},... | collective-permute-start | bytes 1966088 | tf_op jit(solution)/shard_map/ppermute | solution.py:306
  42.1 30.4 %collective-permute-start.3 = (bf16[512,640]{1,0:T(8,128)(2,1)S(1)}, bf16[512,640]{1,0:T(8,128)(2,1)S(1)}, u32[]{:S(2)}, u32[]{:S(2)}) collective-permute-start(bf16[512,640]{1,0:T(8,128)(2,1)S(1)} %bitcast.3), channel_id=1, source_target_pairs={{0,1},{8,11},{1,2},{9,8},{2,3},{10,9},{3,0},{11,10},{4,5},{12,15},... | collective-permute-start | bytes 1966088 | tf_op jit(solution)/shard_map/ppermute | solution.py:307
  51.5 26.6 %collective-permute-start.2 = (bf16[512,640]{1,0:T(8,128)(2,1)S(1)}, bf16[512,640]{1,0:T(8,128)(2,1)S(1)}, u32[]{:S(2)}, u32[]{:S(2)}) collective-permute-start(bf16[512,640]{1,0:T(8,128)(2,1)S(1)} %collective-permute-done.1.one_ref), channel_id=1, source_target_pairs={{0,3},{8,9},{1,0},{9,10},{2,1},{10,11},{3,2},{11,8},{4,7},{12,13},... | collective-permute-start | bytes 1966088 | tf_op jit(solution)/shard_map/ppermute | solution.py:309
  53.7 15.3 %collective-permute-start = (bf16[64,1536]{1,0:T(8,128)(2,1)S(1)}, bf16[64,1536]{1,0:T(8,128)(2,1)S(1)}, u32[]{:S(2)}, u32[]{:S(2)}) collective-permute-start(bf16[64,1536]{1,0:T(8,128)(2,1)S(1)} %pad_maximum_fusion), channel_id=1, source_target_pairs={{0,8},{8,0},{1,9},{9,1},{2,10},{10,2},{3,11},{11,3},{4,12},{12,4},... | collective-permute-start | bytes 589832 | tf_op jit(solution)/shard_map/ppermute | solution.py:308
  78.1 8.7 %copy-start.1 = (bf16[8,512,128]{2,1,0:T(8,128)(2,1)S(1)}, bf16[8,512,128]{2,1,0:T(8,128)(2,1)}, u32[]{:S(2)}) copy-start(bf16[8,512,128]{2,1,0:T(8,128)(2,1)} %value_up_ref.1) | copy-start | bytes 3145732
  81.9 4.9 %collective-permute-start.4 = (f32[512,640]{1,0:T(8,128)S(1)}, f32[512,640]{1,0:T(8,128)S(1)}, u32[]{:S(2)}, u32[]{:S(2)}) collective-permute-start(f32[512,640]{1,0:T(8,128)S(1)} %get-tuple-element.22), channel_id=1, source_target_pairs={{0,8},{8,0},{1,9},{9,1},{2,10},{10,2},{3,11},{11,3},{4,12},{12,4},... | collective-permute-start | bytes 3932168 | tf_op jit(solution)/shard_map/ppermute | solution.py:328

commit v2 on v1

--- a/solution.py
+++ b/solution.py
@@ -39,6 +39,7 @@
 
 VMEM = pl.BlockSpec(memory_space=pltpu.VMEM)
 SMEM = pl.BlockSpec(memory_space=pltpu.SMEM)
+HBM = pl.BlockSpec(memory_space=pltpu.HBM)
 
 
 def lanes_of(shape):
@@ -67,7 +68,33 @@
     return (lax.axis_index("y") * NZH + lax.axis_index("zh")) * NC + lax.axis_index("c")
 
 
-def prep_kernel(span_ref, compressed_ref, gain_ref, frequency_ref, out_ref):
+def prep_kernel(
+    span_hbm,
+    compressed_hbm,
+    gain_hbm,
+    frequency_hbm,
+    out_ref,
+    span_ref,
+    compressed_ref,
+    gain_ref,
+    frequency_ref,
+    sems,
+):
+    copies = [
+        pltpu.make_async_copy(source, target, sems.at[k])
+        for k, (source, target) in enumerate(
+            (
+                (compressed_hbm, compressed_ref),
+                (gain_hbm, gain_ref),
+                (span_hbm, span_ref),
+                (frequency_hbm, frequency_ref),
+            )
+        )
+    ]
+    for copy in copies:
+        copy.start()
+    for copy in copies:
+        copy.wait()
     rows = compressed_ref.shape[0]
     block = block_index()
     x = lax.axis_index("x")
@@ -117,10 +144,10 @@
     return jnp.where(token < HALF, first + token, second + token - HALF).astype(jnp.float32)
 
 
-def attend(span_ref, query_ref, key_refs, carry, finish):
+def attend(span_ref, query_ref, key_refs, carry, finish, rows=(0, 2 * ROWS)):
     keys = [ref[...] for ref in key_refs]
     places = [key_positions(block) for block in keys]
-    for start in range(0, 2 * ROWS, CHUNK):
+    for start in range(*rows, CHUNK):
         queries = query_ref[start : start + CHUNK, :]
         here = query_positions(span_ref, start, CHUNK)
         scores = []
@@ -209,8 +236,7 @@
 def middle_kernel(
     span_ref,
     query_ref,
-    one_ref,
-    two_ref,
+    keys_ref,
     old_acc_ref,
     old_top_ref,
     old_sum_ref,
@@ -226,24 +252,38 @@
     attend(
         span_ref,
         query_ref,
+        [keys_ref],
+        (old_acc_ref, old_top_ref, old_sum_ref),
+        finish,
+    )
+
+
+def last_kernel(
+    side,
+    span_ref,
+    query_ref,
+    one_ref,
+    two_ref,
+    old_acc_ref,
+    old_top_ref,
+    old_sum_ref,
+    out_ref,
+):
+    def finish(start, product, top, total):
+        at = start % ROWS
+        whole = jnp.sum(total, axis=1, keepdims=True)
+        lane = lanes_of((CHUNK, 128))
+        out_ref[at : at + CHUNK, :LATENT] = product
+        out_ref[at : at + CHUNK, LATENT:] = jnp.where(lane < 64, top, whole)
+
+    attend(
+        span_ref,
+        query_ref,
         [one_ref, two_ref],
         (old_acc_ref, old_top_ref, old_sum_ref),
         finish,
-    )
-
-
-def last_kernel(
-    span_ref, query_ref, keys_ref, old_acc_ref, old_top_ref, old_sum_ref, own_ref, send_ref
-):
-    def finish(start, product, top, total):
-        ref = own_ref if start < ROWS else send_ref
-        at = start % ROWS
-        whole = jnp.sum(total, axis=1, keepdims=True)
-        lane = lanes_of((CHUNK, 128))
-        ref[at : at + CHUNK, :LATENT] = product
-        ref[at : at + CHUNK, LATENT:] = jnp.where(lane < 64, top, whole)
-
-    attend(span_ref, query_ref, [keys_ref], (old_acc_ref, old_top_ref, old_sum_ref), finish)
+        (side * ROWS, (side + 1) * ROWS),
+    )
 
 
 def merge_kernel(own_ref, got_ref, value_up_ref, out_ref):
@@ -263,7 +303,7 @@
         ).astype(jnp.bfloat16)
 
 
-def call(kernel, specs, out_shape, name, vmem=32):
+def call(kernel, specs, out_shape, name, vmem=32, scratch=()):
     out_specs = jax.tree.map(lambda _: VMEM, out_shape)
     return pl.pallas_call(
         kernel,
@@ -271,6 +311,7 @@
         out_specs=out_specs,
         out_shape=out_shape,
         name=name,
+        scratch_shapes=list(scratch),
         compiler_params=pltpu.CompilerParams(vmem_limit_bytes=vmem * 1024 * 1024),
     )
 
@@ -295,18 +336,34 @@
     bf16 = jnp.bfloat16
     shape = jax.ShapeDtypeStruct
     frequency = jnp.asarray(FREQUENCY)
-    toward = pairs(lambda y, z, x, c: (y, z, x - 1 + 2 * c, c))
-    away = pairs(lambda y, z, x, c: (y, z, x + 1 - 2 * c, c))
-    across = pairs(lambda y, z, x, c: (y, z, x, 1 - c))
+    def along_x(y, z, x, c):
+        away = c ^ (y % 2)
+        return (y, z, x + 1, 1) if away else (y, z, x - 1, 0)
+
+    first_pairs = pairs(along_x)
+    onward_pairs = pairs(lambda y, z, x, c: (y, z, x - 1 + 2 * c, c))
+    relay_pairs = pairs(lambda y, z, x, c: (y - 1 + 2 * c, z, x, c))
+    sibling_pairs = pairs(lambda y, z, x, c: (y, z, x, 1 - c))
 
     sent = call(
-        prep_kernel, [SMEM, VMEM, VMEM, VMEM], shape((64, 8, WIDE), bf16), "prep", 8
+        prep_kernel,
+        [HBM] * 4,
+        shape((64, 8, WIDE), bf16),
+        "prep",
+        60,
+        [
+            pltpu.SMEM((128,), jnp.int32),
+            pltpu.VMEM((8, LATENT + ROPE), bf16),
+            pltpu.VMEM((1, LATENT), f32),
+            pltpu.VMEM((1, 128), f32),
+            pltpu.SemaphoreType.DMA((4,)),
+        ],
     )(span_order, compressed, latent_gain[None], frequency)
     own_keys = lax.all_to_all(sent, PLANE, 0, 0, tiled=True).reshape(512, WIDE)
-    one = lax.ppermute(own_keys, AXES, toward)
-    two = lax.ppermute(own_keys, AXES, away)
-    sibling = lax.ppermute(jnp.concatenate([query_nope, query_rope], axis=1), AXES, across)
-    three = lax.ppermute(one, AXES, toward)
+    one = lax.ppermute(own_keys, AXES, first_pairs)
+    sibling = lax.ppermute(
+        jnp.concatenate([query_nope, query_rope], axis=1), AXES, sibling_pairs
+    )
     state = (
         shape((2 * ROWS, LATENT), f32),
         shape((2 * ROWS, 128), f32),
@@ -318,14 +375,19 @@
         (shape((2 * ROWS, WIDE), bf16), *state),
         "first",
     )(span_order, frequency, query_nope, query_rope, sibling, key_up, own_keys)
-    carry = call(middle_kernel, [SMEM] + [VMEM] * 6, state, "middle")(
-        span_order, queries, one, two, *carry
+    one, carry = lax.optimization_barrier((one, carry))
+    two = lax.ppermute(one, AXES, onward_pairs)
+    three = lax.ppermute(one, AXES, relay_pairs)
+    carry = call(middle_kernel, [SMEM] + [VMEM] * 5, state, "middle")(
+        span_order, queries, one, *carry
     )
     packet = shape((ROWS, WIDE), f32)
-    own, send = call(last_kernel, [SMEM] + [VMEM] * 5, (packet, packet), "last")(
-        span_order, queries, three, *carry
-    )
-    got = lax.ppermute(send, AXES, across)
+    ending = (span_order, queries, two, three, *carry)
+    send = call(functools.partial(last_kernel, 1), [SMEM] + [VMEM] * 6, packet, "last_sibling")(
+        *ending
+    )
+    got = lax.ppermute(send, AXES, sibling_pairs)
+    own = call(functools.partial(last_kernel, 0), [SMEM] + [VMEM] * 6, packet, "last_own")(*ending)
     return call(
         merge_kernel, [VMEM] * 3, shape((TOK, HEADS_HERE * VDIM), bf16), "merge", 16
     )(own, got, value_up)

time: 89.1 us -> 81.8 us (0.918)
  starting transfers between devices: 25.2 us -> 20.5 us
  local copies, waits for them, and re-layouts: 2.81 us -> 0.03 us
  Pallas kernels: 15 us -> 17 us
  waiting for transfers between devices: 9.72 us -> 7.97 us
    ppermute x5, starting transfers between devices: 25.2 us -> 20.5 us  [the longest x1 7.17 us: shards(): lax.ppermute(jnp.concatenate([query_nope, query_rope], axis=1), AXES, sib...]
    unnamed x20 -> x12, local copies, waits for them, and re-layouts: 2.81 us -> 0.03 us
    pallas_call x3 -> x4, Pallas kernels: 10 us -> 12 us  [the longest x1 3.69 us: shards(): call(middle_kernel, [SMEM] + [VMEM] * 5, state, 'middle')]
    ppermute x5, waiting for transfers between devices: 9.72 us -> 7.97 us  [the longest x1 3.55 us: shards(): two = lax.ppermute(one, AXES, onward_pairs)]
  transfers between devices with their start and end apart: 5 -> 5, of which waited for: 3 -> 3; matrix products, arithmetic and copies ran while one was open for 0% -> 0% of each run, Pallas kernels for 10% -> 13%
where the time goes in v2:
time: 81.8 us; the launch traced here: 81.4 us
  blocking collectives  35.7 us (44%)
  starting transfers between devices  20.5 us (25%)
  Pallas kernels  17 us (21%)
  waiting for transfers between devices  7.97 us (10%)
    all_to_all x1, blocking collectives, shards(): own_keys = lax.all_to_all(sent, PLANE, 0, 0, tiled=True).reshape(512, WIDE)  35.7 us
    ppermute x1, starting transfers between devices, shards(): lax.ppermute(jnp.concatenate([query_nope, query_rope], axis=1), AXES, sib...  7.17 us
    ppermute x1, starting transfers between devices, shards(): three = lax.ppermute(one, AXES, relay_pairs)  4.2 us
    ppermute x1, starting transfers between devices, shards(): got = lax.ppermute(send, AXES, sibling_pairs)  4.15 us
    pallas_call x1, Pallas kernels, shards(): call(middle_kernel, [SMEM] + [VMEM] * 5, state, 'middle')  3.69 us
    ppermute x1, waiting for transfers between devices, shards(): two = lax.ppermute(one, AXES, onward_pairs)  3.55 us
    pallas_call x1, Pallas kernels, shards(): call(first_kernel, [SMEM] + [VMEM] * 6, (shape((2 * ROWS, WIDE), bf16), *...  3.47 us
    ppermute x1, waiting for transfers between devices, shards(): three = lax.ppermute(one, AXES, relay_pairs)  3.36 us
  transfers between devices with their start and end apart: 5, of which 3 were waited for; matrix products, arithmetic and copies ran while one was open for 0% of the time, Pallas kernels for 13%

profile of v2, /device:TPU:1, one launch (start us, length us, event | category | flops | bytes accessed | tf_op | source)
XLA Modules:
  0.0 81.4 jit_solution(4309737424524409281)
XLA Ops:
  0.0 0.0 copy-start.2
  0.0 0.0 copy-start
  0.0 1.8 %prep.1 = bf16[64,8,640]{2,1,0:T(8,128)(2,1)} custom-call(s32[128]{0:T(128)} %span_ref.7, bf16[8,576]{1,0:T(8,128)(2,1)} %compressed_hbm.1, f32[1,512]{1,0:T(1,128)} %bitcast.4, f32[1,128]{1,0:T(1,128)} %constant.2.clone.frequency_hbm.frequency_ref), custom_call_target="tpu_custom_call" | custom-call | tf_op jit(solution)/shard_map/prep/pallas_call | solution.py:348
  1.9 35.7 %all_to_all.5 = bf16[64,8,640]{2,1,0:T(8,128)(2,1)S(1)} all-to-all(bf16[64,8,640]{2,1,0:T(8,128)(2,1)} %prep.1), channel_id=1, replica_groups=mesh['y'=8,'zh'=4,'c'=2,'zl'=2,'x'=4] {'y','zh','zl'}, dimensions={0} | all-to-all | bytes 1310720 | tf_op jit(solution)/shard_map/all_to_all | solution.py:362
  37.5 3.1 %collective-permute-start.1 = (bf16[512,640]{1,0:T(8,128)(2,1)S(1)}, bf16[512,640]{1,0:T(8,128)(2,1)S(1)}, u32[]{:S(2)}, u32[]{:S(2)}) collective-permute-start(bf16[512,640]{1,0:T(8,128)(2,1)S(1)} %bitcast.2), channel_id=1, source_target_pairs={{0,3},{8,9},{1,0},{9,10},{2,1},{10,11},{3,2},{11,8},{4,7},{12,13},... | collective-permute-start | bytes 1966088 | tf_op jit(solution)/shard_map/ppermute | solution.py:363
  40.7 0.0 copy-done.3
  40.7 0.0 copy-done.2
  40.7 7.2 %collective-permute-start = (bf16[64,1536]{1,0:T(8,128)(2,1)S(1)}, bf16[64,1536]{1,0:T(8,128)(2,1)S(1)}, u32[]{:S(2)}, u32[]{:S(2)}) collective-permute-start(bf16[64,1536]{1,0:T(8,128)(2,1)S(1)} %pad_maximum_fusion), channel_id=1, source_target_pairs={{0,8},{8,0},{1,9},{9,1},{2,10},{10,2},{3,11},{11,3},{4,12},{12,4},... | collective-permute-start | bytes 589832 | tf_op jit(solution)/shard_map/ppermute | solution.py:364
  47.9 1.0 %collective-permute-done.sibling_ref = bf16[64,1536]{1,0:T(8,128)(2,1)S(1)} collective-permute-done((bf16[64,1536]{1,0:T(8,128)(2,1)S(1)}, bf16[64,1536]{1,0:T(8,128)(2,1)S(1)}, u32[]{:S(2)}, u32[]{:S(2)}) %collective-permute-start) | collective-permute-done | bytes 196640 | tf_op jit(solution)/shard_map/ppermute | solution.py:364
  48.9 0.0 copy-done.5
  48.9 0.0 copy-done.4
  48.9 3.5 %first.1 = (bf16[1024,640]{1,0:T(8,128)(2,1)S(1)}, f32[1024,512]{1,0:T(8,128)S(1)}, f32[1024,128]{1,0:T(8,128)S(1)}, f32[1024,128]{1,0:T(8,128)S(1)}) custom-call(s32[128]{0:T(128)S(1)} %copy-done.4, f32[1,128]{1,0:T(1,128)S(1)} %copy-done.5, bf16[64,1024]{1,0:T(8,128)(2,1)S(1)} %copy-done.2, bf16[64,512]{1,0:T(8,128)(2,1)S(1)} %copy-done.3, ...), custom_call_target="tpu_custom_call" | custom-call | tf_op jit(solution)/shard_map/first/pallas_call | solution.py:372
  52.4 0.0 collective-permute-done.1.keys_ref
  52.4 4.2 %collective-permute-start.3 = (bf16[512,640]{1,0:T(8,128)(2,1)S(1)}, bf16[512,640]{1,0:T(8,128)(2,1)S(1)}, u32[]{:S(2)}, u32[]{:S(2)}) collective-permute-start(bf16[512,640]{1,0:T(8,128)(2,1)S(1)} %collective-permute-done.1.keys_ref), channel_id=1, source_target_pairs={{0,448},{8,72},{1,449},{9,73},{2,450},{10,74},{3,451},{11,75},{4,4... | collective-permute-start | bytes 1966088 | tf_op jit(solution)/shard_map/ppermute | solution.py:380
  56.6 1.9 %collective-permute-start.2 = (bf16[512,640]{1,0:T(8,128)(2,1)S(1)}, bf16[512,640]{1,0:T(8,128)(2,1)S(1)}, u32[]{:S(2)}, u32[]{:S(2)}) collective-permute-start(bf16[512,640]{1,0:T(8,128)(2,1)S(1)} %collective-permute-done.1.keys_ref), channel_id=1, source_target_pairs={{0,3},{8,9},{1,0},{9,10},{2,1},{10,11},{3,2},{11,8},{4,7},{12,13},... | collective-permute-start | bytes 1966088 | tf_op jit(solution)/shard_map/ppermute | solution.py:379
  58.6 3.7 %middle.1 = (f32[1024,512]{1,0:T(8,128)S(1)}, f32[1024,128]{1,0:T(8,128)S(1)}, f32[1024,128]{1,0:T(8,128)S(1)}) custom-call(s32[128]{0:T(128)S(1)} %copy-done.4, bf16[1024,640]{1,0:T(8,128)(2,1)S(1)} %get-tuple-element.16.query_ref, bf16[512,640]{1,0:T(8,128)(2,1)S(1)} %collective-permute-done.1.keys_ref, f32[1024,512]{1,0:T(8,128)S(1)} %get-tuple-element.21.old_acc_ref, ...), custom_call_target="tpu_custom_call" | custom-call | tf_op jit(solution)/shard_map/middle/pallas_call | solution.py:381
  62.3 3.4 %collective-permute-done.3.two_ref = bf16[512,640]{1,0:T(8,128)(2,1)S(1)} collective-permute-done((bf16[512,640]{1,0:T(8,128)(2,1)S(1)}, bf16[512,640]{1,0:T(8,128)(2,1)S(1)}, u32[]{:S(2)}, u32[]{:S(2)}) %collective-permute-start.3) | collective-permute-done | bytes 655392 | tf_op jit(solution)/shard_map/ppermute | solution.py:380
  65.6 3.5 %collective-permute-done.2.one_ref = bf16[512,640]{1,0:T(8,128)(2,1)S(1)} collective-permute-done((bf16[512,640]{1,0:T(8,128)(2,1)S(1)}, bf16[512,640]{1,0:T(8,128)(2,1)S(1)}, u32[]{:S(2)}, u32[]{:S(2)}) %collective-permute-start.2) | collective-permute-done | bytes 655392 | tf_op jit(solution)/shard_map/ppermute | solution.py:379
  69.2 3.2 %last_sibling.1 = f32[512,640]{1,0:T(8,128)S(1)} custom-call(s32[128]{0:T(128)S(1)} %copy-done.4, bf16[1024,640]{1,0:T(8,128)(2,1)S(1)} %get-tuple-element.16.query_ref, bf16[512,640]{1,0:T(8,128)(2,1)S(1)} %collective-permute-done.2.one_ref, bf16[512,640]{1,0:T(8,128)(2,1)S(1)} %collective-permute-done.3.two_ref, ...), custom_call_target="tpu_custom_call" | custom-call | tf_op jit(solution)/shard_map/last_sibling/pallas_call | solution.py:386
  72.4 0.0 copy-start.1
  72.4 4.1 %collective-permute-start.4 = (f32[512,640]{1,0:T(8,128)S(1)}, f32[512,640]{1,0:T(8,128)S(1)}, u32[]{:S(2)}, u32[]{:S(2)}) collective-permute-start(f32[512,640]{1,0:T(8,128)S(1)} %last_sibling.1), channel_id=1, source_target_pairs={{0,8},{8,0},{1,9},{9,1},{2,10},{10,2},{3,11},{11,3},{4,12},{12,4},... | collective-permute-start | bytes 3932168 | tf_op jit(solution)/shard_map/ppermute | solution.py:389
  76.6 3.3 %last_own.1.own_ref = f32[512,640]{1,0:T(8,128)S(1)} custom-call(s32[128]{0:T(128)S(1)} %copy-done.4, bf16[1024,640]{1,0:T(8,128)(2,1)S(1)} %get-tuple-element.16.query_ref, bf16[512,640]{1,0:T(8,128)(2,1)S(1)} %collective-permute-done.2.one_ref, bf16[512,640]{1,0:T(8,128)(2,1)S(1)} %collective-permute-done.3.two_ref, ...), custom_call_target="tpu_custom_call" | custom-call | tf_op jit(solution)/shard_map/last_own/pallas_call | solution.py:390
  79.9 0.0 collective-permute-done.4.got_ref
  79.9 1.5 %merge.1 = bf16[64,1024]{1,0:T(8,128)(2,1)} custom-call(f32[512,640]{1,0:T(8,128)S(1)} %last_own.1.own_ref, f32[512,640]{1,0:T(8,128)S(1)} %collective-permute-done.4.got_ref, bf16[8,512,128]{2,1,0:T(8,128)(2,1)S(1)} %copy-done.1), custom_call_target="tpu_custom_call" | custom-call | tf_op jit(solution)/shard_map/merge/pallas_call | solution.py:391
  (6 shorter events, 0.0 us)
Async XLA Ops:
  0.0 48.9 %copy-start.5 = (f32[1,128]{1,0:T(1,128)S(1)}, f32[1,128]{1,0:T(1,128)}, u32[]{:S(2)}) copy-start(f32[1,128]{1,0:T(1,128)} %constant.2.clone.frequency_hbm.frequency_ref) | copy-start | bytes 1540
  0.0 48.9 %copy-start.4 = (s32[128]{0:T(128)S(1)}, s32[128]{0:T(128)}, u32[]{:S(2)}) copy-start(s32[128]{0:T(128)} %span_ref.7) | copy-start | bytes 1540
  0.0 40.7 %copy-start.3 = (bf16[64,512]{1,0:T(8,128)(2,1)S(1)}, bf16[64,512]{1,0:T(8,128)(2,1)}, u32[]{:S(2)}) copy-start(bf16[64,512]{1,0:T(8,128)(2,1)} %rope_ref.1) | copy-start | bytes 196612
  0.0 40.7 %copy-start.2 = (bf16[64,1024]{1,0:T(8,128)(2,1)S(1)}, bf16[64,1024]{1,0:T(8,128)(2,1)}, u32[]{:S(2)}) copy-start(bf16[64,1024]{1,0:T(8,128)(2,1)} %nope_ref.1) | copy-start | bytes 393220
  0.0 48.9 %copy-start = (bf16[8,128,512]{2,1,0:T(8,128)(2,1)S(1)}, bf16[8,128,512]{2,1,0:T(8,128)(2,1)}, u32[]{:S(2)}) copy-start(bf16[8,128,512]{2,1,0:T(8,128)(2,1)} %key_up_ref.1) | copy-start | bytes 3145732
  37.5 14.9 %collective-permute-start.1 = (bf16[512,640]{1,0:T(8,128)(2,1)S(1)}, bf16[512,640]{1,0:T(8,128)(2,1)S(1)}, u32[]{:S(2)}, u32[]{:S(2)}) collective-permute-start(bf16[512,640]{1,0:T(8,128)(2,1)S(1)} %bitcast.2), channel_id=1, source_target_pairs={{0,3},{8,9},{1,0},{9,10},{2,1},{10,11},{3,2},{11,8},{4,7},{12,13},... | collective-permute-start | bytes 1966088 | tf_op jit(solution)/shard_map/ppermute | solution.py:363
  40.7 8.2 %collective-permute-start = (bf16[64,1536]{1,0:T(8,128)(2,1)S(1)}, bf16[64,1536]{1,0:T(8,128)(2,1)S(1)}, u32[]{:S(2)}, u32[]{:S(2)}) collective-permute-start(bf16[64,1536]{1,0:T(8,128)(2,1)S(1)} %pad_maximum_fusion), channel_id=1, source_target_pairs={{0,8},{8,0},{1,9},{9,1},{2,10},{10,2},{3,11},{11,3},{4,12},{12,4},... | collective-permute-start | bytes 589832 | tf_op jit(solution)/shard_map/ppermute | solution.py:364
  52.4 13.2 %collective-permute-start.3 = (bf16[512,640]{1,0:T(8,128)(2,1)S(1)}, bf16[512,640]{1,0:T(8,128)(2,1)S(1)}, u32[]{:S(2)}, u32[]{:S(2)}) collective-permute-start(bf16[512,640]{1,0:T(8,128)(2,1)S(1)} %collective-permute-done.1.keys_ref), channel_id=1, source_target_pairs={{0,448},{8,72},{1,449},{9,73},{2,450},{10,74},{3,451},{11,75},{4,4... | collective-permute-start | bytes 1966088 | tf_op jit(solution)/shard_map/ppermute | solution.py:380
  56.6 12.5 %collective-permute-start.2 = (bf16[512,640]{1,0:T(8,128)(2,1)S(1)}, bf16[512,640]{1,0:T(8,128)(2,1)S(1)}, u32[]{:S(2)}, u32[]{:S(2)}) collective-permute-start(bf16[512,640]{1,0:T(8,128)(2,1)S(1)} %collective-permute-done.1.keys_ref), channel_id=1, source_target_pairs={{0,3},{8,9},{1,0},{9,10},{2,1},{10,11},{3,2},{11,8},{4,7},{12,13},... | collective-permute-start | bytes 1966088 | tf_op jit(solution)/shard_map/ppermute | solution.py:379
  72.4 7.4 %copy-start.1 = (bf16[8,512,128]{2,1,0:T(8,128)(2,1)S(1)}, bf16[8,512,128]{2,1,0:T(8,128)(2,1)}, u32[]{:S(2)}) copy-start(bf16[8,512,128]{2,1,0:T(8,128)(2,1)} %value_up_ref.1) | copy-start | bytes 3145732
  72.4 7.4 %collective-permute-start.4 = (f32[512,640]{1,0:T(8,128)S(1)}, f32[512,640]{1,0:T(8,128)S(1)}, u32[]{:S(2)}, u32[]{:S(2)}) collective-permute-start(f32[512,640]{1,0:T(8,128)S(1)} %last_sibling.1), channel_id=1, source_target_pairs={{0,8},{8,0},{1,9},{9,1},{2,10},{10,2},{3,11},{11,3},{4,12},{12,4},... | collective-permute-start | bytes 3932168 | tf_op jit(solution)/shard_map/ppermute | solution.py:389

commit v3 on v2

--- a/solution.py
+++ b/solution.py
@@ -24,7 +24,7 @@
 HALF = 32
 WIDE = 640
 ROWS = TOK * HEADS_HERE
-CHUNK = 256
+CHUNK = 512
 
 norm_epsilon = 1e-06
 rope_base = 10000.0
@@ -130,54 +130,71 @@
     found = lax.dot_general(
         pick, keys, (((1,), (1,)), ((), ())), preferred_element_type=jnp.float32
     )
-    return found[:1]
-
-
-def query_positions(span_ref, start, count):
-    block = block_index()
-    other = start // ROWS
-    block = block + other * (1 - 2 * lax.axis_index("c"))
-    row = lax.broadcasted_iota(jnp.int32, (count, 1), 0)
+    return found[:8]
+
+
+def query_positions(span_ref, other):
+    block = block_index() + other * (1 - 2 * lax.axis_index("c"))
+    token = lax.broadcasted_iota(jnp.int32, (TOK, 128), 0)
     first = span_ref[block * 2] * HALF
-    second = span_ref[block * 2 + 1] * HALF
-    token = row % TOK
-    return jnp.where(token < HALF, first + token, second + token - HALF).astype(jnp.float32)
-
-
-def attend(span_ref, query_ref, key_refs, carry, finish, rows=(0, 2 * ROWS)):
+    second = span_ref[block * 2 + 1] * HALF - HALF
+    return (token + jnp.where(token < HALF, first, second)).astype(jnp.float32)
+
+
+def attend(query_ref, place_ref, key_refs, carry, finish, rows=(0, 2 * ROWS)):
     keys = [ref[...] for ref in key_refs]
     places = [key_positions(block) for block in keys]
     for start in range(*rows, CHUNK):
         queries = query_ref[start : start + CHUNK, :]
-        here = query_positions(span_ref, start, CHUNK)
+        here = place_ref[start : start + CHUNK, :]
         scores = []
         for block, place in zip(keys, places):
             raw = lax.dot_general(
                 queries, block, (((1,), (1,)), ((), ())), preferred_element_type=jnp.float32
             )
-            scores.append(jnp.where(place <= here, raw * (score_scale * log2e), masked_score))
-        tops = [jnp.max(score, axis=1, keepdims=True) for score in scores]
-        top = functools.reduce(jnp.maximum, tops)
+            pieces = []
+            for at in range(0, block.shape[0], 128):
+                there = jnp.tile(place[:, at : at + 128], (CHUNK // 8, 1))
+                pieces.append(
+                    jnp.where(
+                        there <= here, raw[:, at : at + 128] * (score_scale * log2e), masked_score
+                    )
+                )
+            scores.append(pieces)
+        top = functools.reduce(jnp.maximum, [piece for pieces in scores for piece in pieces])
+        top = jnp.broadcast_to(jnp.max(top, axis=1, keepdims=True), (CHUNK, 128))
         if carry is not None:
             old_acc, old_top, old_sum = carry
-            before = old_top[start : start + CHUNK, :1]
+            before = old_top[start : start + CHUNK, :]
             top = jnp.maximum(top, before)
         product = None
         total = None
-        for block, score in zip(keys, scores):
-            weight = jnp.exp2(score - top)
-            for at in range(0, weight.shape[1], 128):
-                part = weight[:, at : at + 128]
-                total = part if total is None else total + part
+        for block, pieces in zip(keys, scores):
+            weights = [jnp.exp2(piece - top) for piece in pieces]
+            for weight in weights:
+                total = weight if total is None else total + weight
             term = jnp.dot(
-                weight.astype(jnp.bfloat16), block[:, :LATENT], preferred_element_type=jnp.float32
+                jnp.concatenate([weight.astype(jnp.bfloat16) for weight in weights], axis=1),
+                block[:, :LATENT],
+                preferred_element_type=jnp.float32,
             )
             product = term if product is None else product + term
         if carry is not None:
             shrink = jnp.exp2(before - top)
-            product = product + old_acc[start : start + CHUNK, :] * shrink
+            product = product + old_acc[start : start + CHUNK, :] * jnp.tile(
+                shrink, (1, LATENT // 128)
+            )
             total = total + old_sum[start : start + CHUNK, :] * shrink
         finish(start, product, top, total)
+
+
+def keep(acc_ref, top_ref, sum_ref):
+    def finish(start, product, top, total):
+        acc_ref[start : start + CHUNK, :] = product
+        top_ref[start : start + CHUNK, :] = top
+        sum_ref[start : start + CHUNK, :] = total
+
+    return finish
 
 
 def first_kernel(
@@ -189,85 +206,47 @@
     key_up_ref,
     keys_ref,
     query_ref,
+    place_ref,
     acc_ref,
     top_ref,
     sum_ref,
 ):
-    for other in range(2):
-        if other == 0:
-            nope = nope_ref[...]
-            rope = rope_ref[...]
-        else:
-            nope = sibling_ref[:, : HEADS_HERE * NOPE]
-            rope = sibling_ref[:, HEADS_HERE * NOPE :]
-        base = other * ROWS
-        positions = jnp.broadcast_to(query_positions(span_ref, base, TOK), (TOK, 128))
-        cosine, sine_value, leading = rotated(positions, positions, frequency_ref[...])
-        lane = lanes_of((TOK, 128))
-        for head in range(HEADS_HERE):
-            at = base + head * TOK
-            query_ref[at : at + TOK, :LATENT] = jnp.dot(
-                nope[:, head * NOPE : (head + 1) * NOPE],
-                key_up_ref[head],
-                preferred_element_type=jnp.float32,
-            ).astype(jnp.bfloat16)
-        for pair in range(HEADS_HERE // 2):
+    nope = jnp.concatenate([nope_ref[...], sibling_ref[:, : HEADS_HERE * NOPE]], axis=0)
+    rope = jnp.concatenate([rope_ref[...], sibling_ref[:, HEADS_HERE * NOPE :]], axis=0)
+    positions = jnp.concatenate([query_positions(span_ref, other) for other in range(2)], axis=0)
+    cosine, sine_value, leading = rotated(positions, positions, frequency_ref[...])
+    lane = lanes_of((2 * TOK, 128))
+    for head in range(HEADS_HERE):
+        raised = jnp.dot(
+            nope[:, head * NOPE : (head + 1) * NOPE],
+            key_up_ref[head],
+            preferred_element_type=jnp.float32,
+        ).astype(jnp.bfloat16)
+        if head % 2 == 0:
             turned = apply_rotation(
-                rope[:, pair * 128 : (pair + 1) * 128].astype(jnp.float32),
+                rope[:, head * ROPE : head * ROPE + 128].astype(jnp.float32),
                 cosine,
                 sine_value,
                 leading,
             )
-            for side in range(2):
-                at = base + (pair * 2 + side) * TOK
-                shifted = turned if side == 0 else pltpu.roll(turned, ROPE, 1)
-                query_ref[at : at + TOK, LATENT:] = jnp.where(lane < ROPE, shifted, 0.0).astype(
-                    jnp.bfloat16
-                )
-
-    def finish(start, product, top, total):
-        acc_ref[start : start + CHUNK, :] = product
-        top_ref[start : start + CHUNK, :] = jnp.broadcast_to(top, (CHUNK, 128))
-        sum_ref[start : start + CHUNK, :] = total
-
-    attend(span_ref, query_ref, [keys_ref], None, finish)
-
-
-def middle_kernel(
-    span_ref,
-    query_ref,
-    keys_ref,
-    old_acc_ref,
-    old_top_ref,
-    old_sum_ref,
-    acc_ref,
-    top_ref,
-    sum_ref,
-):
-    def finish(start, product, top, total):
-        acc_ref[start : start + CHUNK, :] = product
-        top_ref[start : start + CHUNK, :] = jnp.broadcast_to(top, (CHUNK, 128))
-        sum_ref[start : start + CHUNK, :] = total
-
-    attend(
-        span_ref,
-        query_ref,
-        [keys_ref],
-        (old_acc_ref, old_top_ref, old_sum_ref),
-        finish,
-    )
+        else:
+            turned = pltpu.roll(turned, ROPE, 1)
+        tail = jnp.where(lane < ROPE, turned, 0.0).astype(jnp.bfloat16)
+        for other in range(2):
+            at = other * ROWS + head * TOK
+            query_ref[at : at + TOK, :LATENT] = raised[other * TOK : (other + 1) * TOK]
+            query_ref[at : at + TOK, LATENT:] = tail[other * TOK : (other + 1) * TOK]
+            place_ref[at : at + TOK, :] = positions[other * TOK : (other + 1) * TOK]
+    attend(query_ref, place_ref, [keys_ref], None, keep(acc_ref, top_ref, sum_ref))
+
+
+def middle_kernel(count, query_ref, place_ref, *refs):
+    old = refs[count : count + 3]
+    attend(query_ref, place_ref, refs[:count], old, keep(*refs[count + 3 :]))
 
 
 def last_kernel(
-    side,
-    span_ref,
-    query_ref,
-    one_ref,
-    two_ref,
-    old_acc_ref,
-    old_top_ref,
-    old_sum_ref,
-    out_ref,
+    side, query_ref, place_ref, keys_ref, old_acc_ref, old_top_ref, old_sum_ref, out_ref
 ):
     def finish(start, product, top, total):
         at = start % ROWS
@@ -277,9 +256,9 @@
         out_ref[at : at + CHUNK, LATENT:] = jnp.where(lane < 64, top, whole)
 
     attend(
-        span_ref,
         query_ref,
-        [one_ref, two_ref],
+        place_ref,
+        [keys_ref],
         (old_acc_ref, old_top_ref, old_sum_ref),
         finish,
         (side * ROWS, (side + 1) * ROWS),
@@ -337,12 +316,13 @@
     shape = jax.ShapeDtypeStruct
     frequency = jnp.asarray(FREQUENCY)
     def along_x(y, z, x, c):
-        away = c ^ (y % 2)
+        away = c ^ ((y + z) % 2)
         return (y, z, x + 1, 1) if away else (y, z, x - 1, 0)
 
     first_pairs = pairs(along_x)
     onward_pairs = pairs(lambda y, z, x, c: (y, z, x - 1 + 2 * c, c))
-    relay_pairs = pairs(lambda y, z, x, c: (y - 1 + 2 * c, z, x, c))
+    y_pairs = pairs(lambda y, z, x, c: (y - 1 + 2 * c, z, x, c))
+    z_pairs = pairs(lambda y, z, x, c: (y, z - 1 + 2 * c, x, c))
     sibling_pairs = pairs(lambda y, z, x, c: (y, z, x, 1 - c))
 
     sent = call(
@@ -369,25 +349,27 @@
         shape((2 * ROWS, 128), f32),
         shape((2 * ROWS, 128), f32),
     )
-    queries, *carry = call(
+    queries, places, *carry = call(
         first_kernel,
         [SMEM] + [VMEM] * 6,
-        (shape((2 * ROWS, WIDE), bf16), *state),
+        (shape((2 * ROWS, WIDE), bf16), shape((2 * ROWS, 128), f32), *state),
         "first",
     )(span_order, frequency, query_nope, query_rope, sibling, key_up, own_keys)
     one, carry = lax.optimization_barrier((one, carry))
-    two = lax.ppermute(one, AXES, onward_pairs)
-    three = lax.ppermute(one, AXES, relay_pairs)
-    carry = call(middle_kernel, [SMEM] + [VMEM] * 5, state, "middle")(
-        span_order, queries, one, *carry
+    four = lax.ppermute(one, AXES, onward_pairs)
+    two = lax.ppermute(one[:256], AXES, y_pairs)
+    three = lax.ppermute(one[256:], AXES, z_pairs)
+    carry = call(functools.partial(middle_kernel, 1), [VMEM] * 6, state, "middle_x")(
+        queries, places, one, *carry
+    )
+    carry = call(functools.partial(middle_kernel, 2), [VMEM] * 7, state, "middle_yz")(
+        queries, places, two, three, *carry
     )
     packet = shape((ROWS, WIDE), f32)
-    ending = (span_order, queries, two, three, *carry)
-    send = call(functools.partial(last_kernel, 1), [SMEM] + [VMEM] * 6, packet, "last_sibling")(
-        *ending
-    )
+    ending = (queries, places, four, *carry)
+    send = call(functools.partial(last_kernel, 1), [VMEM] * 6, packet, "last_sibling")(*ending)
     got = lax.ppermute(send, AXES, sibling_pairs)
-    own = call(functools.partial(last_kernel, 0), [SMEM] + [VMEM] * 6, packet, "last_own")(*ending)
+    own = call(functools.partial(last_kernel, 0), [VMEM] * 6, packet, "last_own")(*ending)
     return call(
         merge_kernel, [VMEM] * 3, shape((TOK, HEADS_HERE * VDIM), bf16), "merge", 16
     )(own, got, value_up)

time: 81.8 us -> 81.8 us (level)
  starting transfers between devices: 20.5 us -> 25.4 us
  Pallas kernels: 17 us -> 12.5 us
    pallas_call x4 -> x5, Pallas kernels: 13.7 us -> 9.24 us  [the longest x1 2.82 us: shards(): call(first_kernel, [SMEM] + [VMEM] * 6, (shape((2 * ROWS, WIDE), bf16), s...]
    ppermute x2 -> x3, starting transfers between devices: 6.12 us -> 8.95 us  [the longest x1 5.11 us: shards(): three = lax.ppermute(one[256:], AXES, z_pairs)]
    ppermute x1, starting transfers between devices: 4.15 us -> 6.15 us  [shards(): got = lax.ppermute(send, AXES, sibling_pairs)]
    ppermute x2 -> x3, waiting for transfers between devices: 6.91 us -> 5.09 us  [the longest x1 4.76 us: shards(): two = lax.ppermute(one[:256], AXES, y_pairs)]
    ppermute x1, waiting for transfers between devices: 0.01 us -> 1.43 us  [shards(): got = lax.ppermute(send, AXES, sibling_pairs)]
  transfers between devices with their start and end apart: 5 -> 6, of which waited for: 3 -> 4; matrix products, arithmetic and copies ran while one was open for 0% -> 0% of each run, Pallas kernels for 13% -> 10%
where the time goes in v3:
time: 81.8 us; the launch traced here: 81.4 us
  blocking collectives  35.7 us (44%)
  starting transfers between devices  25.4 us (31%)
  Pallas kernels  12.5 us (15%)
  waiting for transfers between devices  7.57 us (9%)
    all_to_all x1, blocking collectives, shards(): own_keys = lax.all_to_all(sent, PLANE, 0, 0, tiled=True).reshape(512, WIDE)  35.7 us
    ppermute x1, starting transfers between devices, shards(): lax.ppermute(jnp.concatenate([query_nope, query_rope], axis=1), AXES, sib...  7.17 us
    ppermute x1, starting transfers between devices, shards(): got = lax.ppermute(send, AXES, sibling_pairs)  6.15 us
    ppermute x1, starting transfers between devices, shards(): three = lax.ppermute(one[256:], AXES, z_pairs)  5.11 us
    ppermute x1, waiting for transfers between devices, shards(): two = lax.ppermute(one[:256], AXES, y_pairs)  4.76 us
    ppermute x1, starting transfers between devices, shards(): one = lax.ppermute(own_keys, AXES, first_pairs)  3.11 us
    pallas_call x1, Pallas kernels, shards(): call(first_kernel, [SMEM] + [VMEM] * 6, (shape((2 * ROWS, WIDE), bf16), s...  2.82 us
    pallas_call x1, Pallas kernels, shards(): call(functools.partial(middle_kernel, 2), [VMEM] * 7, state, 'middle_yz')  2.01 us
  transfers between devices with their start and end apart: 6, of which 4 were waited for; matrix products, arithmetic and copies ran while one was open for 0% of the time, Pallas kernels for 10%

profile of v3, /device:TPU:1, one launch (start us, length us, event | category | flops | bytes accessed | tf_op | source)
XLA Modules:
  0.0 81.4 jit_solution(10010604505231464131)
XLA Ops:
  0.0 1.8 %prep.1 = bf16[64,8,640]{2,1,0:T(8,128)(2,1)} custom-call(s32[128]{0:T(128)} %span_ref.1, bf16[8,576]{1,0:T(8,128)(2,1)} %compressed_hbm.1, f32[1,512]{1,0:T(1,128)} %bitcast.4, f32[1,128]{1,0:T(1,128)} %constant.2.clone.frequency_hbm.frequency_ref), custom_call_target="tpu_custom_call" | custom-call | tf_op jit(solution)/shard_map/prep/pallas_call | solution.py:328
  1.9 35.7 %all_to_all.5 = bf16[64,8,640]{2,1,0:T(8,128)(2,1)S(1)} all-to-all(bf16[64,8,640]{2,1,0:T(8,128)(2,1)} %prep.1), channel_id=1, replica_groups=mesh['y'=8,'zh'=4,'c'=2,'zl'=2,'x'=4] {'y','zh','zl'}, dimensions={0} | all-to-all | bytes 1310720 | tf_op jit(solution)/shard_map/all_to_all | solution.py:342
  37.6 3.1 %collective-permute-start.1 = (bf16[512,640]{1,0:T(8,128)(2,1)S(1)}, bf16[512,640]{1,0:T(8,128)(2,1)S(1)}, u32[]{:S(2)}, u32[]{:S(2)}) collective-permute-start(bf16[512,640]{1,0:T(8,128)(2,1)S(1)} %bitcast.2), channel_id=1, source_target_pairs={{0,3},{8,9},{1,0},{9,10},{2,1},{10,11},{3,2},{11,8},{4,13},{12,7},... | collective-permute-start | bytes 1966088 | tf_op jit(solution)/shard_map/ppermute | solution.py:343
  40.7 7.2 %collective-permute-start = (bf16[64,1536]{1,0:T(8,128)(2,1)S(1)}, bf16[64,1536]{1,0:T(8,128)(2,1)S(1)}, u32[]{:S(2)}, u32[]{:S(2)}) collective-permute-start(bf16[64,1536]{1,0:T(8,128)(2,1)S(1)} %pad_maximum_fusion), channel_id=1, source_target_pairs={{0,8},{8,0},{1,9},{9,1},{2,10},{10,2},{3,11},{11,3},{4,12},{12,4},... | collective-permute-start | bytes 589832 | tf_op jit(solution)/shard_map/ppermute | solution.py:344
  47.9 1.0 %collective-permute-done.sibling_ref = bf16[64,1536]{1,0:T(8,128)(2,1)S(1)} collective-permute-done((bf16[64,1536]{1,0:T(8,128)(2,1)S(1)}, bf16[64,1536]{1,0:T(8,128)(2,1)S(1)}, u32[]{:S(2)}, u32[]{:S(2)}) %collective-permute-start) | collective-permute-done | bytes 196640 | tf_op jit(solution)/shard_map/ppermute | solution.py:344
  48.9 0.0 copy-done.5
  48.9 2.8 %first.1 = (bf16[1024,640]{1,0:T(8,128)(2,1)S(1)}, f32[1024,128]{1,0:T(8,128)S(1)}, f32[1024,512]{1,0:T(8,128)S(1)}, f32[1024,128]{1,0:T(8,128)S(1)}, f32[1024,128]{1,0:T(8,128)S(1)}) custom-call(s32[128]{0:T(128)S(1)} %copy-done.4, f32[1,128]{1,0:T(1,128)S(1)} %copy-done.5, bf16[64,1024]{1,0:T(8,128)(2,1)S(1)} %copy-done.2, bf16[64,512]{1,0:T(8,128)(2,1)S(1)} %copy-done.3, ...), custom_call_target="tpu_custom_call" | custom-call | tf_op jit(solution)/shard_map/first/pallas_call | solution.py:352
  51.8 0.0 collective-permute-done.1.refs_0_
  51.8 1.9 %collective-permute-start.2 = (bf16[512,640]{1,0:T(8,128)(2,1)S(1)}, bf16[512,640]{1,0:T(8,128)(2,1)S(1)}, u32[]{:S(2)}, u32[]{:S(2)}) collective-permute-start(bf16[512,640]{1,0:T(8,128)(2,1)S(1)} %collective-permute-done.1.refs_0_), channel_id=1, source_target_pairs={{0,3},{8,9},{1,0},{9,10},{2,1},{10,11},{3,2},{11,8},{4,7},{12,13},... | collective-permute-start | bytes 1966088 | tf_op jit(solution)/shard_map/ppermute | solution.py:359
  53.7 0.1 fusion
  53.8 5.1 %collective-permute-start.4 = (bf16[256,640]{1,0:T(8,128)(2,1)S(1)}, bf16[256,640]{1,0:T(8,128)(2,1)S(1)}, u32[]{:S(2)}, u32[]{:S(2)}) collective-permute-start(bf16[256,640]{1,0:T(8,128)(2,1)S(1)} %get-tuple-element.35), channel_id=1, source_target_pairs={{0,52},{8,12},{1,53},{9,13},{2,54},{10,14},{3,55},{11,15},{4,0},{1... | collective-permute-start | bytes 983048 | tf_op jit(solution)/shard_map/ppermute | solution.py:361
  58.9 1.9 %collective-permute-start.3 = (bf16[256,640]{1,0:T(8,128)(2,1)S(1)}, bf16[256,640]{1,0:T(8,128)(2,1)S(1)}, u32[]{:S(2)}, u32[]{:S(2)}) collective-permute-start(bf16[256,640]{1,0:T(8,128)(2,1)S(1)} %get-tuple-element.36), channel_id=1, source_target_pairs={{0,448},{8,72},{1,449},{9,73},{2,450},{10,74},{3,451},{11,75},{4,4... | collective-permute-start | bytes 983048 | tf_op jit(solution)/shard_map/ppermute | solution.py:360
  60.8 2.0 %middle_x.1 = (f32[1024,512]{1,0:T(8,128)S(1)}, f32[1024,128]{1,0:T(8,128)S(1)}, f32[1024,128]{1,0:T(8,128)S(1)}) custom-call(bf16[1024,640]{1,0:T(8,128)(2,1)S(1)} %get-tuple-element.20.query_ref, f32[1024,128]{1,0:T(8,128)S(1)} %get-tuple-element.21.place_ref, bf16[512,640]{1,0:T(8,128)(2,1)S(1)} %collective-permute-done.1.refs_0_, ...), custom_call_target="tpu_custom_call" | custom-call | tf_op jit(solution)/shard_map/middle_x/pallas_call | solution.py:362
  62.8 0.3 collective-permute-done.4.refs_1_
  63.2 4.8 %collective-permute-done.3.refs_0_ = bf16[256,640]{1,0:T(8,128)(2,1)S(1)} collective-permute-done((bf16[256,640]{1,0:T(8,128)(2,1)S(1)}, bf16[256,640]{1,0:T(8,128)(2,1)S(1)}, u32[]{:S(2)}, u32[]{:S(2)}) %collective-permute-start.3) | collective-permute-done | bytes 327712 | tf_op jit(solution)/shard_map/ppermute | solution.py:360
  67.9 2.0 %middle_yz.1 = (f32[1024,512]{1,0:T(8,128)S(1)}, f32[1024,128]{1,0:T(8,128)S(1)}, f32[1024,128]{1,0:T(8,128)S(1)}) custom-call(bf16[1024,640]{1,0:T(8,128)(2,1)S(1)} %get-tuple-element.20.query_ref, f32[1024,128]{1,0:T(8,128)S(1)} %get-tuple-element.21.place_ref, bf16[256,640]{1,0:T(8,128)(2,1)S(1)} %collective-permute-done.3.refs_0_, ...), custom_call_target="tpu_custom_call" | custom-call | tf_op jit(solution)/shard_map/middle_yz/pallas_call | solution.py:365
  69.9 0.0 collective-permute-done.2.keys_ref
  69.9 1.2 %last_sibling.1 = f32[512,640]{1,0:T(8,128)S(1)} custom-call(bf16[1024,640]{1,0:T(8,128)(2,1)S(1)} %get-tuple-element.20.query_ref, f32[1024,128]{1,0:T(8,128)S(1)} %get-tuple-element.21.place_ref, bf16[512,640]{1,0:T(8,128)(2,1)S(1)} %collective-permute-done.2.keys_ref, f32[1024,512]{1,0:T(8,128)S(1)} %get-tuple-element.32.old_acc_ref, ...), custom_call_target="tpu_custom_call" | custom-call | tf_op jit(solution)/shard_map/last_sibling/pallas_call | solution.py:370
  71.2 0.0 copy-start.1
  71.2 6.1 %collective-permute-start.5 = (f32[512,640]{1,0:T(8,128)S(1)}, f32[512,640]{1,0:T(8,128)S(1)}, u32[]{:S(2)}, u32[]{:S(2)}) collective-permute-start(f32[512,640]{1,0:T(8,128)S(1)} %last_sibling.1), channel_id=1, source_target_pairs={{0,8},{8,0},{1,9},{9,1},{2,10},{10,2},{3,11},{11,3},{4,12},{12,4},... | collective-permute-start | bytes 3932168 | tf_op jit(solution)/shard_map/ppermute | solution.py:371
  77.3 1.2 %last_own.1.own_ref = f32[512,640]{1,0:T(8,128)S(1)} custom-call(bf16[1024,640]{1,0:T(8,128)(2,1)S(1)} %get-tuple-element.20.query_ref, f32[1024,128]{1,0:T(8,128)S(1)} %get-tuple-element.21.place_ref, bf16[512,640]{1,0:T(8,128)(2,1)S(1)} %collective-permute-done.2.keys_ref, f32[1024,512]{1,0:T(8,128)S(1)} %get-tuple-element.32.old_acc_ref, ...), custom_call_target="tpu_custom_call" | custom-call | tf_op jit(solution)/shard_map/last_own/pallas_call | solution.py:372
  78.5 1.4 %collective-permute-done.5.got_ref = f32[512,640]{1,0:T(8,128)S(1)} collective-permute-done((f32[512,640]{1,0:T(8,128)S(1)}, f32[512,640]{1,0:T(8,128)S(1)}, u32[]{:S(2)}, u32[]{:S(2)}) %collective-permute-start.5) | collective-permute-done | bytes 1310752 | tf_op jit(solution)/shard_map/ppermute | solution.py:371
  80.0 0.0 copy-done.1
  80.0 1.5 %merge.1 = bf16[64,1024]{1,0:T(8,128)(2,1)} custom-call(f32[512,640]{1,0:T(8,128)S(1)} %last_own.1.own_ref, f32[512,640]{1,0:T(8,128)S(1)} %collective-permute-done.5.got_ref, bf16[8,512,128]{2,1,0:T(8,128)(2,1)S(1)} %copy-done.1), custom_call_target="tpu_custom_call" | custom-call | tf_op jit(solution)/shard_map/merge/pallas_call | solution.py:373
  (10 shorter events, 0.0 us)
Async XLA Ops:
  0.0 48.9 %copy-start.5 = (f32[1,128]{1,0:T(1,128)S(1)}, f32[1,128]{1,0:T(1,128)}, u32[]{:S(2)}) copy-start(f32[1,128]{1,0:T(1,128)} %constant.2.clone.frequency_hbm.frequency_ref) | copy-start | bytes 1540
  0.0 48.9 %copy-start.4 = (s32[128]{0:T(128)S(1)}, s32[128]{0:T(128)}, u32[]{:S(2)}) copy-start(s32[128]{0:T(128)} %span_ref.1) | copy-start | bytes 1540
  0.0 40.7 %copy-start.3 = (bf16[64,512]{1,0:T(8,128)(2,1)S(1)}, bf16[64,512]{1,0:T(8,128)(2,1)}, u32[]{:S(2)}) copy-start(bf16[64,512]{1,0:T(8,128)(2,1)} %rope_ref.1) | copy-start | bytes 196612
  0.0 40.7 %copy-start.2 = (bf16[64,1024]{1,0:T(8,128)(2,1)S(1)}, bf16[64,1024]{1,0:T(8,128)(2,1)}, u32[]{:S(2)}) copy-start(bf16[64,1024]{1,0:T(8,128)(2,1)} %nope_ref.1) | copy-start | bytes 393220
  0.0 48.9 %copy-start = (bf16[8,128,512]{2,1,0:T(8,128)(2,1)S(1)}, bf16[8,128,512]{2,1,0:T(8,128)(2,1)}, u32[]{:S(2)}) copy-start(bf16[8,128,512]{2,1,0:T(8,128)(2,1)} %key_up_ref.1) | copy-start | bytes 3145732
  37.6 14.2 %collective-permute-start.1 = (bf16[512,640]{1,0:T(8,128)(2,1)S(1)}, bf16[512,640]{1,0:T(8,128)(2,1)S(1)}, u32[]{:S(2)}, u32[]{:S(2)}) collective-permute-start(bf16[512,640]{1,0:T(8,128)(2,1)S(1)} %bitcast.2), channel_id=1, source_target_pairs={{0,3},{8,9},{1,0},{9,10},{2,1},{10,11},{3,2},{11,8},{4,13},{12,7},... | collective-permute-start | bytes 1966088 | tf_op jit(solution)/shard_map/ppermute | solution.py:343
  40.7 8.2 %collective-permute-start = (bf16[64,1536]{1,0:T(8,128)(2,1)S(1)}, bf16[64,1536]{1,0:T(8,128)(2,1)S(1)}, u32[]{:S(2)}, u32[]{:S(2)}) collective-permute-start(bf16[64,1536]{1,0:T(8,128)(2,1)S(1)} %pad_maximum_fusion), channel_id=1, source_target_pairs={{0,8},{8,0},{1,9},{9,1},{2,10},{10,2},{3,11},{11,3},{4,12},{12,4},... | collective-permute-start | bytes 589832 | tf_op jit(solution)/shard_map/ppermute | solution.py:344
  51.8 18.2 %collective-permute-start.2 = (bf16[512,640]{1,0:T(8,128)(2,1)S(1)}, bf16[512,640]{1,0:T(8,128)(2,1)S(1)}, u32[]{:S(2)}, u32[]{:S(2)}) collective-permute-start(bf16[512,640]{1,0:T(8,128)(2,1)S(1)} %collective-permute-done.1.refs_0_), channel_id=1, source_target_pairs={{0,3},{8,9},{1,0},{9,10},{2,1},{10,11},{3,2},{11,8},{4,7},{12,13},... | collective-permute-start | bytes 1966088 | tf_op jit(solution)/shard_map/ppermute | solution.py:359
  53.8 9.4 %collective-permute-start.4 = (bf16[256,640]{1,0:T(8,128)(2,1)S(1)}, bf16[256,640]{1,0:T(8,128)(2,1)S(1)}, u32[]{:S(2)}, u32[]{:S(2)}) collective-permute-start(bf16[256,640]{1,0:T(8,128)(2,1)S(1)} %get-tuple-element.35), channel_id=1, source_target_pairs={{0,52},{8,12},{1,53},{9,13},{2,54},{10,14},{3,55},{11,15},{4,0},{1... | collective-permute-start | bytes 983048 | tf_op jit(solution)/shard_map/ppermute | solution.py:361
  58.9 9.0 %collective-permute-start.3 = (bf16[256,640]{1,0:T(8,128)(2,1)S(1)}, bf16[256,640]{1,0:T(8,128)(2,1)S(1)}, u32[]{:S(2)}, u32[]{:S(2)}) collective-permute-start(bf16[256,640]{1,0:T(8,128)(2,1)S(1)} %get-tuple-element.36), channel_id=1, source_target_pairs={{0,448},{8,72},{1,449},{9,73},{2,450},{10,74},{3,451},{11,75},{4,4... | collective-permute-start | bytes 983048 | tf_op jit(solution)/shard_map/ppermute | solution.py:360
  71.2 8.8 %copy-start.1 = (bf16[8,512,128]{2,1,0:T(8,128)(2,1)S(1)}, bf16[8,512,128]{2,1,0:T(8,128)(2,1)}, u32[]{:S(2)}) copy-start(bf16[8,512,128]{2,1,0:T(8,128)(2,1)} %value_up_ref.1) | copy-start | bytes 3145732
  71.2 8.8 %collective-permute-start.5 = (f32[512,640]{1,0:T(8,128)S(1)}, f32[512,640]{1,0:T(8,128)S(1)}, u32[]{:S(2)}, u32[]{:S(2)}) collective-permute-start(f32[512,640]{1,0:T(8,128)S(1)} %last_sibling.1), channel_id=1, source_target_pairs={{0,8},{8,0},{1,9},{9,1},{2,10},{10,2},{3,11},{11,3},{4,12},{12,4},... | collective-permute-start | bytes 3932168 | tf_op jit(solution)/shard_map/ppermute | solution.py:371

commit v4 on v3

--- a/solution.py
+++ b/solution.py
@@ -240,43 +240,77 @@
     attend(query_ref, place_ref, [keys_ref], None, keep(acc_ref, top_ref, sum_ref))
 
 
-def middle_kernel(count, query_ref, place_ref, *refs):
-    old = refs[count : count + 3]
-    attend(query_ref, place_ref, refs[:count], old, keep(*refs[count + 3 :]))
-
-
-def last_kernel(
-    side, query_ref, place_ref, keys_ref, old_acc_ref, old_top_ref, old_sum_ref, out_ref
+def middle_kernel(
+    query_ref,
+    place_ref,
+    keys_ref,
+    old_acc_ref,
+    old_top_ref,
+    old_sum_ref,
+    acc_ref,
+    top_ref,
+    sum_ref,
+):
+    old = (old_acc_ref, old_top_ref, old_sum_ref)
+    attend(query_ref, place_ref, [keys_ref], old, keep(acc_ref, top_ref, sum_ref))
+
+
+def send_kernel(query_ref, place_ref, keys_ref, old_acc_ref, old_top_ref, old_sum_ref, out_ref):
+    def finish(start, product, top, total):
+        at = start % ROWS
+        whole = jnp.broadcast_to(jnp.sum(total, axis=1, keepdims=True), (CHUNK, 128))
+        lane = lanes_of((CHUNK, 128))
+        level = top + jnp.log2(whole)
+        high = level.astype(jnp.bfloat16).astype(jnp.float32)
+        rest = level - high
+        middle = rest.astype(jnp.bfloat16).astype(jnp.float32)
+        low = rest - middle
+        pieces = jnp.where(
+            lane == 0, high, jnp.where(lane == 1, middle, jnp.where(lane == 2, low, 0.0))
+        )
+        inverse = jnp.tile(1.0 / whole, (1, LATENT // 128))
+        out_ref[at : at + CHUNK, :LATENT] = (product * inverse).astype(jnp.bfloat16)
+        out_ref[at : at + CHUNK, LATENT:] = pieces.astype(jnp.bfloat16)
+
+    old = (old_acc_ref, old_top_ref, old_sum_ref)
+    attend(query_ref, place_ref, [keys_ref], old, finish, (ROWS, 2 * ROWS))
+
+
+def own_kernel(
+    query_ref,
+    place_ref,
+    keys_ref,
+    old_acc_ref,
+    old_top_ref,
+    old_sum_ref,
+    acc_ref,
+    top_ref,
+    sum_ref,
 ):
     def finish(start, product, top, total):
-        at = start % ROWS
-        whole = jnp.sum(total, axis=1, keepdims=True)
-        lane = lanes_of((CHUNK, 128))
-        out_ref[at : at + CHUNK, :LATENT] = product
-        out_ref[at : at + CHUNK, LATENT:] = jnp.where(lane < 64, top, whole)
-
-    attend(
-        query_ref,
-        place_ref,
-        [keys_ref],
-        (old_acc_ref, old_top_ref, old_sum_ref),
-        finish,
-        (side * ROWS, (side + 1) * ROWS),
-    )
-
-
-def merge_kernel(own_ref, got_ref, value_up_ref, out_ref):
+        acc_ref[start : start + CHUNK, :] = product
+        top_ref[start : start + CHUNK, :] = top
+        sum_ref[start : start + CHUNK, :] = jnp.broadcast_to(
+            jnp.sum(total, axis=1, keepdims=True), (CHUNK, 128)
+        )
+
+    old = (old_acc_ref, old_top_ref, old_sum_ref)
+    attend(query_ref, place_ref, [keys_ref], old, finish, (0, ROWS))
+
+
+def merge_kernel(acc_ref, top_ref, sum_ref, got_ref, value_up_ref, out_ref):
     for head in range(HEADS_HERE):
         at = slice(head * TOK, (head + 1) * TOK)
-        one_top = own_ref[at, LATENT : LATENT + 1]
-        two_top = got_ref[at, LATENT : LATENT + 1]
-        one_sum = own_ref[at, LATENT + 64 : LATENT + 65]
-        two_sum = got_ref[at, LATENT + 64 : LATENT + 65]
-        top = jnp.maximum(one_top, two_top)
-        one = jnp.exp2(one_top - top)
-        two = jnp.exp2(two_top - top)
-        total = one_sum * one + two_sum * two
-        latent = (own_ref[at, :LATENT] * one + got_ref[at, :LATENT] * two) / total
+        level = jnp.sum(got_ref[at, LATENT:].astype(jnp.float32), axis=1, keepdims=True)
+        level = jnp.broadcast_to(level, (TOK, 128))
+        own_top = top_ref[at, :]
+        top = jnp.maximum(own_top, level)
+        one = jnp.exp2(own_top - top)
+        two = jnp.exp2(level - top)
+        inverse = 1.0 / (sum_ref[at, :] * one + two)
+        one = jnp.tile(one * inverse, (1, LATENT // 128))
+        two = jnp.tile(two * inverse, (1, LATENT // 128))
+        latent = acc_ref[at, :] * one + got_ref[at, :LATENT].astype(jnp.float32) * two
         out_ref[:, head * VDIM : (head + 1) * VDIM] = jnp.dot(
             latent.astype(jnp.bfloat16), value_up_ref[head], preferred_element_type=jnp.float32
         ).astype(jnp.bfloat16)
@@ -316,13 +350,12 @@
     shape = jax.ShapeDtypeStruct
     frequency = jnp.asarray(FREQUENCY)
     def along_x(y, z, x, c):
-        away = c ^ ((y + z) % 2)
+        away = c ^ (y % 2)
         return (y, z, x + 1, 1) if away else (y, z, x - 1, 0)
 
     first_pairs = pairs(along_x)
     onward_pairs = pairs(lambda y, z, x, c: (y, z, x - 1 + 2 * c, c))
     y_pairs = pairs(lambda y, z, x, c: (y - 1 + 2 * c, z, x, c))
-    z_pairs = pairs(lambda y, z, x, c: (y, z - 1 + 2 * c, x, c))
     sibling_pairs = pairs(lambda y, z, x, c: (y, z, x, 1 - c))
 
     sent = call(
@@ -356,23 +389,23 @@
         "first",
     )(span_order, frequency, query_nope, query_rope, sibling, key_up, own_keys)
     one, carry = lax.optimization_barrier((one, carry))
-    four = lax.ppermute(one, AXES, onward_pairs)
-    two = lax.ppermute(one[:256], AXES, y_pairs)
-    three = lax.ppermute(one[256:], AXES, z_pairs)
-    carry = call(functools.partial(middle_kernel, 1), [VMEM] * 6, state, "middle_x")(
-        queries, places, one, *carry
-    )
-    carry = call(functools.partial(middle_kernel, 2), [VMEM] * 7, state, "middle_yz")(
-        queries, places, two, three, *carry
-    )
-    packet = shape((ROWS, WIDE), f32)
-    ending = (queries, places, four, *carry)
-    send = call(functools.partial(last_kernel, 1), [VMEM] * 6, packet, "last_sibling")(*ending)
+    two = lax.ppermute(one, AXES, onward_pairs)
+    three = lax.ppermute(one, AXES, y_pairs)
+    middle = call(middle_kernel, [VMEM] * 6, state, "middle")
+    carry = middle(queries, places, one, *carry)
+    carry = middle(queries, places, two, *carry)
+    ending = (queries, places, three, *carry)
+    send = call(send_kernel, [VMEM] * 6, shape((ROWS, WIDE), bf16), "sibling_rows")(*ending)
     got = lax.ppermute(send, AXES, sibling_pairs)
-    own = call(functools.partial(last_kernel, 0), [VMEM] * 6, packet, "last_own")(*ending)
+    own_state = (
+        shape((ROWS, LATENT), f32),
+        shape((ROWS, 128), f32),
+        shape((ROWS, 128), f32),
+    )
+    own = call(own_kernel, [VMEM] * 6, own_state, "own_rows")(*ending)
     return call(
-        merge_kernel, [VMEM] * 3, shape((TOK, HEADS_HERE * VDIM), bf16), "merge", 16
-    )(own, got, value_up)
+        merge_kernel, [VMEM] * 5, shape((TOK, HEADS_HERE * VDIM), bf16), "merge", 16
+    )(*own, got, value_up)
 
 
 def solution(mesh):

time: 81.8 us -> 78.6 us (0.961)
  starting transfers between devices: 25.4 us -> 22.7 us
  waiting for transfers between devices: 7.57 us -> 6.51 us
  other arithmetic: 0.02 us -> 0.96 us
    ppermute x3 -> x2, starting transfers between devices: 8.95 us -> 5.84 us  [the longest x1 3.92 us: shards(): three = lax.ppermute(one, AXES, y_pairs)]
    concatenate x1, other arithmetic: 0.02 us -> 0.96 us  [shards(): jnp.concatenate([query_nope, query_rope], axis=1)]
    ppermute x1, waiting for transfers between devices: 1.43 us -> 0.49 us  [shards(): got = lax.ppermute(send, AXES, sibling_pairs)]
    ppermute x3 -> x2, waiting for transfers between devices: 5.09 us -> 4.97 us  [the longest x1 4.68 us: shards(): two = lax.ppermute(one, AXES, onward_pairs)]
  transfers between devices with their start and end apart: 6 -> 5, of which waited for: 4 -> 4; matrix products, arithmetic and copies ran while one was open for 0% -> 1% of each run, Pallas kernels for 10% -> 10%
where the time goes in v4:
time: 78.6 us; the launch traced here: 78.2 us
  blocking collectives  35.7 us (45%)
  starting transfers between devices  22.7 us (29%)
  Pallas kernels  12.2 us (16%)
  waiting for transfers between devices  6.51 us (8%)
  other arithmetic  0.96 us (1%)
    all_to_all x1, blocking collectives, shards(): own_keys = lax.all_to_all(sent, PLANE, 0, 0, tiled=True).reshape(512, WIDE)  35.7 us
    ppermute x1, starting transfers between devices, shards(): lax.ppermute(jnp.concatenate([query_nope, query_rope], axis=1), AXES, sib...  7.17 us
    ppermute x1, starting transfers between devices, shards(): got = lax.ppermute(send, AXES, sibling_pairs)  6.56 us
    ppermute x1, waiting for transfers between devices, shards(): two = lax.ppermute(one, AXES, onward_pairs)  4.68 us
    ppermute x1, starting transfers between devices, shards(): three = lax.ppermute(one, AXES, y_pairs)  3.92 us
    ppermute x1, starting transfers between devices, shards(): one = lax.ppermute(own_keys, AXES, first_pairs)  3.11 us
    pallas_call x1, Pallas kernels, shards(): call(first_kernel, [SMEM] + [VMEM] * 6, (shape((2 * ROWS, WIDE), bf16), s...  2.82 us
    pallas_call x1, Pallas kernels, shards(): carry = middle(queries, places, two, *carry)  2.01 us
  transfers between devices with their start and end apart: 5, of which 4 were waited for; matrix products, arithmetic and copies ran while one was open for 1% of the time, Pallas kernels for 10%

profile of v4, /device:TPU:1, one launch (start us, length us, event | category | flops | bytes accessed | tf_op | source)
XLA Modules:
  0.0 78.2 jit_solution(786492445480912116)
XLA Ops:
  0.0 0.0 copy-start.2
  0.0 1.8 %prep.1 = bf16[64,8,640]{2,1,0:T(8,128)(2,1)} custom-call(s32[128]{0:T(128)} %span_ref.1, bf16[8,576]{1,0:T(8,128)(2,1)} %compressed_hbm.1, f32[1,512]{1,0:T(1,128)} %bitcast.4, f32[1,128]{1,0:T(1,128)} %constant.2.clone.frequency_hbm.frequency_ref), custom_call_target="tpu_custom_call" | custom-call | tf_op jit(solution)/shard_map/prep/pallas_call | solution.py:361
  1.9 35.7 %all_to_all.5 = bf16[64,8,640]{2,1,0:T(8,128)(2,1)S(1)} all-to-all(bf16[64,8,640]{2,1,0:T(8,128)(2,1)} %prep.1), channel_id=1, replica_groups=mesh['y'=8,'zh'=4,'c'=2,'zl'=2,'x'=4] {'y','zh','zl'}, dimensions={0} | all-to-all | bytes 1310720 | tf_op jit(solution)/shard_map/all_to_all | solution.py:375
  37.6 3.1 %collective-permute-start.1 = (bf16[512,640]{1,0:T(8,128)(2,1)S(1)}, bf16[512,640]{1,0:T(8,128)(2,1)S(1)}, u32[]{:S(2)}, u32[]{:S(2)}) collective-permute-start(bf16[512,640]{1,0:T(8,128)(2,1)S(1)} %bitcast.2), channel_id=1, source_target_pairs={{0,3},{8,9},{1,0},{9,10},{2,1},{10,11},{3,2},{11,8},{4,7},{12,13},... | collective-permute-start | bytes 1966088 | tf_op jit(solution)/shard_map/ppermute | solution.py:376
  40.7 1.0 %pad_maximum_fusion = bf16[64,1536]{1,0:T(8,128)(2,1)S(1)} fusion(bf16[64,512]{1,0:T(8,128)(2,1)} %rope_ref.1, bf16[64,1024]{1,0:T(8,128)(2,1)} %nope_ref.1), kind=kLoop, calls=%fused_computation | loop fusion | flops 393216 | bytes 393216 | tf_op jit(solution)/shard_map/concatenate | solution.py:378
  41.6 7.2 %collective-permute-start = (bf16[64,1536]{1,0:T(8,128)(2,1)S(1)}, bf16[64,1536]{1,0:T(8,128)(2,1)S(1)}, u32[]{:S(2)}, u32[]{:S(2)}) collective-permute-start(bf16[64,1536]{1,0:T(8,128)(2,1)S(1)} %pad_maximum_fusion), channel_id=1, source_target_pairs={{0,8},{8,0},{1,9},{9,1},{2,10},{10,2},{3,11},{11,3},{4,12},{12,4},... | collective-permute-start | bytes 589832 | tf_op jit(solution)/shard_map/ppermute | solution.py:377
  48.8 1.0 %collective-permute-done.sibling_ref = bf16[64,1536]{1,0:T(8,128)(2,1)S(1)} collective-permute-done((bf16[64,1536]{1,0:T(8,128)(2,1)S(1)}, bf16[64,1536]{1,0:T(8,128)(2,1)S(1)}, u32[]{:S(2)}, u32[]{:S(2)}) %collective-permute-start) | collective-permute-done | bytes 196640 | tf_op jit(solution)/shard_map/ppermute | solution.py:377
  49.9 0.0 copy-done.5
  49.9 0.0 copy-done.3
  49.9 2.8 %first.1 = (bf16[1024,640]{1,0:T(8,128)(2,1)S(1)}, f32[1024,128]{1,0:T(8,128)S(1)}, f32[1024,512]{1,0:T(8,128)S(1)}, f32[1024,128]{1,0:T(8,128)S(1)}, f32[1024,128]{1,0:T(8,128)S(1)}) custom-call(s32[128]{0:T(128)S(1)} %copy-done.4, f32[1,128]{1,0:T(1,128)S(1)} %copy-done.5, bf16[64,1024]{1,0:T(8,128)(2,1)S(1)} %copy-done.2, bf16[64,512]{1,0:T(8,128)(2,1)S(1)} %copy-done.3, ...), custom_call_target="tpu_custom_call" | custom-call | tf_op jit(solution)/shard_map/first/pallas_call | solution.py:385
  52.7 0.0 collective-permute-done.1.keys_ref
  52.7 1.9 %collective-permute-start.3 = (bf16[512,640]{1,0:T(8,128)(2,1)S(1)}, bf16[512,640]{1,0:T(8,128)(2,1)S(1)}, u32[]{:S(2)}, u32[]{:S(2)}) collective-permute-start(bf16[512,640]{1,0:T(8,128)(2,1)S(1)} %collective-permute-done.1.keys_ref), channel_id=1, source_target_pairs={{0,3},{8,9},{1,0},{9,10},{2,1},{10,11},{3,2},{11,8},{4,7},{12,13},... | collective-permute-start | bytes 1966088 | tf_op jit(solution)/shard_map/ppermute | solution.py:392
  54.6 3.9 %collective-permute-start.2 = (bf16[512,640]{1,0:T(8,128)(2,1)S(1)}, bf16[512,640]{1,0:T(8,128)(2,1)S(1)}, u32[]{:S(2)}, u32[]{:S(2)}) collective-permute-start(bf16[512,640]{1,0:T(8,128)(2,1)S(1)} %collective-permute-done.1.keys_ref), channel_id=1, source_target_pairs={{0,448},{8,72},{1,449},{9,73},{2,450},{10,74},{3,451},{11,75},{4,4... | collective-permute-start | bytes 1966088 | tf_op jit(solution)/shard_map/ppermute | solution.py:393
  58.6 2.0 %middle.2 = (f32[1024,512]{1,0:T(8,128)S(1)}, f32[1024,128]{1,0:T(8,128)S(1)}, f32[1024,128]{1,0:T(8,128)S(1)}) custom-call(bf16[1024,640]{1,0:T(8,128)(2,1)S(1)} %get-tuple-element.23.query_ref, f32[1024,128]{1,0:T(8,128)S(1)} %get-tuple-element.24.place_ref, bf16[512,640]{1,0:T(8,128)(2,1)S(1)} %collective-permute-done.1.keys_ref, ...), custom_call_target="tpu_custom_call" | custom-call | tf_op jit(solution)/shard_map/middle/pallas_call | solution.py:395
  60.6 4.7 %collective-permute-done.3.keys_ref = bf16[512,640]{1,0:T(8,128)(2,1)S(1)} collective-permute-done((bf16[512,640]{1,0:T(8,128)(2,1)S(1)}, bf16[512,640]{1,0:T(8,128)(2,1)S(1)}, u32[]{:S(2)}, u32[]{:S(2)}) %collective-permute-start.3) | collective-permute-done | bytes 655392 | tf_op jit(solution)/shard_map/ppermute | solution.py:392
  65.3 2.0 %middle.3 = (f32[1024,512]{1,0:T(8,128)S(1)}, f32[1024,128]{1,0:T(8,128)S(1)}, f32[1024,128]{1,0:T(8,128)S(1)}) custom-call(bf16[1024,640]{1,0:T(8,128)(2,1)S(1)} %get-tuple-element.23.query_ref, f32[1024,128]{1,0:T(8,128)S(1)} %get-tuple-element.24.place_ref, bf16[512,640]{1,0:T(8,128)(2,1)S(1)} %collective-permute-done.3.keys_ref, ...), custom_call_target="tpu_custom_call" | custom-call | tf_op jit(solution)/shard_map/middle/pallas_call | solution.py:396
  67.3 0.3 collective-permute-done.2.keys_ref
  67.6 1.2 %sibling_rows.1 = bf16[512,640]{1,0:T(8,128)(2,1)S(1)} custom-call(bf16[1024,640]{1,0:T(8,128)(2,1)S(1)} %get-tuple-element.23.query_ref, f32[1024,128]{1,0:T(8,128)S(1)} %get-tuple-element.24.place_ref, bf16[512,640]{1,0:T(8,128)(2,1)S(1)} %collective-permute-done.2.keys_ref, f32[1024,512]{1,0:T(8,128)S(1)} %get-tuple-element.35.old_acc_ref, ...), custom_call_target="tpu_custom_call" | custom-call | tf_op jit(solution)/shard_map/sibling_rows/pallas_call | solution.py:398
  68.8 0.0 copy-start
  68.8 6.6 %collective-permute-start.4 = (bf16[512,640]{1,0:T(8,128)(2,1)S(1)}, bf16[512,640]{1,0:T(8,128)(2,1)S(1)}, u32[]{:S(2)}, u32[]{:S(2)}) collective-permute-start(bf16[512,640]{1,0:T(8,128)(2,1)S(1)} %sibling_rows.1), channel_id=1, source_target_pairs={{0,8},{8,0},{1,9},{9,1},{2,10},{10,2},{3,11},{11,3},{4,12},{12,4},... | collective-permute-start | bytes 1966088 | tf_op jit(solution)/shard_map/ppermute | solution.py:399
  75.4 1.2 %own_rows.1 = (f32[512,512]{1,0:T(8,128)S(1)}, f32[512,128]{1,0:T(8,128)S(1)}, f32[512,128]{1,0:T(8,128)S(1)}) custom-call(bf16[1024,640]{1,0:T(8,128)(2,1)S(1)} %get-tuple-element.23.query_ref, f32[1024,128]{1,0:T(8,128)S(1)} %get-tuple-element.24.place_ref, bf16[512,640]{1,0:T(8,128)(2,1)S(1)} %collective-permute-done.2.keys_ref, ...), custom_call_target="tpu_custom_call" | custom-call | tf_op jit(solution)/shard_map/own_rows/pallas_call | solution.py:405
  76.6 0.5 collective-permute-done.4.got_ref
  77.1 0.0 copy-done
  77.1 1.1 %merge.1 = bf16[64,1024]{1,0:T(8,128)(2,1)} custom-call(f32[512,512]{1,0:T(8,128)S(1)} %get-tuple-element.38.acc_ref, f32[512,128]{1,0:T(8,128)S(1)} %get-tuple-element.39.top_ref, f32[512,128]{1,0:T(8,128)S(1)} %get-tuple-element.40.sum_ref, bf16[512,640]{1,0:T(8,128)(2,1)S(1)} %collective-permute-done.4.got_ref, bf16[8,512,128]{2,1,0:T(8,128)(2,1)S(1)} %copy-done), custom_call_target="tpu_custom_call" | custom-call | tf_op jit(solution)/shard_map/merge/pallas_call | solution.py:406
  (7 shorter events, 0.0 us)
Async XLA Ops:
  0.0 49.9 %copy-start.5 = (f32[1,128]{1,0:T(1,128)S(1)}, f32[1,128]{1,0:T(1,128)}, u32[]{:S(2)}) copy-start(f32[1,128]{1,0:T(1,128)} %constant.2.clone.frequency_hbm.frequency_ref) | copy-start | bytes 1540
  0.0 49.9 %copy-start.4 = (s32[128]{0:T(128)S(1)}, s32[128]{0:T(128)}, u32[]{:S(2)}) copy-start(s32[128]{0:T(128)} %span_ref.1) | copy-start | bytes 1540
  0.0 49.9 %copy-start.3 = (bf16[64,512]{1,0:T(8,128)(2,1)S(1)}, bf16[64,512]{1,0:T(8,128)(2,1)}, u32[]{:S(2)}) copy-start(bf16[64,512]{1,0:T(8,128)(2,1)} %rope_ref.1) | copy-start | bytes 196612
  0.0 49.9 %copy-start.2 = (bf16[64,1024]{1,0:T(8,128)(2,1)S(1)}, bf16[64,1024]{1,0:T(8,128)(2,1)}, u32[]{:S(2)}) copy-start(bf16[64,1024]{1,0:T(8,128)(2,1)} %nope_ref.1) | copy-start | bytes 393220
  0.0 49.9 %copy-start.1 = (bf16[8,128,512]{2,1,0:T(8,128)(2,1)S(1)}, bf16[8,128,512]{2,1,0:T(8,128)(2,1)}, u32[]{:S(2)}) copy-start(bf16[8,128,512]{2,1,0:T(8,128)(2,1)} %key_up_ref.1) | copy-start | bytes 3145732
  37.6 15.2 %collective-permute-start.1 = (bf16[512,640]{1,0:T(8,128)(2,1)S(1)}, bf16[512,640]{1,0:T(8,128)(2,1)S(1)}, u32[]{:S(2)}, u32[]{:S(2)}) collective-permute-start(bf16[512,640]{1,0:T(8,128)(2,1)S(1)} %bitcast.2), channel_id=1, source_target_pairs={{0,3},{8,9},{1,0},{9,10},{2,1},{10,11},{3,2},{11,8},{4,7},{12,13},... | collective-permute-start | bytes 1966088 | tf_op jit(solution)/shard_map/ppermute | solution.py:376
  41.6 8.2 %collective-permute-start = (bf16[64,1536]{1,0:T(8,128)(2,1)S(1)}, bf16[64,1536]{1,0:T(8,128)(2,1)S(1)}, u32[]{:S(2)}, u32[]{:S(2)}) collective-permute-start(bf16[64,1536]{1,0:T(8,128)(2,1)S(1)} %pad_maximum_fusion), channel_id=1, source_target_pairs={{0,8},{8,0},{1,9},{9,1},{2,10},{10,2},{3,11},{11,3},{4,12},{12,4},... | collective-permute-start | bytes 589832 | tf_op jit(solution)/shard_map/ppermute | solution.py:377
  52.7 12.5 %collective-permute-start.3 = (bf16[512,640]{1,0:T(8,128)(2,1)S(1)}, bf16[512,640]{1,0:T(8,128)(2,1)S(1)}, u32[]{:S(2)}, u32[]{:S(2)}) collective-permute-start(bf16[512,640]{1,0:T(8,128)(2,1)S(1)} %collective-permute-done.1.keys_ref), channel_id=1, source_target_pairs={{0,3},{8,9},{1,0},{9,10},{2,1},{10,11},{3,2},{11,8},{4,7},{12,13},... | collective-permute-start | bytes 1966088 | tf_op jit(solution)/shard_map/ppermute | solution.py:392
  54.6 12.9 %collective-permute-start.2 = (bf16[512,640]{1,0:T(8,128)(2,1)S(1)}, bf16[512,640]{1,0:T(8,128)(2,1)S(1)}, u32[]{:S(2)}, u32[]{:S(2)}) collective-permute-start(bf16[512,640]{1,0:T(8,128)(2,1)S(1)} %collective-permute-done.1.keys_ref), channel_id=1, source_target_pairs={{0,448},{8,72},{1,449},{9,73},{2,450},{10,74},{3,451},{11,75},{4,4... | collective-permute-start | bytes 1966088 | tf_op jit(solution)/shard_map/ppermute | solution.py:393
  68.8 8.3 %copy-start = (bf16[8,512,128]{2,1,0:T(8,128)(2,1)S(1)}, bf16[8,512,128]{2,1,0:T(8,128)(2,1)}, u32[]{:S(2)}) copy-start(bf16[8,512,128]{2,1,0:T(8,128)(2,1)} %value_up_ref.1) | copy-start | bytes 3145732
  68.8 8.3 %collective-permute-start.4 = (bf16[512,640]{1,0:T(8,128)(2,1)S(1)}, bf16[512,640]{1,0:T(8,128)(2,1)S(1)}, u32[]{:S(2)}, u32[]{:S(2)}) collective-permute-start(bf16[512,640]{1,0:T(8,128)(2,1)S(1)} %sibling_rows.1), channel_id=1, source_target_pairs={{0,8},{8,0},{1,9},{9,1},{2,10},{10,2},{3,11},{11,3},{4,12},{12,4},... | collective-permute-start | bytes 1966088 | tf_op jit(solution)/shard_map/ppermute | solution.py:399

commit v5 on v4

--- a/solution.py
+++ b/solution.py
@@ -12,7 +12,6 @@
 AXES = ("y", "zh", "c", "zl", "x")
 BLK = ("y", "zh", "c")
 HEAD = ("zl", "x")
-PLANE = ("y", "zh", "zl")
 NY, NZH, NC, NZL, NX = 8, 4, 2, 2, 4
 
 LATENT = 512
@@ -243,7 +242,8 @@
 def middle_kernel(
     query_ref,
     place_ref,
-    keys_ref,
+    one_ref,
+    two_ref,
     old_acc_ref,
     old_top_ref,
     old_sum_ref,
@@ -252,7 +252,7 @@
     sum_ref,
 ):
     old = (old_acc_ref, old_top_ref, old_sum_ref)
-    attend(query_ref, place_ref, [keys_ref], old, keep(acc_ref, top_ref, sum_ref))
+    attend(query_ref, place_ref, [one_ref, two_ref], old, keep(acc_ref, top_ref, sum_ref))
 
 
 def send_kernel(query_ref, place_ref, keys_ref, old_acc_ref, old_top_ref, old_sum_ref, out_ref):
@@ -344,18 +344,28 @@
     ]
 
 
+def colours():
+    return [
+        [
+            device_at(y, z, x, c)
+            for y in range(NY)
+            for z in range(NZH * NZL)
+            for x in range(NX)
+            if (x + y + 2 * z) % 4 == colour
+        ]
+        for colour in range(4)
+        for c in range(NC)
+    ]
+
+
 def shards(query_nope, query_rope, compressed, latent_gain, key_up, value_up, span_order):
     f32 = jnp.float32
     bf16 = jnp.bfloat16
     shape = jax.ShapeDtypeStruct
     frequency = jnp.asarray(FREQUENCY)
-    def along_x(y, z, x, c):
-        away = c ^ (y % 2)
-        return (y, z, x + 1, 1) if away else (y, z, x - 1, 0)
-
-    first_pairs = pairs(along_x)
-    onward_pairs = pairs(lambda y, z, x, c: (y, z, x - 1 + 2 * c, c))
-    y_pairs = pairs(lambda y, z, x, c: (y - 1 + 2 * c, z, x, c))
+    x_pairs = pairs(lambda y, z, x, c: (y, z, x - 1 + 2 * c, c))
+    y_pairs = pairs(lambda y, z, x, c: (y + 1 - 2 * c, z, x, 1 - c))
+    z_pairs = pairs(lambda y, z, x, c: (y, z - 1 + 2 * c, x, c))
     sibling_pairs = pairs(lambda y, z, x, c: (y, z, x, 1 - c))
 
     sent = call(
@@ -372,8 +382,12 @@
             pltpu.SemaphoreType.DMA((4,)),
         ],
     )(span_order, compressed, latent_gain[None], frequency)
-    own_keys = lax.all_to_all(sent, PLANE, 0, 0, tiled=True).reshape(512, WIDE)
-    one = lax.ppermute(own_keys, AXES, first_pairs)
+    own_keys = lax.all_to_all(
+        sent, AXES, 0, 0, tiled=True, axis_index_groups=colours()
+    ).reshape(512, WIDE)
+    one = lax.ppermute(own_keys, AXES, x_pairs)
+    two = lax.ppermute(own_keys, AXES, y_pairs)
+    three = lax.ppermute(own_keys, AXES, z_pairs)
     sibling = lax.ppermute(
         jnp.concatenate([query_nope, query_rope], axis=1), AXES, sibling_pairs
     )
@@ -388,12 +402,7 @@
         (shape((2 * ROWS, WIDE), bf16), shape((2 * ROWS, 128), f32), *state),
         "first",
     )(span_order, frequency, query_nope, query_rope, sibling, key_up, own_keys)
-    one, carry = lax.optimization_barrier((one, carry))
-    two = lax.ppermute(one, AXES, onward_pairs)
-    three = lax.ppermute(one, AXES, y_pairs)
-    middle = call(middle_kernel, [VMEM] * 6, state, "middle")
-    carry = middle(queries, places, one, *carry)
-    carry = middle(queries, places, two, *carry)
+    carry = call(middle_kernel, [VMEM] * 7, state, "middle")(queries, places, one, two, *carry)
     ending = (queries, places, three, *carry)
     send = call(send_kernel, [VMEM] * 6, shape((ROWS, WIDE), bf16), "sibling_rows")(*ending)
     got = lax.ppermute(send, AXES, sibling_pairs)

time: 78.6 us -> 71.4 us (0.908)
  starting transfers between devices: 22.7 us -> 15.6 us
  blocking collectives: 35.7 us -> 40.8 us
  waiting for transfers between devices: 6.51 us -> 1.55 us
    all_to_all x1, blocking collectives: 35.7 us -> 40.8 us  [shards(): lax.all_to_all(sent, AXES, 0, 0, tiled=True, axis_index_groups=colours())]
    ppermute x3, waiting for transfers between devices: 4.97 us -> 0.01 us  [the longest x1 0.01 us: shards(): two = lax.ppermute(own_keys, AXES, y_pairs)]
    ppermute x1, starting transfers between devices: 7.17 us -> 2.63 us  [shards(): lax.ppermute(jnp.concatenate([query_nope, query_rope], axis=1), AXES, sib...]
    ppermute x1, starting transfers between devices: 6.56 us -> 2.41 us  [shards(): got = lax.ppermute(send, AXES, sibling_pairs)]
    ppermute x3, starting transfers between devices: 8.94 us -> 10.6 us  [the longest x1 4.98 us: shards(): two = lax.ppermute(own_keys, AXES, y_pairs)]
    pallas_call x2 -> x1, Pallas kernels: 4.01 us -> 3.67 us  [shards(): call(middle_kernel, [VMEM] * 7, state, 'middle')]
  transfers between devices with their start and end apart: 5 -> 5, of which waited for: 4 -> 2; matrix products, arithmetic and copies ran while one was open for 1% -> 1% of each run, Pallas kernels for 10% -> 11%
where the time goes in v5:
time: 71.4 us; the launch traced here: 71.1 us
  blocking collectives  40.8 us (57%)
  starting transfers between devices  15.6 us (22%)
  Pallas kernels  11.9 us (17%)
  waiting for transfers between devices  1.55 us (2%)
  other arithmetic  0.96 us (1%)
    all_to_all x1, blocking collectives, shards(): lax.all_to_all(sent, AXES, 0, 0, tiled=True, axis_index_groups=colours())  40.8 us
    ppermute x1, starting transfers between devices, shards(): two = lax.ppermute(own_keys, AXES, y_pairs)  4.98 us
    ppermute x1, starting transfers between devices, shards(): one = lax.ppermute(own_keys, AXES, x_pairs)  3.7 us
    pallas_call x1, Pallas kernels, shards(): call(middle_kernel, [VMEM] * 7, state, 'middle')  3.67 us
    pallas_call x1, Pallas kernels, shards(): call(first_kernel, [SMEM] + [VMEM] * 6, (shape((2 * ROWS, WIDE), bf16), s...  2.82 us
    ppermute x1, starting transfers between devices, shards(): lax.ppermute(jnp.concatenate([query_nope, query_rope], axis=1), AXES, sib...  2.63 us
    ppermute x1, starting transfers between devices, shards(): got = lax.ppermute(send, AXES, sibling_pairs)  2.41 us
    ppermute x1, starting transfers between devices, shards(): three = lax.ppermute(own_keys, AXES, z_pairs)  1.92 us
  transfers between devices with their start and end apart: 5, of which 2 were waited for; matrix products, arithmetic and copies ran while one was open for 1% of the time, Pallas kernels for 11%

profile of v5, /device:TPU:1, one launch (start us, length us, event | category | flops | bytes accessed | tf_op | source)
XLA Modules:
  0.0 71.1 jit_solution(15209969415967673727)
XLA Ops:
  0.0 0.0 copy-start.2
  0.0 0.0 copy-start.1
  0.0 1.8 %prep.1 = bf16[64,8,640]{2,1,0:T(8,128)(2,1)} custom-call(s32[128]{0:T(128)} %span_ref.1, bf16[8,576]{1,0:T(8,128)(2,1)} %compressed_hbm.1, f32[1,512]{1,0:T(1,128)} %bitcast.6, f32[1,128]{1,0:T(1,128)} %constant.2.clone.frequency_hbm.frequency_ref), custom_call_target="tpu_custom_call" | custom-call | tf_op jit(solution)/shard_map/prep/pallas_call | solution.py:371
  1.9 40.8 %all_to_all.5 = bf16[64,8,640]{2,1,0:T(8,128)(2,1)S(1)} all-to-all(bf16[64,8,640]{2,1,0:T(8,128)(2,1)} %prep.1), channel_id=1, replica_groups={{0,6,16,22,32,38,48,54,67,69,83,85,99,101,115,117,130,132,146,148,162,1..., dimensions={0} | all-to-all | bytes 1310720 | tf_op jit(solution)/shard_map/all_to_all | solution.py:385
  42.7 5.0 %collective-permute-start.3 = (bf16[512,640]{1,0:T(8,128)(2,1)S(1)}, bf16[512,640]{1,0:T(8,128)(2,1)S(1)}, u32[]{:S(2)}, u32[]{:S(2)}) collective-permute-start(bf16[512,640]{1,0:T(8,128)(2,1)S(1)} %bitcast.2), channel_id=1, source_target_pairs={{0,72},{8,448},{1,73},{9,449},{2,74},{10,450},{3,75},{11,451},{4,7... | collective-permute-start | bytes 1966088 | tf_op jit(solution)/shard_map/ppermute | solution.py:389
  47.7 3.7 %collective-permute-start.2 = (bf16[512,640]{1,0:T(8,128)(2,1)S(1)}, bf16[512,640]{1,0:T(8,128)(2,1)S(1)}, u32[]{:S(2)}, u32[]{:S(2)}) collective-permute-start(bf16[512,640]{1,0:T(8,128)(2,1)S(1)} %bitcast.3), channel_id=1, source_target_pairs={{0,3},{8,9},{1,0},{9,10},{2,1},{10,11},{3,2},{11,8},{4,7},{12,13},... | collective-permute-start | bytes 1966088 | tf_op jit(solution)/shard_map/ppermute | solution.py:388
  51.4 1.9 %collective-permute-start.1 = (bf16[512,640]{1,0:T(8,128)(2,1)S(1)}, bf16[512,640]{1,0:T(8,128)(2,1)S(1)}, u32[]{:S(2)}, u32[]{:S(2)}) collective-permute-start(bf16[512,640]{1,0:T(8,128)(2,1)S(1)} %bitcast.4), channel_id=1, source_target_pairs={{0,52},{8,12},{1,53},{9,13},{2,54},{10,14},{3,55},{11,15},{4,0},{1... | collective-permute-start | bytes 1966088 | tf_op jit(solution)/shard_map/ppermute | solution.py:390
  53.4 1.0 %pad_maximum_fusion = bf16[64,1536]{1,0:T(8,128)(2,1)S(1)} fusion(bf16[64,512]{1,0:T(8,128)(2,1)} %rope_ref.1, bf16[64,1024]{1,0:T(8,128)(2,1)} %nope_ref.1), kind=kLoop, calls=%fused_computation | loop fusion | flops 393216 | bytes 393216 | tf_op jit(solution)/shard_map/concatenate | solution.py:392
  54.3 2.6 %collective-permute-start = (bf16[64,1536]{1,0:T(8,128)(2,1)S(1)}, bf16[64,1536]{1,0:T(8,128)(2,1)S(1)}, u32[]{:S(2)}, u32[]{:S(2)}) collective-permute-start(bf16[64,1536]{1,0:T(8,128)(2,1)S(1)} %pad_maximum_fusion), channel_id=1, source_target_pairs={{0,8},{8,0},{1,9},{9,1},{2,10},{10,2},{3,11},{11,3},{4,12},{12,4},... | collective-permute-start | bytes 589832 | tf_op jit(solution)/shard_map/ppermute | solution.py:391
  57.0 1.0 %collective-permute-done.sibling_ref = bf16[64,1536]{1,0:T(8,128)(2,1)S(1)} collective-permute-done((bf16[64,1536]{1,0:T(8,128)(2,1)S(1)}, bf16[64,1536]{1,0:T(8,128)(2,1)S(1)}, u32[]{:S(2)}, u32[]{:S(2)}) %collective-permute-start) | collective-permute-done | bytes 196640 | tf_op jit(solution)/shard_map/ppermute | solution.py:391
  58.0 0.0 copy-done.5
  58.0 0.0 copy-done.3
  58.0 2.8 %first.1 = (bf16[1024,640]{1,0:T(8,128)(2,1)S(1)}, f32[1024,128]{1,0:T(8,128)S(1)}, f32[1024,512]{1,0:T(8,128)S(1)}, f32[1024,128]{1,0:T(8,128)S(1)}, f32[1024,128]{1,0:T(8,128)S(1)}) custom-call(s32[128]{0:T(128)S(1)} %copy-done.4, f32[1,128]{1,0:T(1,128)S(1)} %copy-done.5, bf16[64,1024]{1,0:T(8,128)(2,1)S(1)} %copy-done.2, bf16[64,512]{1,0:T(8,128)(2,1)S(1)} %copy-done.3, ...), custom_call_target="tpu_custom_call" | custom-call | tf_op jit(solution)/shard_map/first/pallas_call | solution.py:399
  60.9 0.0 collective-permute-done.3.two_ref
  60.9 0.0 collective-permute-done.2.one_ref
  60.9 3.7 %middle.1 = (f32[1024,512]{1,0:T(8,128)S(1)}, f32[1024,128]{1,0:T(8,128)S(1)}, f32[1024,128]{1,0:T(8,128)S(1)}) custom-call(bf16[1024,640]{1,0:T(8,128)(2,1)S(1)} %get-tuple-element.16.query_ref, f32[1024,128]{1,0:T(8,128)S(1)} %get-tuple-element.17.place_ref, bf16[512,640]{1,0:T(8,128)(2,1)S(1)} %collective-permute-done.2.one_ref, ...), custom_call_target="tpu_custom_call" | custom-call | tf_op jit(solution)/shard_map/middle/pallas_call | solution.py:405
  64.6 0.0 collective-permute-done.1.keys_ref
  64.6 1.2 %sibling_rows.1 = bf16[512,640]{1,0:T(8,128)(2,1)S(1)} custom-call(bf16[1024,640]{1,0:T(8,128)(2,1)S(1)} %get-tuple-element.16.query_ref, f32[1024,128]{1,0:T(8,128)S(1)} %get-tuple-element.17.place_ref, bf16[512,640]{1,0:T(8,128)(2,1)S(1)} %collective-permute-done.1.keys_ref, f32[1024,512]{1,0:T(8,128)S(1)} %get-tuple-element.21.old_acc_ref, ...), custom_call_target="tpu_custom_call" | custom-call | tf_op jit(solution)/shard_map/sibling_rows/pallas_call | solution.py:407
  65.8 0.0 copy-start
  65.8 2.4 %collective-permute-start.4 = (bf16[512,640]{1,0:T(8,128)(2,1)S(1)}, bf16[512,640]{1,0:T(8,128)(2,1)S(1)}, u32[]{:S(2)}, u32[]{:S(2)}) collective-permute-start(bf16[512,640]{1,0:T(8,128)(2,1)S(1)} %sibling_rows.1), channel_id=1, source_target_pairs={{0,8},{8,0},{1,9},{9,1},{2,10},{10,2},{3,11},{11,3},{4,12},{12,4},... | collective-permute-start | bytes 1966088 | tf_op jit(solution)/shard_map/ppermute | solution.py:408
  68.2 1.2 %own_rows.1 = (f32[512,512]{1,0:T(8,128)S(1)}, f32[512,128]{1,0:T(8,128)S(1)}, f32[512,128]{1,0:T(8,128)S(1)}) custom-call(bf16[1024,640]{1,0:T(8,128)(2,1)S(1)} %get-tuple-element.16.query_ref, f32[1024,128]{1,0:T(8,128)S(1)} %get-tuple-element.17.place_ref, bf16[512,640]{1,0:T(8,128)(2,1)S(1)} %collective-permute-done.1.keys_ref, ...), custom_call_target="tpu_custom_call" | custom-call | tf_op jit(solution)/shard_map/own_rows/pallas_call | solution.py:414
  69.5 0.5 collective-permute-done.4.got_ref
  69.9 0.0 copy-done
  69.9 1.1 %merge.1 = bf16[64,1024]{1,0:T(8,128)(2,1)} custom-call(f32[512,512]{1,0:T(8,128)S(1)} %get-tuple-element.24.acc_ref, f32[512,128]{1,0:T(8,128)S(1)} %get-tuple-element.25.top_ref, f32[512,128]{1,0:T(8,128)S(1)} %get-tuple-element.26.sum_ref, bf16[512,640]{1,0:T(8,128)(2,1)S(1)} %collective-permute-done.4.got_ref, bf16[8,512,128]{2,1,0:T(8,128)(2,1)S(1)} %copy-done), custom_call_target="tpu_custom_call" | custom-call | tf_op jit(solution)/shard_map/merge/pallas_call | solution.py:415
  (6 shorter events, 0.0 us)
Async XLA Ops:
  0.0 58.0 %copy-start.5 = (f32[1,128]{1,0:T(1,128)S(1)}, f32[1,128]{1,0:T(1,128)}, u32[]{:S(2)}) copy-start(f32[1,128]{1,0:T(1,128)} %constant.2.clone.frequency_hbm.frequency_ref) | copy-start | bytes 1540
  0.0 58.0 %copy-start.4 = (s32[128]{0:T(128)S(1)}, s32[128]{0:T(128)}, u32[]{:S(2)}) copy-start(s32[128]{0:T(128)} %span_ref.1) | copy-start | bytes 1540
  0.0 58.0 %copy-start.3 = (bf16[64,512]{1,0:T(8,128)(2,1)S(1)}, bf16[64,512]{1,0:T(8,128)(2,1)}, u32[]{:S(2)}) copy-start(bf16[64,512]{1,0:T(8,128)(2,1)} %rope_ref.1) | copy-start | bytes 196612
  0.0 58.0 %copy-start.2 = (bf16[64,1024]{1,0:T(8,128)(2,1)S(1)}, bf16[64,1024]{1,0:T(8,128)(2,1)}, u32[]{:S(2)}) copy-start(bf16[64,1024]{1,0:T(8,128)(2,1)} %nope_ref.1) | copy-start | bytes 393220
  0.0 58.0 %copy-start.1 = (bf16[8,128,512]{2,1,0:T(8,128)(2,1)S(1)}, bf16[8,128,512]{2,1,0:T(8,128)(2,1)}, u32[]{:S(2)}) copy-start(bf16[8,128,512]{2,1,0:T(8,128)(2,1)} %key_up_ref.1) | copy-start | bytes 3145732
  42.7 18.1 %collective-permute-start.3 = (bf16[512,640]{1,0:T(8,128)(2,1)S(1)}, bf16[512,640]{1,0:T(8,128)(2,1)S(1)}, u32[]{:S(2)}, u32[]{:S(2)}) collective-permute-start(bf16[512,640]{1,0:T(8,128)(2,1)S(1)} %bitcast.2), channel_id=1, source_target_pairs={{0,72},{8,448},{1,73},{9,449},{2,74},{10,450},{3,75},{11,451},{4,7... | collective-permute-start | bytes 1966088 | tf_op jit(solution)/shard_map/ppermute | solution.py:389
  47.7 13.2 %collective-permute-start.2 = (bf16[512,640]{1,0:T(8,128)(2,1)S(1)}, bf16[512,640]{1,0:T(8,128)(2,1)S(1)}, u32[]{:S(2)}, u32[]{:S(2)}) collective-permute-start(bf16[512,640]{1,0:T(8,128)(2,1)S(1)} %bitcast.3), channel_id=1, source_target_pairs={{0,3},{8,9},{1,0},{9,10},{2,1},{10,11},{3,2},{11,8},{4,7},{12,13},... | collective-permute-start | bytes 1966088 | tf_op jit(solution)/shard_map/ppermute | solution.py:388
  51.4 13.1 %collective-permute-start.1 = (bf16[512,640]{1,0:T(8,128)(2,1)S(1)}, bf16[512,640]{1,0:T(8,128)(2,1)S(1)}, u32[]{:S(2)}, u32[]{:S(2)}) collective-permute-start(bf16[512,640]{1,0:T(8,128)(2,1)S(1)} %bitcast.4), channel_id=1, source_target_pairs={{0,52},{8,12},{1,53},{9,13},{2,54},{10,14},{3,55},{11,15},{4,0},{1... | collective-permute-start | bytes 1966088 | tf_op jit(solution)/shard_map/ppermute | solution.py:390
  54.3 3.7 %collective-permute-start = (bf16[64,1536]{1,0:T(8,128)(2,1)S(1)}, bf16[64,1536]{1,0:T(8,128)(2,1)S(1)}, u32[]{:S(2)}, u32[]{:S(2)}) collective-permute-start(bf16[64,1536]{1,0:T(8,128)(2,1)S(1)} %pad_maximum_fusion), channel_id=1, source_target_pairs={{0,8},{8,0},{1,9},{9,1},{2,10},{10,2},{3,11},{11,3},{4,12},{12,4},... | collective-permute-start | bytes 589832 | tf_op jit(solution)/shard_map/ppermute | solution.py:391
  65.8 4.1 %copy-start = (bf16[8,512,128]{2,1,0:T(8,128)(2,1)S(1)}, bf16[8,512,128]{2,1,0:T(8,128)(2,1)}, u32[]{:S(2)}) copy-start(bf16[8,512,128]{2,1,0:T(8,128)(2,1)} %value_up_ref.1) | copy-start | bytes 3145732
  65.8 4.1 %collective-permute-start.4 = (bf16[512,640]{1,0:T(8,128)(2,1)S(1)}, bf16[512,640]{1,0:T(8,128)(2,1)S(1)}, u32[]{:S(2)}, u32[]{:S(2)}) collective-permute-start(bf16[512,640]{1,0:T(8,128)(2,1)S(1)} %sibling_rows.1), channel_id=1, source_target_pairs={{0,8},{8,0},{1,9},{9,1},{2,10},{10,2},{3,11},{11,3},{4,12},{12,4},... | collective-permute-start | bytes 1966088 | tf_op jit(solution)/shard_map/ppermute | solution.py:408

commit v6 on v5

--- a/solution.py
+++ b/solution.py
@@ -1,8 +1,8 @@
 import functools
+import math
 
 import jax
 import jax.numpy as jnp
-import numpy as np
 from jax import lax
 from jax.experimental import pallas as pl
 from jax.experimental.pallas import tpu as pltpu
@@ -23,6 +23,9 @@
 HALF = 32
 WIDE = 640
 ROWS = TOK * HEADS_HERE
+NOPES = HEADS_HERE * NOPE
+ROPES = HEADS_HERE * ROPE
+JOINED = NOPES + ROPES + 128
 CHUNK = 512
 
 norm_epsilon = 1e-06
@@ -31,11 +34,6 @@
 score_scale = (NOPE + ROPE) ** (-0.5)
 log2e = 1.4426950408889634
 
-FREQUENCY = np.tile(
-    np.float32(rope_base) ** (-np.arange(ROPE // 2, dtype=np.float32) / np.float32(ROPE // 2)),
-    128 // (ROPE // 2),
-).astype(np.float32)[None]
-
 VMEM = pl.BlockSpec(memory_space=pltpu.VMEM)
 SMEM = pl.BlockSpec(memory_space=pltpu.SMEM)
 HBM = pl.BlockSpec(memory_space=pltpu.HBM)
@@ -45,13 +43,14 @@
     return lax.broadcasted_iota(jnp.int32, shape, 1)
 
 
-def rotated(values, positions, frequency):
-    lane = lanes_of(values.shape)
-    leading = lane % ROPE < ROPE // 2
-    angles = positions * frequency
-    cosine = jnp.cos(angles)
-    sine_value = jnp.where(leading, -jnp.sin(angles), jnp.sin(angles))
-    return cosine, sine_value, leading
+def rotation(positions):
+    half = ROPE // 2
+    lane = lanes_of(positions.shape)
+    index = (lane % half).astype(jnp.float32)
+    angles = positions * jnp.exp2(index * (-math.log2(rope_base) / half))
+    leading = lane % ROPE < half
+    sine_value = jnp.sin(angles)
+    return jnp.cos(angles), jnp.where(leading, -sine_value, sine_value), leading
 
 
 def apply_rotation(values, cosine, sine_value, leading):
@@ -71,12 +70,14 @@
     span_hbm,
     compressed_hbm,
     gain_hbm,
-    frequency_hbm,
+    nope_hbm,
+    rope_hbm,
     out_ref,
+    joined_hbm,
+    place_ref,
     span_ref,
     compressed_ref,
     gain_ref,
-    frequency_ref,
     sems,
 ):
     copies = [
@@ -86,11 +87,20 @@
                 (compressed_hbm, compressed_ref),
                 (gain_hbm, gain_ref),
                 (span_hbm, span_ref),
-                (frequency_hbm, frequency_ref),
             )
         )
     ]
-    for copy in copies:
+    joins = [
+        pltpu.make_async_copy(source, joined_hbm.at[:, start : start + width], sems.at[3 + k])
+        for k, (source, start, width) in enumerate(
+            (
+                (nope_hbm, 0, NOPES),
+                (rope_hbm, NOPES, ROPES),
+                (place_ref, NOPES + ROPES, 128),
+            )
+        )
+    ]
+    for copy in copies + joins[:2]:
         copy.start()
     for copy in copies:
         copy.wait()
@@ -105,8 +115,7 @@
     rope = compressed_ref[:, LATENT:].astype(jnp.float32)
     rope = jnp.concatenate([rope, jnp.zeros_like(rope)], axis=1)
     positions = (span * HALF + offset).astype(jnp.float32)
-    cosine, sine_value, leading = rotated(rope, positions, frequency_ref[...])
-    turned = apply_rotation(rope, cosine, sine_value, leading)
+    turned = apply_rotation(rope, *rotation(positions))
     lane = lanes_of((rows, 128))
     tail = jnp.where(
         lane < ROPE,
@@ -119,6 +128,17 @@
     ).astype(jnp.bfloat16)
     row = jnp.concatenate([latent, tail], axis=1)
     out_ref[...] = jnp.broadcast_to(row[None], out_ref.shape)
+    token = lax.broadcasted_iota(jnp.int32, (TOK, 128), 0)
+    lane = lanes_of((TOK, 128))
+    span = jnp.where(token < HALF, span_ref[block * 2], span_ref[block * 2 + 1])
+    place_ref[...] = (
+        jnp.where(lane == 0, span, jnp.where(lane == 1, token % HALF, 0))
+        .astype(jnp.float32)
+        .astype(jnp.bfloat16)
+    )
+    joins[2].start()
+    for copy in joins:
+        copy.wait()
 
 
 def key_positions(keys):
@@ -132,12 +152,10 @@
     return found[:8]
 
 
-def query_positions(span_ref, other):
-    block = block_index() + other * (1 - 2 * lax.axis_index("c"))
-    token = lax.broadcasted_iota(jnp.int32, (TOK, 128), 0)
-    first = span_ref[block * 2] * HALF
-    second = span_ref[block * 2 + 1] * HALF - HALF
-    return (token + jnp.where(token < HALF, first, second)).astype(jnp.float32)
+def query_positions(places):
+    row = lax.broadcasted_iota(jnp.int32, (128, 128), 0)
+    pick = jnp.where(row == 0, float(HALF), jnp.where(row == 1, 1.0, 0.0)).astype(jnp.bfloat16)
+    return jnp.dot(places, pick, preferred_element_type=jnp.float32)
 
 
 def attend(query_ref, place_ref, key_refs, carry, finish, rows=(0, 2 * ROWS)):
@@ -196,11 +214,14 @@
     return finish
 
 
+def pair_kernel(own_ref, other_ref, whole_ref):
+    rows = own_ref.shape[0]
+    whole_ref[:rows, :] = own_ref[...]
+    whole_ref[rows:, :] = other_ref[...]
+
+
 def first_kernel(
-    span_ref,
-    frequency_ref,
-    nope_ref,
-    rope_ref,
+    own_ref,
     sibling_ref,
     key_up_ref,
     keys_ref,
@@ -210,10 +231,11 @@
     top_ref,
     sum_ref,
 ):
-    nope = jnp.concatenate([nope_ref[...], sibling_ref[:, : HEADS_HERE * NOPE]], axis=0)
-    rope = jnp.concatenate([rope_ref[...], sibling_ref[:, HEADS_HERE * NOPE :]], axis=0)
-    positions = jnp.concatenate([query_positions(span_ref, other) for other in range(2)], axis=0)
-    cosine, sine_value, leading = rotated(positions, positions, frequency_ref[...])
+    both = jnp.concatenate([own_ref[...], sibling_ref[...]], axis=0)
+    nope = both[:, :NOPES]
+    rope = both[:, NOPES : NOPES + ROPES]
+    positions = query_positions(both[:, NOPES + ROPES :])
+    turning = rotation(positions)
     lane = lanes_of((2 * TOK, 128))
     for head in range(HEADS_HERE):
         raised = jnp.dot(
@@ -223,10 +245,7 @@
         ).astype(jnp.bfloat16)
         if head % 2 == 0:
             turned = apply_rotation(
-                rope[:, head * ROPE : head * ROPE + 128].astype(jnp.float32),
-                cosine,
-                sine_value,
-                leading,
+                rope[:, head * ROPE : head * ROPE + 128].astype(jnp.float32), *turning
             )
         else:
             turned = pltpu.roll(turned, ROPE, 1)
@@ -244,6 +263,7 @@
     place_ref,
     one_ref,
     two_ref,
+    four_ref,
     old_acc_ref,
     old_top_ref,
     old_sum_ref,
@@ -252,7 +272,9 @@
     sum_ref,
 ):
     old = (old_acc_ref, old_top_ref, old_sum_ref)
-    attend(query_ref, place_ref, [one_ref, two_ref], old, keep(acc_ref, top_ref, sum_ref))
+    attend(
+        query_ref, place_ref, [one_ref, two_ref, four_ref], old, keep(acc_ref, top_ref, sum_ref)
+    )
 
 
 def send_kernel(query_ref, place_ref, keys_ref, old_acc_ref, old_top_ref, old_sum_ref, out_ref):
@@ -316,8 +338,8 @@
         ).astype(jnp.bfloat16)
 
 
-def call(kernel, specs, out_shape, name, vmem=32, scratch=()):
-    out_specs = jax.tree.map(lambda _: VMEM, out_shape)
+def call(kernel, specs, out_shape, name, vmem=32, scratch=(), out_specs=None):
+    out_specs = out_specs or jax.tree.map(lambda _: VMEM, out_shape)
     return pl.pallas_call(
         kernel,
         in_specs=specs,
@@ -351,9 +373,9 @@
             for y in range(NY)
             for z in range(NZH * NZL)
             for x in range(NX)
-            if (x + y + 2 * z) % 4 == colour
+            if (2 * x + y + 3 * z) % 8 == colour
         ]
-        for colour in range(4)
+        for colour in range(8)
         for c in range(NC)
     ]
 
@@ -362,35 +384,39 @@
     f32 = jnp.float32
     bf16 = jnp.bfloat16
     shape = jax.ShapeDtypeStruct
-    frequency = jnp.asarray(FREQUENCY)
     x_pairs = pairs(lambda y, z, x, c: (y, z, x - 1 + 2 * c, c))
-    y_pairs = pairs(lambda y, z, x, c: (y + 1 - 2 * c, z, x, 1 - c))
+    y_pairs = pairs(lambda y, z, x, c: (y - 1 + 2 * c, z, x, c))
     z_pairs = pairs(lambda y, z, x, c: (y, z - 1 + 2 * c, x, c))
+    yz_pairs = pairs(lambda y, z, x, c: (y - 1 + 2 * c, z - 1 + 2 * c, x, c))
     sibling_pairs = pairs(lambda y, z, x, c: (y, z, x, 1 - c))
 
-    sent = call(
+    sent, joined = call(
         prep_kernel,
-        [HBM] * 4,
-        shape((64, 8, WIDE), bf16),
+        [HBM] * 5,
+        (shape((32, 8, WIDE), bf16), shape((TOK, JOINED), bf16)),
         "prep",
         60,
         [
+            pltpu.VMEM((TOK, 128), bf16),
             pltpu.SMEM((128,), jnp.int32),
             pltpu.VMEM((8, LATENT + ROPE), bf16),
             pltpu.VMEM((1, LATENT), f32),
-            pltpu.VMEM((1, 128), f32),
-            pltpu.SemaphoreType.DMA((4,)),
+            pltpu.SemaphoreType.DMA((6,)),
         ],
-    )(span_order, compressed, latent_gain[None], frequency)
+        (VMEM, HBM),
+    )(span_order, compressed, latent_gain[None], query_nope, query_rope)
     own_keys = lax.all_to_all(
         sent, AXES, 0, 0, tiled=True, axis_index_groups=colours()
-    ).reshape(512, WIDE)
-    one = lax.ppermute(own_keys, AXES, x_pairs)
-    two = lax.ppermute(own_keys, AXES, y_pairs)
-    three = lax.ppermute(own_keys, AXES, z_pairs)
-    sibling = lax.ppermute(
-        jnp.concatenate([query_nope, query_rope], axis=1), AXES, sibling_pairs
-    )
+    ).reshape(256, WIDE)
+    other_half = lax.ppermute(own_keys, AXES, sibling_pairs)
+    four = lax.ppermute(own_keys, AXES, yz_pairs)
+    whole = call(pair_kernel, [VMEM] * 2, shape((512, WIDE), bf16), "pair", 8)(
+        own_keys, other_half
+    )
+    one = lax.ppermute(whole, AXES, x_pairs)
+    two = lax.ppermute(whole, AXES, y_pairs)
+    three = lax.ppermute(whole, AXES, z_pairs)
+    sibling = lax.ppermute(joined, AXES, sibling_pairs)
     state = (
         shape((2 * ROWS, LATENT), f32),
         shape((2 * ROWS, 128), f32),
@@ -398,11 +424,13 @@
     )
     queries, places, *carry = call(
         first_kernel,
-        [SMEM] + [VMEM] * 6,
+        [VMEM] * 4,
         (shape((2 * ROWS, WIDE), bf16), shape((2 * ROWS, 128), f32), *state),
         "first",
-    )(span_order, frequency, query_nope, query_rope, sibling, key_up, own_keys)
-    carry = call(middle_kernel, [VMEM] * 7, state, "middle")(queries, places, one, two, *carry)
+    )(joined, sibling, key_up, own_keys)
+    carry = call(middle_kernel, [VMEM] * 8, state, "middle")(
+        queries, places, one, two, four, *carry
+    )
     ending = (queries, places, three, *carry)
     send = call(send_kernel, [VMEM] * 6, shape((ROWS, WIDE), bf16), "sibling_rows")(*ending)
     got = lax.ppermute(send, AXES, sibling_pairs)

time: 71.4 us -> 78.2 us (1.095)
  blocking collectives: 40.8 us -> 32.6 us
  starting transfers between devices: 15.6 us -> 23.2 us
  Pallas kernels: 11.9 us -> 18.3 us
  waiting for transfers between devices: 1.55 us -> 3.54 us
  other arithmetic: 0.96 us -> 0 us
    all_to_all x1, blocking collectives: 40.8 us -> 32.6 us  [shards(): lax.all_to_all(sent, AXES, 0, 0, tiled=True, axis_index_groups=colours())]
    ppermute x4 -> x6, starting transfers between devices: 13.2 us -> 20.3 us  [the longest x1 5.07 us: shards(): other_half = lax.ppermute(own_keys, AXES, sibling_pairs)]
    pallas_call x3 -> x4, Pallas kernels: 8.34 us -> 14.8 us  [the longest x1 7.82 us: shards(): call(prep_kernel, [HBM] * 5, (shape((32, 8, WIDE), bf16), shape((TOK, JOI...]
    ppermute x4 -> x6, waiting for transfers between devices: 1.06 us -> 3.05 us  [the longest x1 1.28 us: shards(): sibling = lax.ppermute(joined, AXES, sibling_pairs)]
    concatenate x1 -> x0, other arithmetic: 0.96 us -> none  [shards(): jnp.concatenate([query_nope, query_rope], axis=1)]
  transfers between devices with their start and end apart: 5 -> 7, of which waited for: 2 -> 4; matrix products, arithmetic and copies ran while one was open for 1% -> 0% of each run, Pallas kernels for 11% -> 10%
where the time goes in v6:
time: 78.2 us; the launch traced here: 77.8 us
  blocking collectives  32.6 us (42%)
  starting transfers between devices  23.2 us (30%)
  Pallas kernels  18.3 us (23%)
  waiting for transfers between devices  3.54 us (5%)
    all_to_all x1, blocking collectives, shards(): lax.all_to_all(sent, AXES, 0, 0, tiled=True, axis_index_groups=colours())  32.6 us
    pallas_call x1, Pallas kernels, shards(): call(prep_kernel, [HBM] * 5, (shape((32, 8, WIDE), bf16), shape((TOK, JOI...  7.82 us
    ppermute x1, starting transfers between devices, shards(): other_half = lax.ppermute(own_keys, AXES, sibling_pairs)  5.07 us
    pallas_call x1, Pallas kernels, shards(): call(middle_kernel, [VMEM] * 8, state, 'middle')  4.8 us
    ppermute x1, starting transfers between devices, shards(): sibling = lax.ppermute(joined, AXES, sibling_pairs)  4.33 us
    ppermute x1, starting transfers between devices, shards(): one = lax.ppermute(whole, AXES, x_pairs)  3.7 us
    ppermute x1, starting transfers between devices, shards(): four = lax.ppermute(own_keys, AXES, yz_pairs)  2.97 us
    ppermute x1, starting transfers between devices, shards(): got = lax.ppermute(send, AXES, sibling_pairs)  2.91 us
  transfers between devices with their start and end apart: 7, of which 4 were waited for; matrix products, arithmetic and copies ran while one was open for 0% of the time, Pallas kernels for 10%

profile of v6, /device:TPU:1, one launch (start us, length us, event | category | flops | bytes accessed | tf_op | source)
XLA Modules:
  0.0 77.8 jit_solution(15419510070759395312)
XLA Ops:
  0.0 7.8 %prep.1 = (bf16[32,8,640]{2,1,0:T(8,128)(2,1)}, bf16[64,1664]{1,0:T(8,128)(2,1)}) custom-call(s32[128]{0:T(128)} %span_hbm.1, bf16[8,576]{1,0:T(8,128)(2,1)} %compressed_hbm.1, f32[1,512]{1,0:T(1,128)} %bitcast.6, bf16[64,1024]{1,0:T(8,128)(2,1)} %nope_hbm.1, bf16[64,512]{1,0:T(8,128)(2,1)} %rope_hbm.1), custom_call_target="tpu_custom_call" | custom-call | tf_op jit(solution)/shard_map/prep/pallas_call | solution.py:393
  7.8 32.6 %all_to_all.5 = bf16[32,8,640]{2,1,0:T(8,128)(2,1)S(1)} all-to-all(bf16[32,8,640]{2,1,0:T(8,128)(2,1)} %get-tuple-element.19), channel_id=1, replica_groups={{0,17,34,51,70,87,100,117,131,144,161,178,197,214,231,244,258,275,288,3..., dimensions={0} | all-to-all | bytes 655360 | tf_op jit(solution)/shard_map/all_to_all | solution.py:408
  40.4 5.1 %collective-permute-start.1 = (bf16[256,640]{1,0:T(8,128)(2,1)S(1)}, bf16[256,640]{1,0:T(8,128)(2,1)S(1)}, u32[]{:S(2)}, u32[]{:S(2)}) collective-permute-start(bf16[256,640]{1,0:T(8,128)(2,1)S(1)} %bitcast.2), channel_id=1, source_target_pairs={{0,8},{8,0},{1,9},{9,1},{2,10},{10,2},{3,11},{11,3},{4,12},{12,4},... | collective-permute-start | bytes 983048 | tf_op jit(solution)/shard_map/ppermute | solution.py:411
  45.5 1.2 %collective-permute-done.1.other_ref = bf16[256,640]{1,0:T(8,128)(2,1)S(1)} collective-permute-done((bf16[256,640]{1,0:T(8,128)(2,1)S(1)}, bf16[256,640]{1,0:T(8,128)(2,1)S(1)}, u32[]{:S(2)}, u32[]{:S(2)}) %collective-permute-start.1) | collective-permute-done | bytes 327712 | tf_op jit(solution)/shard_map/ppermute | solution.py:411
  46.7 0.1 pair.1
  46.8 2.3 %collective-permute-start.4 = (bf16[512,640]{1,0:T(8,128)(2,1)S(1)}, bf16[512,640]{1,0:T(8,128)(2,1)S(1)}, u32[]{:S(2)}, u32[]{:S(2)}) collective-permute-start(bf16[512,640]{1,0:T(8,128)(2,1)S(1)} %pair.1), channel_id=1, source_target_pairs={{0,448},{8,72},{1,449},{9,73},{2,450},{10,74},{3,451},{11,75},{4,4... | collective-permute-start | bytes 1966088 | tf_op jit(solution)/shard_map/ppermute | solution.py:417
  49.1 3.7 %collective-permute-start.3 = (bf16[512,640]{1,0:T(8,128)(2,1)S(1)}, bf16[512,640]{1,0:T(8,128)(2,1)S(1)}, u32[]{:S(2)}, u32[]{:S(2)}) collective-permute-start(bf16[512,640]{1,0:T(8,128)(2,1)S(1)} %pair.1), channel_id=1, source_target_pairs={{0,3},{8,9},{1,0},{9,10},{2,1},{10,11},{3,2},{11,8},{4,7},{12,13},... | collective-permute-start | bytes 1966088 | tf_op jit(solution)/shard_map/ppermute | solution.py:416
  52.8 1.9 %collective-permute-start.2 = (bf16[512,640]{1,0:T(8,128)(2,1)S(1)}, bf16[512,640]{1,0:T(8,128)(2,1)S(1)}, u32[]{:S(2)}, u32[]{:S(2)}) collective-permute-start(bf16[512,640]{1,0:T(8,128)(2,1)S(1)} %pair.1), channel_id=1, source_target_pairs={{0,52},{8,12},{1,53},{9,13},{2,54},{10,14},{3,55},{11,15},{4,0},{1... | collective-permute-start | bytes 1966088 | tf_op jit(solution)/shard_map/ppermute | solution.py:418
  54.7 3.0 %collective-permute-start.5 = (bf16[256,640]{1,0:T(8,128)(2,1)S(1)}, bf16[256,640]{1,0:T(8,128)(2,1)S(1)}, u32[]{:S(2)}, u32[]{:S(2)}) collective-permute-start(bf16[256,640]{1,0:T(8,128)(2,1)S(1)} %bitcast.4), channel_id=1, source_target_pairs={{0,500},{8,76},{1,501},{9,77},{2,502},{10,78},{3,503},{11,79},{4,4... | collective-permute-start | bytes 983048 | tf_op jit(solution)/shard_map/ppermute | solution.py:412
  57.7 4.3 %collective-permute-start = (bf16[64,1664]{1,0:T(8,128)(2,1)}, bf16[64,1664]{1,0:T(8,128)(2,1)S(1)}, u32[]{:S(2)}, u32[]{:S(2)}) collective-permute-start(bf16[64,1664]{1,0:T(8,128)(2,1)} %get-tuple-element.18.own_ref), channel_id=1, source_target_pairs={{0,8},{8,0},{1,9},{9,1},{2,10},{10,2},{3,11},{11,3},{4,12},{12,4},... | collective-permute-start | bytes 638984 | tf_op jit(solution)/shard_map/ppermute | solution.py:419
  62.1 1.3 %collective-permute-done.sibling_ref = bf16[64,1664]{1,0:T(8,128)(2,1)S(1)} collective-permute-done((bf16[64,1664]{1,0:T(8,128)(2,1)}, bf16[64,1664]{1,0:T(8,128)(2,1)S(1)}, u32[]{:S(2)}, u32[]{:S(2)}) %collective-permute-start) | collective-permute-done | bytes 213024 | tf_op jit(solution)/shard_map/ppermute | solution.py:419
  63.3 0.0 copy-done
  63.3 2.1 %first.1 = (bf16[1024,640]{1,0:T(8,128)(2,1)S(1)}, f32[1024,128]{1,0:T(8,128)S(1)}, f32[1024,512]{1,0:T(8,128)S(1)}, f32[1024,128]{1,0:T(8,128)S(1)}, f32[1024,128]{1,0:T(8,128)S(1)}) custom-call(bf16[64,1664]{1,0:T(8,128)(2,1)S(1)} %copy-done.2, bf16[64,1664]{1,0:T(8,128)(2,1)S(1)} %collective-permute-done.sibling_ref, bf16[8,128,512]{2,1,0:T(8,128)(2,1)S(1)} %copy-done, ...), custom_call_target="tpu_custom_call" | custom-call | tf_op jit(solution)/shard_map/first/pallas_call | solution.py:425
  65.5 0.5 collective-permute-done.5.four_ref
  66.0 0.0 collective-permute-done.4.two_ref
  66.0 0.0 collective-permute-done.3.one_ref
  66.0 4.8 %middle.1 = (f32[1024,512]{1,0:T(8,128)S(1)}, f32[1024,128]{1,0:T(8,128)S(1)}, f32[1024,128]{1,0:T(8,128)S(1)}) custom-call(bf16[1024,640]{1,0:T(8,128)(2,1)S(1)} %get-tuple-element.20.query_ref, f32[1024,128]{1,0:T(8,128)S(1)} %get-tuple-element.21.place_ref, bf16[512,640]{1,0:T(8,128)(2,1)S(1)} %collective-permute-done.3.one_ref, ...), custom_call_target="tpu_custom_call" | custom-call | tf_op jit(solution)/shard_map/middle/pallas_call | solution.py:431
  70.8 0.0 collective-permute-done.2.keys_ref
  70.8 1.2 %sibling_rows.1 = bf16[512,640]{1,0:T(8,128)(2,1)S(1)} custom-call(bf16[1024,640]{1,0:T(8,128)(2,1)S(1)} %get-tuple-element.20.query_ref, f32[1024,128]{1,0:T(8,128)S(1)} %get-tuple-element.21.place_ref, bf16[512,640]{1,0:T(8,128)(2,1)S(1)} %collective-permute-done.2.keys_ref, f32[1024,512]{1,0:T(8,128)S(1)} %get-tuple-element.25.old_acc_ref, ...), custom_call_target="tpu_custom_call" | custom-call | tf_op jit(solution)/shard_map/sibling_rows/pallas_call | solution.py:435
  72.1 0.0 copy-start.1
  72.1 2.9 %collective-permute-start.6 = (bf16[512,640]{1,0:T(8,128)(2,1)S(1)}, bf16[512,640]{1,0:T(8,128)(2,1)S(1)}, u32[]{:S(2)}, u32[]{:S(2)}) collective-permute-start(bf16[512,640]{1,0:T(8,128)(2,1)S(1)} %sibling_rows.1), channel_id=1, source_target_pairs={{0,8},{8,0},{1,9},{9,1},{2,10},{10,2},{3,11},{11,3},{4,12},{12,4},... | collective-permute-start | bytes 1966088 | tf_op jit(solution)/shard_map/ppermute | solution.py:436
  75.0 1.2 %own_rows.1 = (f32[512,512]{1,0:T(8,128)S(1)}, f32[512,128]{1,0:T(8,128)S(1)}, f32[512,128]{1,0:T(8,128)S(1)}) custom-call(bf16[1024,640]{1,0:T(8,128)(2,1)S(1)} %get-tuple-element.20.query_ref, f32[1024,128]{1,0:T(8,128)S(1)} %get-tuple-element.21.place_ref, bf16[512,640]{1,0:T(8,128)(2,1)S(1)} %collective-permute-done.2.keys_ref, ...), custom_call_target="tpu_custom_call" | custom-call | tf_op jit(solution)/shard_map/own_rows/pallas_call | solution.py:442
  76.2 0.5 collective-permute-done.6.got_ref
  76.7 1.1 %merge.1 = bf16[64,1024]{1,0:T(8,128)(2,1)} custom-call(f32[512,512]{1,0:T(8,128)S(1)} %get-tuple-element.28.acc_ref, f32[512,128]{1,0:T(8,128)S(1)} %get-tuple-element.29.top_ref, f32[512,128]{1,0:T(8,128)S(1)} %get-tuple-element.30.sum_ref, bf16[512,640]{1,0:T(8,128)(2,1)S(1)} %collective-permute-done.6.got_ref, bf16[8,512,128]{2,1,0:T(8,128)(2,1)S(1)} %copy-done.1), custom_call_target="tpu_custom_call" | custom-call | tf_op jit(solution)/shard_map/merge/pallas_call | solution.py:443
  (4 shorter events, 0.0 us)
Async XLA Ops:
  0.0 63.3 %copy-start = (bf16[8,128,512]{2,1,0:T(8,128)(2,1)S(1)}, bf16[8,128,512]{2,1,0:T(8,128)(2,1)}, u32[]{:S(2)}) copy-start(bf16[8,128,512]{2,1,0:T(8,128)(2,1)} %key_up_ref.1) | copy-start | bytes 3145732
  7.8 55.5 %copy-start.2 = (bf16[64,1664]{1,0:T(8,128)(2,1)S(1)}, bf16[64,1664]{1,0:T(8,128)(2,1)}, u32[]{:S(2)}) copy-start(bf16[64,1664]{1,0:T(8,128)(2,1)} %get-tuple-element.18.own_ref) | copy-start | bytes 638980
  40.4 6.3 %collective-permute-start.1 = (bf16[256,640]{1,0:T(8,128)(2,1)S(1)}, bf16[256,640]{1,0:T(8,128)(2,1)S(1)}, u32[]{:S(2)}, u32[]{:S(2)}) collective-permute-start(bf16[256,640]{1,0:T(8,128)(2,1)S(1)} %bitcast.2), channel_id=1, source_target_pairs={{0,8},{8,0},{1,9},{9,1},{2,10},{10,2},{3,11},{11,3},{4,12},{12,4},... | collective-permute-start | bytes 983048 | tf_op jit(solution)/shard_map/ppermute | solution.py:411
  46.8 19.2 %collective-permute-start.4 = (bf16[512,640]{1,0:T(8,128)(2,1)S(1)}, bf16[512,640]{1,0:T(8,128)(2,1)S(1)}, u32[]{:S(2)}, u32[]{:S(2)}) collective-permute-start(bf16[512,640]{1,0:T(8,128)(2,1)S(1)} %pair.1), channel_id=1, source_target_pairs={{0,448},{8,72},{1,449},{9,73},{2,450},{10,74},{3,451},{11,75},{4,4... | collective-permute-start | bytes 1966088 | tf_op jit(solution)/shard_map/ppermute | solution.py:417
  49.1 16.9 %collective-permute-start.3 = (bf16[512,640]{1,0:T(8,128)(2,1)S(1)}, bf16[512,640]{1,0:T(8,128)(2,1)S(1)}, u32[]{:S(2)}, u32[]{:S(2)}) collective-permute-start(bf16[512,640]{1,0:T(8,128)(2,1)S(1)} %pair.1), channel_id=1, source_target_pairs={{0,3},{8,9},{1,0},{9,10},{2,1},{10,11},{3,2},{11,8},{4,7},{12,13},... | collective-permute-start | bytes 1966088 | tf_op jit(solution)/shard_map/ppermute | solution.py:416
  52.8 18.0 %collective-permute-start.2 = (bf16[512,640]{1,0:T(8,128)(2,1)S(1)}, bf16[512,640]{1,0:T(8,128)(2,1)S(1)}, u32[]{:S(2)}, u32[]{:S(2)}) collective-permute-start(bf16[512,640]{1,0:T(8,128)(2,1)S(1)} %pair.1), channel_id=1, source_target_pairs={{0,52},{8,12},{1,53},{9,13},{2,54},{10,14},{3,55},{11,15},{4,0},{1... | collective-permute-start | bytes 1966088 | tf_op jit(solution)/shard_map/ppermute | solution.py:418
  54.7 11.2 %collective-permute-start.5 = (bf16[256,640]{1,0:T(8,128)(2,1)S(1)}, bf16[256,640]{1,0:T(8,128)(2,1)S(1)}, u32[]{:S(2)}, u32[]{:S(2)}) collective-permute-start(bf16[256,640]{1,0:T(8,128)(2,1)S(1)} %bitcast.4), channel_id=1, source_target_pairs={{0,500},{8,76},{1,501},{9,77},{2,502},{10,78},{3,503},{11,79},{4,4... | collective-permute-start | bytes 983048 | tf_op jit(solution)/shard_map/ppermute | solution.py:412
  57.7 5.6 %collective-permute-start = (bf16[64,1664]{1,0:T(8,128)(2,1)}, bf16[64,1664]{1,0:T(8,128)(2,1)S(1)}, u32[]{:S(2)}, u32[]{:S(2)}) collective-permute-start(bf16[64,1664]{1,0:T(8,128)(2,1)} %get-tuple-element.18.own_ref), channel_id=1, source_target_pairs={{0,8},{8,0},{1,9},{9,1},{2,10},{10,2},{3,11},{11,3},{4,12},{12,4},... | collective-permute-start | bytes 638984 | tf_op jit(solution)/shard_map/ppermute | solution.py:419
  72.1 4.6 %copy-start.1 = (bf16[8,512,128]{2,1,0:T(8,128)(2,1)S(1)}, bf16[8,512,128]{2,1,0:T(8,128)(2,1)}, u32[]{:S(2)}) copy-start(bf16[8,512,128]{2,1,0:T(8,128)(2,1)} %value_up_ref.1) | copy-start | bytes 3145732
  72.1 4.6 %collective-permute-start.6 = (bf16[512,640]{1,0:T(8,128)(2,1)S(1)}, bf16[512,640]{1,0:T(8,128)(2,1)S(1)}, u32[]{:S(2)}, u32[]{:S(2)}) collective-permute-start(bf16[512,640]{1,0:T(8,128)(2,1)S(1)} %sibling_rows.1), channel_id=1, source_target_pairs={{0,8},{8,0},{1,9},{9,1},{2,10},{10,2},{3,11},{11,3},{4,12},{12,4},... | collective-permute-start | bytes 1966088 | tf_op jit(solution)/shard_map/ppermute | solution.py:436

commit v7 on v6

--- a/solution.py
+++ b/solution.py
@@ -73,8 +73,7 @@
     nope_hbm,
     rope_hbm,
     out_ref,
-    joined_hbm,
-    place_ref,
+    joined_ref,
     span_ref,
     compressed_ref,
     gain_ref,
@@ -91,16 +90,15 @@
         )
     ]
     joins = [
-        pltpu.make_async_copy(source, joined_hbm.at[:, start : start + width], sems.at[3 + k])
+        pltpu.make_async_copy(source, joined_ref.at[:, start : start + width], sems.at[3 + k])
         for k, (source, start, width) in enumerate(
             (
                 (nope_hbm, 0, NOPES),
                 (rope_hbm, NOPES, ROPES),
-                (place_ref, NOPES + ROPES, 128),
             )
         )
     ]
-    for copy in copies + joins[:2]:
+    for copy in copies + joins:
         copy.start()
     for copy in copies:
         copy.wait()
@@ -131,12 +129,11 @@
     token = lax.broadcasted_iota(jnp.int32, (TOK, 128), 0)
     lane = lanes_of((TOK, 128))
     span = jnp.where(token < HALF, span_ref[block * 2], span_ref[block * 2 + 1])
-    place_ref[...] = (
+    joined_ref[:, NOPES + ROPES :] = (
         jnp.where(lane == 0, span, jnp.where(lane == 1, token % HALF, 0))
         .astype(jnp.float32)
         .astype(jnp.bfloat16)
     )
-    joins[2].start()
     for copy in joins:
         copy.wait()
 
@@ -263,7 +260,6 @@
     place_ref,
     one_ref,
     two_ref,
-    four_ref,
     old_acc_ref,
     old_top_ref,
     old_sum_ref,
@@ -272,12 +268,12 @@
     sum_ref,
 ):
     old = (old_acc_ref, old_top_ref, old_sum_ref)
-    attend(
-        query_ref, place_ref, [one_ref, two_ref, four_ref], old, keep(acc_ref, top_ref, sum_ref)
-    )
-
-
-def send_kernel(query_ref, place_ref, keys_ref, old_acc_ref, old_top_ref, old_sum_ref, out_ref):
+    attend(query_ref, place_ref, [one_ref, two_ref], old, keep(acc_ref, top_ref, sum_ref))
+
+
+def send_kernel(
+    query_ref, place_ref, keys_ref, four_ref, old_acc_ref, old_top_ref, old_sum_ref, out_ref
+):
     def finish(start, product, top, total):
         at = start % ROWS
         whole = jnp.broadcast_to(jnp.sum(total, axis=1, keepdims=True), (CHUNK, 128))
@@ -295,13 +291,14 @@
         out_ref[at : at + CHUNK, LATENT:] = pieces.astype(jnp.bfloat16)
 
     old = (old_acc_ref, old_top_ref, old_sum_ref)
-    attend(query_ref, place_ref, [keys_ref], old, finish, (ROWS, 2 * ROWS))
+    attend(query_ref, place_ref, [keys_ref, four_ref], old, finish, (ROWS, 2 * ROWS))
 
 
 def own_kernel(
     query_ref,
     place_ref,
     keys_ref,
+    four_ref,
     old_acc_ref,
     old_top_ref,
     old_sum_ref,
@@ -317,7 +314,7 @@
         )
 
     old = (old_acc_ref, old_top_ref, old_sum_ref)
-    attend(query_ref, place_ref, [keys_ref], old, finish, (0, ROWS))
+    attend(query_ref, place_ref, [keys_ref, four_ref], old, finish, (0, ROWS))
 
 
 def merge_kernel(acc_ref, top_ref, sum_ref, got_ref, value_up_ref, out_ref):
@@ -397,18 +394,18 @@
         "prep",
         60,
         [
-            pltpu.VMEM((TOK, 128), bf16),
             pltpu.SMEM((128,), jnp.int32),
             pltpu.VMEM((8, LATENT + ROPE), bf16),
             pltpu.VMEM((1, LATENT), f32),
-            pltpu.SemaphoreType.DMA((6,)),
+            pltpu.SemaphoreType.DMA((5,)),
         ],
-        (VMEM, HBM),
     )(span_order, compressed, latent_gain[None], query_nope, query_rope)
     own_keys = lax.all_to_all(
         sent, AXES, 0, 0, tiled=True, axis_index_groups=colours()
     ).reshape(256, WIDE)
     other_half = lax.ppermute(own_keys, AXES, sibling_pairs)
+    sibling = lax.ppermute(joined, AXES, sibling_pairs)
+    other_half, sibling = lax.optimization_barrier((other_half, sibling))
     four = lax.ppermute(own_keys, AXES, yz_pairs)
     whole = call(pair_kernel, [VMEM] * 2, shape((512, WIDE), bf16), "pair", 8)(
         own_keys, other_half
@@ -416,7 +413,6 @@
     one = lax.ppermute(whole, AXES, x_pairs)
     two = lax.ppermute(whole, AXES, y_pairs)
     three = lax.ppermute(whole, AXES, z_pairs)
-    sibling = lax.ppermute(joined, AXES, sibling_pairs)
     state = (
         shape((2 * ROWS, LATENT), f32),
         shape((2 * ROWS, 128), f32),
@@ -428,18 +424,16 @@
         (shape((2 * ROWS, WIDE), bf16), shape((2 * ROWS, 128), f32), *state),
         "first",
     )(joined, sibling, key_up, own_keys)
-    carry = call(middle_kernel, [VMEM] * 8, state, "middle")(
-        queries, places, one, two, four, *carry
-    )
-    ending = (queries, places, three, *carry)
-    send = call(send_kernel, [VMEM] * 6, shape((ROWS, WIDE), bf16), "sibling_rows")(*ending)
+    carry = call(middle_kernel, [VMEM] * 7, state, "middle")(queries, places, one, two, *carry)
+    ending = (queries, places, three, four, *carry)
+    send = call(send_kernel, [VMEM] * 7, shape((ROWS, WIDE), bf16), "sibling_rows")(*ending)
     got = lax.ppermute(send, AXES, sibling_pairs)
     own_state = (
         shape((ROWS, LATENT), f32),
         shape((ROWS, 128), f32),
         shape((ROWS, 128), f32),
     )
-    own = call(own_kernel, [VMEM] * 6, own_state, "own_rows")(*ending)
+    own = call(own_kernel, [VMEM] * 7, own_state, "own_rows")(*ending)
     return call(
         merge_kernel, [VMEM] * 5, shape((TOK, HEADS_HERE * VDIM), bf16), "merge", 16
     )(*own, got, value_up)

time: 78.2 us -> 75.5 us (0.965)
  Pallas kernels: 18.3 us -> 13.7 us
  waiting for transfers between devices: 3.54 us -> 6.97 us
  starting transfers between devices: 23.2 us -> 21.7 us
    pallas_call x1, Pallas kernels: 7.82 us -> 1.87 us  [shards(): call(prep_kernel, [HBM] * 5, (shape((32, 8, WIDE), bf16), shape((TOK, JOI...]
    ppermute x1, waiting for transfers between devices: 0.01 us -> 2.87 us  [shards(): three = lax.ppermute(whole, AXES, z_pairs)]
    ppermute x1, starting transfers between devices: 4.33 us -> 1.92 us  [shards(): sibling = lax.ppermute(joined, AXES, sibling_pairs)]
    ppermute x1, waiting for transfers between devices: 0.01 us -> 1.78 us  [shards(): one = lax.ppermute(whole, AXES, x_pairs)]
    pallas_call x3, Pallas kernels: 7.24 us -> 8.57 us  [the longest x1 3.67 us: shards(): call(middle_kernel, [VMEM] * 7, state, 'middle')]
    ppermute x1, waiting for transfers between devices: 1.23 us -> 0.01 us  [shards(): other_half = lax.ppermute(own_keys, AXES, sibling_pairs)]
    ppermute x1, starting transfers between devices: 2.91 us -> 3.76 us  [shards(): got = lax.ppermute(send, AXES, sibling_pairs)]
  transfers between devices with their start and end apart: 7 -> 7, of which waited for: 4 -> 4; matrix products, arithmetic and copies ran while one was open for 0% -> 0% of each run, Pallas kernels for 10% -> 11%
where the time goes in v7:
time: 75.5 us; the launch traced here: 75.1 us
  blocking collectives  32.6 us (43%)
  starting transfers between devices  21.7 us (29%)
  Pallas kernels  13.7 us (18%)
  waiting for transfers between devices  6.97 us (9%)
    all_to_all x1, blocking collectives, shards(): lax.all_to_all(sent, AXES, 0, 0, tiled=True, axis_index_groups=colours())  32.6 us
    ppermute x1, starting transfers between devices, shards(): other_half = lax.ppermute(own_keys, AXES, sibling_pairs)  5.07 us
    ppermute x1, starting transfers between devices, shards(): got = lax.ppermute(send, AXES, sibling_pairs)  3.76 us
    ppermute x1, starting transfers between devices, shards(): one = lax.ppermute(whole, AXES, x_pairs)  3.7 us
    pallas_call x1, Pallas kernels, shards(): call(middle_kernel, [VMEM] * 7, state, 'middle')  3.67 us
    ppermute x1, starting transfers between devices, shards(): four = lax.ppermute(own_keys, AXES, yz_pairs)  2.97 us
    ppermute x1, waiting for transfers between devices, shards(): three = lax.ppermute(whole, AXES, z_pairs)  2.87 us
    pallas_call x1, Pallas kernels, shards(): call(send_kernel, [VMEM] * 7, shape((ROWS, WIDE), bf16), 'sibling_rows')  2.46 us
  transfers between devices with their start and end apart: 7, of which 4 were waited for; matrix products, arithmetic and copies ran while one was open for 0% of the time, Pallas kernels for 11%

profile of v7, /device:TPU:1, one launch (start us, length us, event | category | flops | bytes accessed | tf_op | source)
XLA Modules:
  0.0 75.1 jit_solution(4004303151258899932)
XLA Ops:
  0.0 1.9 %prep.1 = (bf16[32,8,640]{2,1,0:T(8,128)(2,1)}, bf16[64,1664]{1,0:T(8,128)(2,1)}) custom-call(s32[128]{0:T(128)} %span_hbm.1, bf16[8,576]{1,0:T(8,128)(2,1)} %compressed_hbm.1, f32[1,512]{1,0:T(1,128)} %bitcast.6, bf16[64,1024]{1,0:T(8,128)(2,1)} %nope_hbm.1, bf16[64,512]{1,0:T(8,128)(2,1)} %rope_hbm.1), custom_call_target="tpu_custom_call" | custom-call | tf_op jit(solution)/shard_map/prep/pallas_call | solution.py:390
  1.9 0.0 copy-start.2
  1.9 32.6 %all_to_all.5 = bf16[32,8,640]{2,1,0:T(8,128)(2,1)S(1)} all-to-all(bf16[32,8,640]{2,1,0:T(8,128)(2,1)} %get-tuple-element.21), channel_id=1, replica_groups={{0,17,34,51,70,87,100,117,131,144,161,178,197,214,231,244,258,275,288,3..., dimensions={0} | all-to-all | bytes 655360 | tf_op jit(solution)/shard_map/all_to_all | solution.py:403
  34.4 5.1 %collective-permute-start = (bf16[256,640]{1,0:T(8,128)(2,1)S(1)}, bf16[256,640]{1,0:T(8,128)(2,1)S(1)}, u32[]{:S(2)}, u32[]{:S(2)}) collective-permute-start(bf16[256,640]{1,0:T(8,128)(2,1)S(1)} %bitcast.2), channel_id=1, source_target_pairs={{0,8},{8,0},{1,9},{9,1},{2,10},{10,2},{3,11},{11,3},{4,12},{12,4},... | collective-permute-start | bytes 983048 | tf_op jit(solution)/shard_map/ppermute | solution.py:406
  39.5 1.9 %collective-permute-start.1 = (bf16[64,1664]{1,0:T(8,128)(2,1)}, bf16[64,1664]{1,0:T(8,128)(2,1)S(1)}, u32[]{:S(2)}, u32[]{:S(2)}) collective-permute-start(bf16[64,1664]{1,0:T(8,128)(2,1)} %get-tuple-element.20.own_ref), channel_id=1, source_target_pairs={{0,8},{8,0},{1,9},{9,1},{2,10},{10,2},{3,11},{11,3},{4,12},{12,4},... | collective-permute-start | bytes 638984 | tf_op jit(solution)/shard_map/ppermute | solution.py:407
  41.5 1.6 %collective-permute-done.1.sibling_ref = bf16[64,1664]{1,0:T(8,128)(2,1)S(1)} collective-permute-done((bf16[64,1664]{1,0:T(8,128)(2,1)}, bf16[64,1664]{1,0:T(8,128)(2,1)S(1)}, u32[]{:S(2)}, u32[]{:S(2)}) %collective-permute-start.1) | collective-permute-done | bytes 213024 | tf_op jit(solution)/shard_map/ppermute | solution.py:407
  43.1 0.0 collective-permute-done.other_ref
  43.1 0.1 pair.1
  43.2 2.3 %collective-permute-start.5 = (bf16[512,640]{1,0:T(8,128)(2,1)S(1)}, bf16[512,640]{1,0:T(8,128)(2,1)S(1)}, u32[]{:S(2)}, u32[]{:S(2)}) collective-permute-start(bf16[512,640]{1,0:T(8,128)(2,1)S(1)} %pair.1), channel_id=1, source_target_pairs={{0,448},{8,72},{1,449},{9,73},{2,450},{10,74},{3,451},{11,75},{4,4... | collective-permute-start | bytes 1966088 | tf_op jit(solution)/shard_map/ppermute | solution.py:414
  45.5 3.7 %collective-permute-start.4 = (bf16[512,640]{1,0:T(8,128)(2,1)S(1)}, bf16[512,640]{1,0:T(8,128)(2,1)S(1)}, u32[]{:S(2)}, u32[]{:S(2)}) collective-permute-start(bf16[512,640]{1,0:T(8,128)(2,1)S(1)} %pair.1), channel_id=1, source_target_pairs={{0,3},{8,9},{1,0},{9,10},{2,1},{10,11},{3,2},{11,8},{4,7},{12,13},... | collective-permute-start | bytes 1966088 | tf_op jit(solution)/shard_map/ppermute | solution.py:413
  49.2 1.9 %collective-permute-start.2 = (bf16[512,640]{1,0:T(8,128)(2,1)S(1)}, bf16[512,640]{1,0:T(8,128)(2,1)S(1)}, u32[]{:S(2)}, u32[]{:S(2)}) collective-permute-start(bf16[512,640]{1,0:T(8,128)(2,1)S(1)} %pair.1), channel_id=1, source_target_pairs={{0,52},{8,12},{1,53},{9,13},{2,54},{10,14},{3,55},{11,15},{4,0},{1... | collective-permute-start | bytes 1966088 | tf_op jit(solution)/shard_map/ppermute | solution.py:415
  51.1 3.0 %collective-permute-start.3 = (bf16[256,640]{1,0:T(8,128)(2,1)S(1)}, bf16[256,640]{1,0:T(8,128)(2,1)S(1)}, u32[]{:S(2)}, u32[]{:S(2)}) collective-permute-start(bf16[256,640]{1,0:T(8,128)(2,1)S(1)} %bitcast.4), channel_id=1, source_target_pairs={{0,500},{8,76},{1,501},{9,77},{2,502},{10,78},{3,503},{11,79},{4,4... | collective-permute-start | bytes 983048 | tf_op jit(solution)/shard_map/ppermute | solution.py:409
  54.1 2.1 %first.1 = (bf16[1024,640]{1,0:T(8,128)(2,1)S(1)}, f32[1024,128]{1,0:T(8,128)S(1)}, f32[1024,512]{1,0:T(8,128)S(1)}, f32[1024,128]{1,0:T(8,128)S(1)}, f32[1024,128]{1,0:T(8,128)S(1)}) custom-call(bf16[64,1664]{1,0:T(8,128)(2,1)S(1)} %copy-done.2, bf16[64,1664]{1,0:T(8,128)(2,1)S(1)} %collective-permute-done.1.sibling_ref, bf16[8,128,512]{2,1,0:T(8,128)(2,1)S(1)} %copy-done, ...), custom_call_target="tpu_custom_call" | custom-call | tf_op jit(solution)/shard_map/first/pallas_call | solution.py:421
  56.2 0.0 collective-permute-done.5.two_ref
  56.2 1.8 %collective-permute-done.4.one_ref = bf16[512,640]{1,0:T(8,128)(2,1)S(1)} collective-permute-done((bf16[512,640]{1,0:T(8,128)(2,1)S(1)}, bf16[512,640]{1,0:T(8,128)(2,1)S(1)}, u32[]{:S(2)}, u32[]{:S(2)}) %collective-permute-start.4) | collective-permute-done | bytes 655392 | tf_op jit(solution)/shard_map/ppermute | solution.py:413
  58.0 3.7 %middle.1 = (f32[1024,512]{1,0:T(8,128)S(1)}, f32[1024,128]{1,0:T(8,128)S(1)}, f32[1024,128]{1,0:T(8,128)S(1)}) custom-call(bf16[1024,640]{1,0:T(8,128)(2,1)S(1)} %get-tuple-element.23.query_ref, f32[1024,128]{1,0:T(8,128)S(1)} %get-tuple-element.24.place_ref, bf16[512,640]{1,0:T(8,128)(2,1)S(1)} %collective-permute-done.4.one_ref, ...), custom_call_target="tpu_custom_call" | custom-call | tf_op jit(solution)/shard_map/middle/pallas_call | solution.py:427
  61.7 0.7 collective-permute-done.3.four_ref
  62.4 2.9 %collective-permute-done.2.keys_ref = bf16[512,640]{1,0:T(8,128)(2,1)S(1)} collective-permute-done((bf16[512,640]{1,0:T(8,128)(2,1)S(1)}, bf16[512,640]{1,0:T(8,128)(2,1)S(1)}, u32[]{:S(2)}, u32[]{:S(2)}) %collective-permute-start.2) | collective-permute-done | bytes 655392 | tf_op jit(solution)/shard_map/ppermute | solution.py:415
  65.3 2.5 %sibling_rows.1 = bf16[512,640]{1,0:T(8,128)(2,1)S(1)} custom-call(bf16[1024,640]{1,0:T(8,128)(2,1)S(1)} %get-tuple-element.23.query_ref, f32[1024,128]{1,0:T(8,128)S(1)} %get-tuple-element.24.place_ref, bf16[512,640]{1,0:T(8,128)(2,1)S(1)} %collective-permute-done.2.keys_ref, bf16[256,640]{1,0:T(8,128)(2,1)S(1)} %collective-permute-done.3.four_ref, ...), custom_call_target="tpu_custom_call" | custom-call | tf_op jit(solution)/shard_map/sibling_rows/pallas_call | solution.py:429
  67.7 0.0 copy-start.1
  67.7 3.8 %collective-permute-start.6 = (bf16[512,640]{1,0:T(8,128)(2,1)S(1)}, bf16[512,640]{1,0:T(8,128)(2,1)S(1)}, u32[]{:S(2)}, u32[]{:S(2)}) collective-permute-start(bf16[512,640]{1,0:T(8,128)(2,1)S(1)} %sibling_rows.1), channel_id=1, source_target_pairs={{0,8},{8,0},{1,9},{9,1},{2,10},{10,2},{3,11},{11,3},{4,12},{12,4},... | collective-permute-start | bytes 1966088 | tf_op jit(solution)/shard_map/ppermute | solution.py:430
  71.5 2.4 %own_rows.1 = (f32[512,512]{1,0:T(8,128)S(1)}, f32[512,128]{1,0:T(8,128)S(1)}, f32[512,128]{1,0:T(8,128)S(1)}) custom-call(bf16[1024,640]{1,0:T(8,128)(2,1)S(1)} %get-tuple-element.23.query_ref, f32[1024,128]{1,0:T(8,128)S(1)} %get-tuple-element.24.place_ref, bf16[512,640]{1,0:T(8,128)(2,1)S(1)} %collective-permute-done.2.keys_ref, ...), custom_call_target="tpu_custom_call" | custom-call | tf_op jit(solution)/shard_map/own_rows/pallas_call | solution.py:436
  73.9 0.0 collective-permute-done.6.got_ref
  74.0 1.1 %merge.1 = bf16[64,1024]{1,0:T(8,128)(2,1)} custom-call(f32[512,512]{1,0:T(8,128)S(1)} %get-tuple-element.32.acc_ref, f32[512,128]{1,0:T(8,128)S(1)} %get-tuple-element.33.top_ref, f32[512,128]{1,0:T(8,128)S(1)} %get-tuple-element.34.sum_ref, bf16[512,640]{1,0:T(8,128)(2,1)S(1)} %collective-permute-done.6.got_ref, bf16[8,512,128]{2,1,0:T(8,128)(2,1)S(1)} %copy-done.1), custom_call_target="tpu_custom_call" | custom-call | tf_op jit(solution)/shard_map/merge/pallas_call | solution.py:437
  (4 shorter events, 0.0 us)
Async XLA Ops:
  0.0 54.1 %copy-start = (bf16[8,128,512]{2,1,0:T(8,128)(2,1)S(1)}, bf16[8,128,512]{2,1,0:T(8,128)(2,1)}, u32[]{:S(2)}) copy-start(bf16[8,128,512]{2,1,0:T(8,128)(2,1)} %key_up_ref.1) | copy-start | bytes 3145732
  1.9 52.2 %copy-start.2 = (bf16[64,1664]{1,0:T(8,128)(2,1)S(1)}, bf16[64,1664]{1,0:T(8,128)(2,1)}, u32[]{:S(2)}) copy-start(bf16[64,1664]{1,0:T(8,128)(2,1)} %get-tuple-element.20.own_ref) | copy-start | bytes 638980
  34.4 8.7 %collective-permute-start = (bf16[256,640]{1,0:T(8,128)(2,1)S(1)}, bf16[256,640]{1,0:T(8,128)(2,1)S(1)}, u32[]{:S(2)}, u32[]{:S(2)}) collective-permute-start(bf16[256,640]{1,0:T(8,128)(2,1)S(1)} %bitcast.2), channel_id=1, source_target_pairs={{0,8},{8,0},{1,9},{9,1},{2,10},{10,2},{3,11},{11,3},{4,12},{12,4},... | collective-permute-start | bytes 983048 | tf_op jit(solution)/shard_map/ppermute | solution.py:406
  39.5 3.6 %collective-permute-start.1 = (bf16[64,1664]{1,0:T(8,128)(2,1)}, bf16[64,1664]{1,0:T(8,128)(2,1)S(1)}, u32[]{:S(2)}, u32[]{:S(2)}) collective-permute-start(bf16[64,1664]{1,0:T(8,128)(2,1)} %get-tuple-element.20.own_ref), channel_id=1, source_target_pairs={{0,8},{8,0},{1,9},{9,1},{2,10},{10,2},{3,11},{11,3},{4,12},{12,4},... | collective-permute-start | bytes 638984 | tf_op jit(solution)/shard_map/ppermute | solution.py:407
  43.2 13.1 %collective-permute-start.5 = (bf16[512,640]{1,0:T(8,128)(2,1)S(1)}, bf16[512,640]{1,0:T(8,128)(2,1)S(1)}, u32[]{:S(2)}, u32[]{:S(2)}) collective-permute-start(bf16[512,640]{1,0:T(8,128)(2,1)S(1)} %pair.1), channel_id=1, source_target_pairs={{0,448},{8,72},{1,449},{9,73},{2,450},{10,74},{3,451},{11,75},{4,4... | collective-permute-start | bytes 1966088 | tf_op jit(solution)/shard_map/ppermute | solution.py:414
  45.5 12.5 %collective-permute-start.4 = (bf16[512,640]{1,0:T(8,128)(2,1)S(1)}, bf16[512,640]{1,0:T(8,128)(2,1)S(1)}, u32[]{:S(2)}, u32[]{:S(2)}) collective-permute-start(bf16[512,640]{1,0:T(8,128)(2,1)S(1)} %pair.1), channel_id=1, source_target_pairs={{0,3},{8,9},{1,0},{9,10},{2,1},{10,11},{3,2},{11,8},{4,7},{12,13},... | collective-permute-start | bytes 1966088 | tf_op jit(solution)/shard_map/ppermute | solution.py:413
  49.2 16.1 %collective-permute-start.2 = (bf16[512,640]{1,0:T(8,128)(2,1)S(1)}, bf16[512,640]{1,0:T(8,128)(2,1)S(1)}, u32[]{:S(2)}, u32[]{:S(2)}) collective-permute-start(bf16[512,640]{1,0:T(8,128)(2,1)S(1)} %pair.1), channel_id=1, source_target_pairs={{0,52},{8,12},{1,53},{9,13},{2,54},{10,14},{3,55},{11,15},{4,0},{1... | collective-permute-start | bytes 1966088 | tf_op jit(solution)/shard_map/ppermute | solution.py:415
  51.1 11.2 %collective-permute-start.3 = (bf16[256,640]{1,0:T(8,128)(2,1)S(1)}, bf16[256,640]{1,0:T(8,128)(2,1)S(1)}, u32[]{:S(2)}, u32[]{:S(2)}) collective-permute-start(bf16[256,640]{1,0:T(8,128)(2,1)S(1)} %bitcast.4), channel_id=1, source_target_pairs={{0,500},{8,76},{1,501},{9,77},{2,502},{10,78},{3,503},{11,79},{4,4... | collective-permute-start | bytes 983048 | tf_op jit(solution)/shard_map/ppermute | solution.py:409
  67.7 6.2 %copy-start.1 = (bf16[8,512,128]{2,1,0:T(8,128)(2,1)S(1)}, bf16[8,512,128]{2,1,0:T(8,128)(2,1)}, u32[]{:S(2)}) copy-start(bf16[8,512,128]{2,1,0:T(8,128)(2,1)} %value_up_ref.1) | copy-start | bytes 3145732
  67.7 6.2 %collective-permute-start.6 = (bf16[512,640]{1,0:T(8,128)(2,1)S(1)}, bf16[512,640]{1,0:T(8,128)(2,1)S(1)}, u32[]{:S(2)}, u32[]{:S(2)}) collective-permute-start(bf16[512,640]{1,0:T(8,128)(2,1)S(1)} %sibling_rows.1), channel_id=1, source_target_pairs={{0,8},{8,0},{1,9},{9,1},{2,10},{10,2},{3,11},{11,3},{4,12},{12,4},... | collective-permute-start | bytes 1966088 | tf_op jit(solution)/shard_map/ppermute | solution.py:430

commit v8 on v7

--- a/solution.py
+++ b/solution.py
@@ -138,15 +138,11 @@
         copy.wait()
 
 
-def key_positions(keys):
+def position_rows():
     lane = lanes_of((16, WIDE))
-    pick = jnp.where(
+    return jnp.where(
         lane == LATENT + ROPE, float(HALF), jnp.where(lane == LATENT + ROPE + 1, 1.0, 0.0)
     ).astype(jnp.bfloat16)
-    found = lax.dot_general(
-        pick, keys, (((1,), (1,)), ((), ())), preferred_element_type=jnp.float32
-    )
-    return found[:8]
 
 
 def query_positions(places):
@@ -157,15 +153,21 @@
 
 def attend(query_ref, place_ref, key_refs, carry, finish, rows=(0, 2 * ROWS)):
     keys = [ref[...] for ref in key_refs]
-    places = [key_positions(block) for block in keys]
+    places = [None] * len(keys)
     for start in range(*rows, CHUNK):
         queries = query_ref[start : start + CHUNK, :]
+        if start == rows[0]:
+            queries = jnp.concatenate([queries, position_rows()], axis=0)
         here = place_ref[start : start + CHUNK, :]
         scores = []
-        for block, place in zip(keys, places):
+        for k, block in enumerate(keys):
             raw = lax.dot_general(
                 queries, block, (((1,), (1,)), ((), ())), preferred_element_type=jnp.float32
             )
+            if start == rows[0]:
+                places[k] = raw[CHUNK : CHUNK + 8]
+                raw = raw[:CHUNK]
+            place = places[k]
             pieces = []
             for at in range(0, block.shape[0], 128):
                 there = jnp.tile(place[:, at : at + 128], (CHUNK // 8, 1))
@@ -209,12 +211,6 @@
         sum_ref[start : start + CHUNK, :] = total
 
     return finish
-
-
-def pair_kernel(own_ref, other_ref, whole_ref):
-    rows = own_ref.shape[0]
-    whole_ref[:rows, :] = own_ref[...]
-    whole_ref[rows:, :] = other_ref[...]
 
 
 def first_kernel(
@@ -272,7 +268,7 @@
 
 
 def send_kernel(
-    query_ref, place_ref, keys_ref, four_ref, old_acc_ref, old_top_ref, old_sum_ref, out_ref
+    query_ref, place_ref, keys_ref, old_acc_ref, old_top_ref, old_sum_ref, out_ref
 ):
     def finish(start, product, top, total):
         at = start % ROWS
@@ -291,14 +287,13 @@
         out_ref[at : at + CHUNK, LATENT:] = pieces.astype(jnp.bfloat16)
 
     old = (old_acc_ref, old_top_ref, old_sum_ref)
-    attend(query_ref, place_ref, [keys_ref, four_ref], old, finish, (ROWS, 2 * ROWS))
+    attend(query_ref, place_ref, [keys_ref], old, finish, (ROWS, 2 * ROWS))
 
 
 def own_kernel(
     query_ref,
     place_ref,
     keys_ref,
-    four_ref,
     old_acc_ref,
     old_top_ref,
     old_sum_ref,
@@ -314,7 +309,7 @@
         )
 
     old = (old_acc_ref, old_top_ref, old_sum_ref)
-    attend(query_ref, place_ref, [keys_ref, four_ref], old, finish, (0, ROWS))
+    attend(query_ref, place_ref, [keys_ref], old, finish, (0, ROWS))
 
 
 def merge_kernel(acc_ref, top_ref, sum_ref, got_ref, value_up_ref, out_ref):
@@ -370,9 +365,9 @@
             for y in range(NY)
             for z in range(NZH * NZL)
             for x in range(NX)
-            if (2 * x + y + 3 * z) % 8 == colour
+            if (x + y + 2 * z) % 4 == colour
         ]
-        for colour in range(8)
+        for colour in range(4)
         for c in range(NC)
     ]
 
@@ -382,15 +377,14 @@
     bf16 = jnp.bfloat16
     shape = jax.ShapeDtypeStruct
     x_pairs = pairs(lambda y, z, x, c: (y, z, x - 1 + 2 * c, c))
-    y_pairs = pairs(lambda y, z, x, c: (y - 1 + 2 * c, z, x, c))
+    y_pairs = pairs(lambda y, z, x, c: (y + 1 - 2 * c, z, x, 1 - c))
     z_pairs = pairs(lambda y, z, x, c: (y, z - 1 + 2 * c, x, c))
-    yz_pairs = pairs(lambda y, z, x, c: (y - 1 + 2 * c, z - 1 + 2 * c, x, c))
     sibling_pairs = pairs(lambda y, z, x, c: (y, z, x, 1 - c))
 
     sent, joined = call(
         prep_kernel,
         [HBM] * 5,
-        (shape((32, 8, WIDE), bf16), shape((TOK, JOINED), bf16)),
+        (shape((64, 8, WIDE), bf16), shape((TOK, JOINED), bf16)),
         "prep",
         60,
         [
@@ -402,17 +396,11 @@
     )(span_order, compressed, latent_gain[None], query_nope, query_rope)
     own_keys = lax.all_to_all(
         sent, AXES, 0, 0, tiled=True, axis_index_groups=colours()
-    ).reshape(256, WIDE)
-    other_half = lax.ppermute(own_keys, AXES, sibling_pairs)
+    ).reshape(512, WIDE)
+    one = lax.ppermute(own_keys, AXES, x_pairs)
+    two = lax.ppermute(own_keys, AXES, y_pairs)
+    three = lax.ppermute(own_keys, AXES, z_pairs)
     sibling = lax.ppermute(joined, AXES, sibling_pairs)
-    other_half, sibling = lax.optimization_barrier((other_half, sibling))
-    four = lax.ppermute(own_keys, AXES, yz_pairs)
-    whole = call(pair_kernel, [VMEM] * 2, shape((512, WIDE), bf16), "pair", 8)(
-        own_keys, other_half
-    )
-    one = lax.ppermute(whole, AXES, x_pairs)
-    two = lax.ppermute(whole, AXES, y_pairs)
-    three = lax.ppermute(whole, AXES, z_pairs)
     state = (
         shape((2 * ROWS, LATENT), f32),
         shape((2 * ROWS, 128), f32),
@@ -425,15 +413,15 @@
         "first",
     )(joined, sibling, key_up, own_keys)
     carry = call(middle_kernel, [VMEM] * 7, state, "middle")(queries, places, one, two, *carry)
-    ending = (queries, places, three, four, *carry)
-    send = call(send_kernel, [VMEM] * 7, shape((ROWS, WIDE), bf16), "sibling_rows")(*ending)
+    ending = (queries, places, three, *carry)
+    send = call(send_kernel, [VMEM] * 6, shape((ROWS, WIDE), bf16), "sibling_rows")(*ending)
     got = lax.ppermute(send, AXES, sibling_pairs)
     own_state = (
         shape((ROWS, LATENT), f32),
         shape((ROWS, 128), f32),
         shape((ROWS, 128), f32),
     )
-    own = call(own_kernel, [VMEM] * 7, own_state, "own_rows")(*ending)
+    own = call(own_kernel, [VMEM] * 6, own_state, "own_rows")(*ending)
     return call(
         merge_kernel, [VMEM] * 5, shape((TOK, HEADS_HERE * VDIM), bf16), "merge", 16
     )(*own, got, value_up)

time: 75.5 us -> 71.2 us (0.943)
  blocking collectives: 32.6 us -> 40.8 us
  starting transfers between devices: 21.7 us -> 15.7 us
  waiting for transfers between devices: 6.97 us -> 1.75 us
  Pallas kernels: 13.7 us -> 11.5 us
  local copies, waits for them, and re-layouts: 0.01 us -> 0.94 us
    all_to_all x1, blocking collectives: 32.6 us -> 40.8 us  [shards(): lax.all_to_all(sent, AXES, 0, 0, tiled=True, axis_index_groups=colours())]
    ppermute x5 -> x3, starting transfers between devices: 16 us -> 10.6 us  [the longest x1 4.98 us: shards(): two = lax.ppermute(own_keys, AXES, y_pairs)]
    ppermute x5 -> x3, waiting for transfers between devices: 5.33 us -> 0.01 us  [the longest x1 0.01 us: shards(): two = lax.ppermute(own_keys, AXES, y_pairs)]
    pallas_call x4 -> x3, Pallas kernels: 6.82 us -> 4.45 us  [the longest x1 2 us: shards(): call(prep_kernel, [HBM] * 5, (shape((64, 8, WIDE), bf16), shape((TOK, JOI...]
    ppermute x1, starting transfers between devices: 3.76 us -> 2.42 us  [shards(): got = lax.ppermute(send, AXES, sibling_pairs)]
    unnamed x6, local copies, waits for them, and re-layouts: 0.01 us -> 0.94 us
  transfers between devices with their start and end apart: 7 -> 5, of which waited for: 4 -> 2; matrix products, arithmetic and copies ran while one was open for 0% -> 0% of each run, Pallas kernels for 11% -> 10%
where the time goes in v8:
time: 71.2 us; the launch traced here: 70.8 us
  blocking collectives  40.8 us (57%)
  starting transfers between devices  15.7 us (22%)
  Pallas kernels  11.5 us (16%)
  waiting for transfers between devices  1.75 us (2%)
  local copies, waits for them, and re-layouts  0.94 us (1%)
    all_to_all x1, blocking collectives, shards(): lax.all_to_all(sent, AXES, 0, 0, tiled=True, axis_index_groups=colours())  40.8 us
    ppermute x1, starting transfers between devices, shards(): two = lax.ppermute(own_keys, AXES, y_pairs)  4.98 us
    ppermute x1, starting transfers between devices, shards(): one = lax.ppermute(own_keys, AXES, x_pairs)  3.7 us
    pallas_call x1, Pallas kernels, shards(): call(middle_kernel, [VMEM] * 7, state, 'middle')  3.61 us
    ppermute x1, starting transfers between devices, shards(): sibling = lax.ppermute(joined, AXES, sibling_pairs)  2.63 us
    ppermute x1, starting transfers between devices, shards(): got = lax.ppermute(send, AXES, sibling_pairs)  2.42 us
    pallas_call x1, Pallas kernels, shards(): call(first_kernel, [VMEM] * 4, (shape((2 * ROWS, WIDE), bf16), shape((2 *...  2.37 us
    pallas_call x1, Pallas kernels, shards(): call(prep_kernel, [HBM] * 5, (shape((64, 8, WIDE), bf16), shape((TOK, JOI...  2 us
  transfers between devices with their start and end apart: 5, of which 2 were waited for; matrix products, arithmetic and copies ran while one was open for 0% of the time, Pallas kernels for 10%

profile of v8, /device:TPU:1, one launch (start us, length us, event | category | flops | bytes accessed | tf_op | source)
XLA Modules:
  0.0 70.8 jit_solution(1559051386469760116)
XLA Ops:
  0.0 0.0 copy-start
  0.0 2.0 %prep.1 = (bf16[64,8,640]{2,1,0:T(8,128)(2,1)}, bf16[64,1664]{1,0:T(8,128)(2,1)}) custom-call(s32[128]{0:T(128)} %span_hbm.1, bf16[8,576]{1,0:T(8,128)(2,1)} %compressed_hbm.1, f32[1,512]{1,0:T(1,128)} %bitcast.6, bf16[64,1024]{1,0:T(8,128)(2,1)} %nope_hbm.1, bf16[64,512]{1,0:T(8,128)(2,1)} %rope_hbm.1), custom_call_target="tpu_custom_call" | custom-call | tf_op jit(solution)/shard_map/prep/pallas_call | solution.py:384
  2.0 40.8 %all_to_all.5 = bf16[64,8,640]{2,1,0:T(8,128)(2,1)S(1)} all-to-all(bf16[64,8,640]{2,1,0:T(8,128)(2,1)} %get-tuple-element.19), channel_id=1, replica_groups={{0,6,16,22,32,38,48,54,67,69,83,85,99,101,115,117,130,132,146,148,162,1..., dimensions={0} | all-to-all | bytes 1310720 | tf_op jit(solution)/shard_map/all_to_all | solution.py:397
  42.9 5.0 %collective-permute-start.3 = (bf16[512,640]{1,0:T(8,128)(2,1)S(1)}, bf16[512,640]{1,0:T(8,128)(2,1)S(1)}, u32[]{:S(2)}, u32[]{:S(2)}) collective-permute-start(bf16[512,640]{1,0:T(8,128)(2,1)S(1)} %bitcast.2), channel_id=1, source_target_pairs={{0,72},{8,448},{1,73},{9,449},{2,74},{10,450},{3,75},{11,451},{4,7... | collective-permute-start | bytes 1966088 | tf_op jit(solution)/shard_map/ppermute | solution.py:401
  47.8 3.7 %collective-permute-start.2 = (bf16[512,640]{1,0:T(8,128)(2,1)S(1)}, bf16[512,640]{1,0:T(8,128)(2,1)S(1)}, u32[]{:S(2)}, u32[]{:S(2)}) collective-permute-start(bf16[512,640]{1,0:T(8,128)(2,1)S(1)} %bitcast.3), channel_id=1, source_target_pairs={{0,3},{8,9},{1,0},{9,10},{2,1},{10,11},{3,2},{11,8},{4,7},{12,13},... | collective-permute-start | bytes 1966088 | tf_op jit(solution)/shard_map/ppermute | solution.py:400
  51.6 1.9 %collective-permute-start.1 = (bf16[512,640]{1,0:T(8,128)(2,1)S(1)}, bf16[512,640]{1,0:T(8,128)(2,1)S(1)}, u32[]{:S(2)}, u32[]{:S(2)}) collective-permute-start(bf16[512,640]{1,0:T(8,128)(2,1)S(1)} %bitcast.4), channel_id=1, source_target_pairs={{0,52},{8,12},{1,53},{9,13},{2,54},{10,14},{3,55},{11,15},{4,0},{1... | collective-permute-start | bytes 1966088 | tf_op jit(solution)/shard_map/ppermute | solution.py:402
  53.5 2.6 %collective-permute-start = (bf16[64,1664]{1,0:T(8,128)(2,1)}, bf16[64,1664]{1,0:T(8,128)(2,1)S(1)}, u32[]{:S(2)}, u32[]{:S(2)}) collective-permute-start(bf16[64,1664]{1,0:T(8,128)(2,1)} %get-tuple-element.18.own_ref), channel_id=1, source_target_pairs={{0,8},{8,0},{1,9},{9,1},{2,10},{10,2},{3,11},{11,3},{4,12},{12,4},... | collective-permute-start | bytes 638984 | tf_op jit(solution)/shard_map/ppermute | solution.py:403
  56.1 1.3 %collective-permute-done.sibling_ref = bf16[64,1664]{1,0:T(8,128)(2,1)S(1)} collective-permute-done((bf16[64,1664]{1,0:T(8,128)(2,1)}, bf16[64,1664]{1,0:T(8,128)(2,1)S(1)}, u32[]{:S(2)}, u32[]{:S(2)}) %collective-permute-start) | collective-permute-done | bytes 213024 | tf_op jit(solution)/shard_map/ppermute | solution.py:403
  57.4 0.0 copy-done
  57.4 0.0 copy-start.2
  57.4 0.9 %copy-done.2 = bf16[64,1664]{1,0:T(8,128)(2,1)S(1)} copy-done((bf16[64,1664]{1,0:T(8,128)(2,1)S(1)}, bf16[64,1664]{1,0:T(8,128)(2,1)}, u32[]{:S(2)}) %copy-start.2) | copy-done | bytes 213016
  58.3 2.4 %first.1 = (bf16[1024,640]{1,0:T(8,128)(2,1)S(1)}, f32[1024,128]{1,0:T(8,128)S(1)}, f32[1024,512]{1,0:T(8,128)S(1)}, f32[1024,128]{1,0:T(8,128)S(1)}, f32[1024,128]{1,0:T(8,128)S(1)}) custom-call(bf16[64,1664]{1,0:T(8,128)(2,1)S(1)} %copy-done.2, bf16[64,1664]{1,0:T(8,128)(2,1)S(1)} %collective-permute-done.sibling_ref, bf16[8,128,512]{2,1,0:T(8,128)(2,1)S(1)} %copy-done, ...), custom_call_target="tpu_custom_call" | custom-call | tf_op jit(solution)/shard_map/first/pallas_call | solution.py:409
  60.7 0.0 collective-permute-done.3.two_ref
  60.7 0.0 collective-permute-done.2.one_ref
  60.7 3.6 %middle.1 = (f32[1024,512]{1,0:T(8,128)S(1)}, f32[1024,128]{1,0:T(8,128)S(1)}, f32[1024,128]{1,0:T(8,128)S(1)}) custom-call(bf16[1024,640]{1,0:T(8,128)(2,1)S(1)} %get-tuple-element.20.query_ref, f32[1024,128]{1,0:T(8,128)S(1)} %get-tuple-element.21.place_ref, bf16[512,640]{1,0:T(8,128)(2,1)S(1)} %collective-permute-done.2.one_ref, ...), custom_call_target="tpu_custom_call" | custom-call | tf_op jit(solution)/shard_map/middle/pallas_call | solution.py:415
  64.3 0.0 collective-permute-done.1.keys_ref
  64.4 1.2 %sibling_rows.1 = bf16[512,640]{1,0:T(8,128)(2,1)S(1)} custom-call(bf16[1024,640]{1,0:T(8,128)(2,1)S(1)} %get-tuple-element.20.query_ref, f32[1024,128]{1,0:T(8,128)S(1)} %get-tuple-element.21.place_ref, bf16[512,640]{1,0:T(8,128)(2,1)S(1)} %collective-permute-done.1.keys_ref, f32[1024,512]{1,0:T(8,128)S(1)} %get-tuple-element.25.old_acc_ref, ...), custom_call_target="tpu_custom_call" | custom-call | tf_op jit(solution)/shard_map/sibling_rows/pallas_call | solution.py:417
  65.6 0.0 copy-start.1
  65.6 2.4 %collective-permute-start.4 = (bf16[512,640]{1,0:T(8,128)(2,1)S(1)}, bf16[512,640]{1,0:T(8,128)(2,1)S(1)}, u32[]{:S(2)}, u32[]{:S(2)}) collective-permute-start(bf16[512,640]{1,0:T(8,128)(2,1)S(1)} %sibling_rows.1), channel_id=1, source_target_pairs={{0,8},{8,0},{1,9},{9,1},{2,10},{10,2},{3,11},{11,3},{4,12},{12,4},... | collective-permute-start | bytes 1966088 | tf_op jit(solution)/shard_map/ppermute | solution.py:418
  68.0 1.2 %own_rows.1 = (f32[512,512]{1,0:T(8,128)S(1)}, f32[512,128]{1,0:T(8,128)S(1)}, f32[512,128]{1,0:T(8,128)S(1)}) custom-call(bf16[1024,640]{1,0:T(8,128)(2,1)S(1)} %get-tuple-element.20.query_ref, f32[1024,128]{1,0:T(8,128)S(1)} %get-tuple-element.21.place_ref, bf16[512,640]{1,0:T(8,128)(2,1)S(1)} %collective-permute-done.1.keys_ref, ...), custom_call_target="tpu_custom_call" | custom-call | tf_op jit(solution)/shard_map/own_rows/pallas_call | solution.py:424
  69.3 0.5 collective-permute-done.4.got_ref
  69.7 0.0 copy-done.1
  69.7 1.1 %merge.1 = bf16[64,1024]{1,0:T(8,128)(2,1)} custom-call(f32[512,512]{1,0:T(8,128)S(1)} %get-tuple-element.28.acc_ref, f32[512,128]{1,0:T(8,128)S(1)} %get-tuple-element.29.top_ref, f32[512,128]{1,0:T(8,128)S(1)} %get-tuple-element.30.sum_ref, bf16[512,640]{1,0:T(8,128)(2,1)S(1)} %collective-permute-done.4.got_ref, bf16[8,512,128]{2,1,0:T(8,128)(2,1)S(1)} %copy-done.1), custom_call_target="tpu_custom_call" | custom-call | tf_op jit(solution)/shard_map/merge/pallas_call | solution.py:425
Async XLA Ops:
  0.0 57.4 %copy-start = (bf16[8,128,512]{2,1,0:T(8,128)(2,1)S(1)}, bf16[8,128,512]{2,1,0:T(8,128)(2,1)}, u32[]{:S(2)}) copy-start(bf16[8,128,512]{2,1,0:T(8,128)(2,1)} %key_up_ref.1) | copy-start | bytes 3145732
  42.9 17.9 %collective-permute-start.3 = (bf16[512,640]{1,0:T(8,128)(2,1)S(1)}, bf16[512,640]{1,0:T(8,128)(2,1)S(1)}, u32[]{:S(2)}, u32[]{:S(2)}) collective-permute-start(bf16[512,640]{1,0:T(8,128)(2,1)S(1)} %bitcast.2), channel_id=1, source_target_pairs={{0,72},{8,448},{1,73},{9,449},{2,74},{10,450},{3,75},{11,451},{4,7... | collective-permute-start | bytes 1966088 | tf_op jit(solution)/shard_map/ppermute | solution.py:401
  47.8 12.9 %collective-permute-start.2 = (bf16[512,640]{1,0:T(8,128)(2,1)S(1)}, bf16[512,640]{1,0:T(8,128)(2,1)S(1)}, u32[]{:S(2)}, u32[]{:S(2)}) collective-permute-start(bf16[512,640]{1,0:T(8,128)(2,1)S(1)} %bitcast.3), channel_id=1, source_target_pairs={{0,3},{8,9},{1,0},{9,10},{2,1},{10,11},{3,2},{11,8},{4,7},{12,13},... | collective-permute-start | bytes 1966088 | tf_op jit(solution)/shard_map/ppermute | solution.py:400
  51.6 12.8 %collective-permute-start.1 = (bf16[512,640]{1,0:T(8,128)(2,1)S(1)}, bf16[512,640]{1,0:T(8,128)(2,1)S(1)}, u32[]{:S(2)}, u32[]{:S(2)}) collective-permute-start(bf16[512,640]{1,0:T(8,128)(2,1)S(1)} %bitcast.4), channel_id=1, source_target_pairs={{0,52},{8,12},{1,53},{9,13},{2,54},{10,14},{3,55},{11,15},{4,0},{1... | collective-permute-start | bytes 1966088 | tf_op jit(solution)/shard_map/ppermute | solution.py:402
  53.5 3.9 %collective-permute-start = (bf16[64,1664]{1,0:T(8,128)(2,1)}, bf16[64,1664]{1,0:T(8,128)(2,1)S(1)}, u32[]{:S(2)}, u32[]{:S(2)}) collective-permute-start(bf16[64,1664]{1,0:T(8,128)(2,1)} %get-tuple-element.18.own_ref), channel_id=1, source_target_pairs={{0,8},{8,0},{1,9},{9,1},{2,10},{10,2},{3,11},{11,3},{4,12},{12,4},... | collective-permute-start | bytes 638984 | tf_op jit(solution)/shard_map/ppermute | solution.py:403
  57.4 0.9 %copy-start.2 = (bf16[64,1664]{1,0:T(8,128)(2,1)S(1)}, bf16[64,1664]{1,0:T(8,128)(2,1)}, u32[]{:S(2)}) copy-start(bf16[64,1664]{1,0:T(8,128)(2,1)} %get-tuple-element.18.own_ref) | copy-start | bytes 638980
  65.6 4.1 %copy-start.1 = (bf16[8,512,128]{2,1,0:T(8,128)(2,1)S(1)}, bf16[8,512,128]{2,1,0:T(8,128)(2,1)}, u32[]{:S(2)}) copy-start(bf16[8,512,128]{2,1,0:T(8,128)(2,1)} %value_up_ref.1) | copy-start | bytes 3145732
  65.6 4.1 %collective-permute-start.4 = (bf16[512,640]{1,0:T(8,128)(2,1)S(1)}, bf16[512,640]{1,0:T(8,128)(2,1)S(1)}, u32[]{:S(2)}, u32[]{:S(2)}) collective-permute-start(bf16[512,640]{1,0:T(8,128)(2,1)S(1)} %sibling_rows.1), channel_id=1, source_target_pairs={{0,8},{8,0},{1,9},{9,1},{2,10},{10,2},{3,11},{11,3},{4,12},{12,4},... | collective-permute-start | bytes 1966088 | tf_op jit(solution)/shard_map/ppermute | solution.py:418

commit v9 on v8

--- a/solution.py
+++ b/solution.py
@@ -151,7 +151,7 @@
     return jnp.dot(places, pick, preferred_element_type=jnp.float32)
 
 
-def attend(query_ref, place_ref, key_refs, carry, finish, rows=(0, 2 * ROWS)):
+def attend(query_ref, place_ref, key_refs, carry, finish, rows=(0, ROWS)):
     keys = [ref[...] for ref in key_refs]
     places = [None] * len(keys)
     for start in range(*rows, CHUNK):
@@ -213,47 +213,40 @@
     return finish
 
 
-def first_kernel(
-    own_ref,
-    sibling_ref,
-    key_up_ref,
-    keys_ref,
-    query_ref,
-    place_ref,
-    acc_ref,
-    top_ref,
-    sum_ref,
-):
-    both = jnp.concatenate([own_ref[...], sibling_ref[...]], axis=0)
-    nope = both[:, :NOPES]
-    rope = both[:, NOPES : NOPES + ROPES]
-    positions = query_positions(both[:, NOPES + ROPES :])
+def project(joined_ref, key_up_ref, query_ref, place_ref):
+    joined = joined_ref[...]
+    positions = query_positions(joined[:, NOPES + ROPES :])
     turning = rotation(positions)
-    lane = lanes_of((2 * TOK, 128))
+    lane = lanes_of((TOK, 128))
     for head in range(HEADS_HERE):
-        raised = jnp.dot(
-            nope[:, head * NOPE : (head + 1) * NOPE],
+        at = slice(head * TOK, (head + 1) * TOK)
+        query_ref[at, :LATENT] = jnp.dot(
+            joined[:, head * NOPE : (head + 1) * NOPE],
             key_up_ref[head],
             preferred_element_type=jnp.float32,
         ).astype(jnp.bfloat16)
         if head % 2 == 0:
-            turned = apply_rotation(
-                rope[:, head * ROPE : head * ROPE + 128].astype(jnp.float32), *turning
-            )
+            first = NOPES + head * ROPE
+            turned = apply_rotation(joined[:, first : first + 128].astype(jnp.float32), *turning)
         else:
             turned = pltpu.roll(turned, ROPE, 1)
-        tail = jnp.where(lane < ROPE, turned, 0.0).astype(jnp.bfloat16)
-        for other in range(2):
-            at = other * ROWS + head * TOK
-            query_ref[at : at + TOK, :LATENT] = raised[other * TOK : (other + 1) * TOK]
-            query_ref[at : at + TOK, LATENT:] = tail[other * TOK : (other + 1) * TOK]
-            place_ref[at : at + TOK, :] = positions[other * TOK : (other + 1) * TOK]
+        query_ref[at, LATENT:] = jnp.where(lane < ROPE, turned, 0.0).astype(jnp.bfloat16)
+        place_ref[at, :] = positions
+
+
+def first_kernel(
+    own_ref, key_up_ref, keys_ref, query_ref, place_ref, acc_ref, top_ref, sum_ref
+):
+    project(own_ref, key_up_ref, query_ref, place_ref)
     attend(query_ref, place_ref, [keys_ref], None, keep(acc_ref, top_ref, sum_ref))
 
 
 def middle_kernel(
     query_ref,
     place_ref,
+    sibling_ref,
+    key_up_ref,
+    keys_ref,
     one_ref,
     two_ref,
     old_acc_ref,
@@ -262,9 +255,22 @@
     acc_ref,
     top_ref,
     sum_ref,
+    sibling_query_ref,
+    sibling_place_ref,
+    sibling_acc_ref,
+    sibling_top_ref,
+    sibling_sum_ref,
 ):
+    project(sibling_ref, key_up_ref, sibling_query_ref, sibling_place_ref)
     old = (old_acc_ref, old_top_ref, old_sum_ref)
     attend(query_ref, place_ref, [one_ref, two_ref], old, keep(acc_ref, top_ref, sum_ref))
+    attend(
+        sibling_query_ref,
+        sibling_place_ref,
+        [keys_ref, one_ref, two_ref],
+        None,
+        keep(sibling_acc_ref, sibling_top_ref, sibling_sum_ref),
+    )
 
 
 def send_kernel(
@@ -287,7 +293,7 @@
         out_ref[at : at + CHUNK, LATENT:] = pieces.astype(jnp.bfloat16)
 
     old = (old_acc_ref, old_top_ref, old_sum_ref)
-    attend(query_ref, place_ref, [keys_ref], old, finish, (ROWS, 2 * ROWS))
+    attend(query_ref, place_ref, [keys_ref], old, finish)
 
 
 def own_kernel(
@@ -309,7 +315,7 @@
         )
 
     old = (old_acc_ref, old_top_ref, old_sum_ref)
-    attend(query_ref, place_ref, [keys_ref], old, finish, (0, ROWS))
+    attend(query_ref, place_ref, [keys_ref], old, finish)
 
 
 def merge_kernel(acc_ref, top_ref, sum_ref, got_ref, value_up_ref, out_ref):
@@ -401,27 +407,20 @@
     two = lax.ppermute(own_keys, AXES, y_pairs)
     three = lax.ppermute(own_keys, AXES, z_pairs)
     sibling = lax.ppermute(joined, AXES, sibling_pairs)
-    state = (
-        shape((2 * ROWS, LATENT), f32),
-        shape((2 * ROWS, 128), f32),
-        shape((2 * ROWS, 128), f32),
-    )
-    queries, places, *carry = call(
-        first_kernel,
-        [VMEM] * 4,
-        (shape((2 * ROWS, WIDE), bf16), shape((2 * ROWS, 128), f32), *state),
-        "first",
-    )(joined, sibling, key_up, own_keys)
-    carry = call(middle_kernel, [VMEM] * 7, state, "middle")(queries, places, one, two, *carry)
-    ending = (queries, places, three, *carry)
-    send = call(send_kernel, [VMEM] * 6, shape((ROWS, WIDE), bf16), "sibling_rows")(*ending)
+    state = (shape((ROWS, LATENT), f32), shape((ROWS, 128), f32), shape((ROWS, 128), f32))
+    rows = (shape((ROWS, WIDE), bf16), shape((ROWS, 128), f32))
+    queries, places, *carry = call(first_kernel, [VMEM] * 3, (*rows, *state), "first")(
+        joined, key_up, own_keys
+    )
+    *carry, acc, top, total = call(middle_kernel, [VMEM] * 10, (*state, *rows, *state), "middle")(
+        queries, places, sibling, key_up, own_keys, one, two, *carry
+    )
+    *carry, sibling_queries, sibling_places = carry
+    send = call(send_kernel, [VMEM] * 6, shape((ROWS, WIDE), bf16), "sibling_rows")(
+        sibling_queries, sibling_places, three, acc, top, total
+    )
     got = lax.ppermute(send, AXES, sibling_pairs)
-    own_state = (
-        shape((ROWS, LATENT), f32),
-        shape((ROWS, 128), f32),
-        shape((ROWS, 128), f32),
-    )
-    own = call(own_kernel, [VMEM] * 6, own_state, "own_rows")(*ending)
+    own = call(own_kernel, [VMEM] * 6, state, "own_rows")(queries, places, three, *carry)
     return call(
         merge_kernel, [VMEM] * 5, shape((TOK, HEADS_HERE * VDIM), bf16), "merge", 16
     )(*own, got, value_up)

time: 71.2 us -> 73 us (1.025)
  starting transfers between devices: 15.7 us -> 17.3 us
  local copies, waits for them, and re-layouts: 0.94 us -> 0.01 us
  waiting for transfers between devices: 1.75 us -> 2.49 us
    ppermute x1, waiting for transfers between devices: 0.01 us -> 1.99 us  [shards(): two = lax.ppermute(own_keys, AXES, y_pairs)]
    ppermute x1, starting transfers between devices: 4.98 us -> 6.73 us  [shards(): two = lax.ppermute(own_keys, AXES, y_pairs)]
    ppermute x1, waiting for transfers between devices: 1.28 us -> 0.04 us  [shards(): sibling = lax.ppermute(joined, AXES, sibling_pairs)]
    ppermute x1, starting transfers between devices: 3.7 us -> 2.61 us  [shards(): one = lax.ppermute(own_keys, AXES, x_pairs)]
    ppermute x1, starting transfers between devices: 1.92 us -> 2.88 us  [shards(): three = lax.ppermute(own_keys, AXES, z_pairs)]
    unnamed x6, local copies, waits for them, and re-layouts: 0.94 us -> 0.01 us
    ppermute x1, starting transfers between devices: 2.42 us -> 3.17 us  [shards(): got = lax.ppermute(send, AXES, sibling_pairs)]
where the time goes in v9:
time: 73 us; the launch traced here: 72.7 us
  blocking collectives  41 us (56%)
  starting transfers between devices  17.3 us (24%)
  Pallas kernels  11.8 us (16%)
  waiting for transfers between devices  2.49 us (3%)
    all_to_all x1, blocking collectives, shards(): lax.all_to_all(sent, AXES, 0, 0, tiled=True, axis_index_groups=colours())  41 us
    ppermute x1, starting transfers between devices, shards(): two = lax.ppermute(own_keys, AXES, y_pairs)  6.73 us
    pallas_call x1, Pallas kernels, shards(): call(middle_kernel, [VMEM] * 10, (*state, *rows, *state), 'middle')  4.84 us
    ppermute x1, starting transfers between devices, shards(): got = lax.ppermute(send, AXES, sibling_pairs)  3.17 us
    ppermute x1, starting transfers between devices, shards(): three = lax.ppermute(own_keys, AXES, z_pairs)  2.88 us
    ppermute x1, starting transfers between devices, shards(): one = lax.ppermute(own_keys, AXES, x_pairs)  2.61 us
    pallas_call x1, Pallas kernels, shards(): call(prep_kernel, [HBM] * 5, (shape((64, 8, WIDE), bf16), shape((TOK, JOI...  2 us
    ppermute x1, waiting for transfers between devices, shards(): two = lax.ppermute(own_keys, AXES, y_pairs)  1.99 us
  transfers between devices with their start and end apart: 5, of which 2 were waited for; matrix products, arithmetic and copies ran while one was open for 0% of the time, Pallas kernels for 10%

profile of v9, /device:TPU:1, one launch (start us, length us, event | category | flops | bytes accessed | tf_op | source)
XLA Modules:
  0.0 72.7 jit_solution(12498758533941598336)
XLA Ops:
  0.0 0.0 copy-start
  0.0 2.0 %prep.1 = (bf16[64,8,640]{2,1,0:T(8,128)(2,1)}, bf16[64,1664]{1,0:T(8,128)(2,1)}) custom-call(s32[128]{0:T(128)} %span_hbm.1, bf16[8,576]{1,0:T(8,128)(2,1)} %compressed_hbm.1, f32[1,512]{1,0:T(1,128)} %bitcast.7, bf16[64,1024]{1,0:T(8,128)(2,1)} %nope_hbm.1, bf16[64,512]{1,0:T(8,128)(2,1)} %rope_hbm.1), custom_call_target="tpu_custom_call" | custom-call | tf_op jit(solution)/shard_map/prep/pallas_call | solution.py:390
  2.0 0.0 copy-start.2
  2.0 41.0 %all_to_all.5 = bf16[64,8,640]{2,1,0:T(8,128)(2,1)S(1)} all-to-all(bf16[64,8,640]{2,1,0:T(8,128)(2,1)} %get-tuple-element.24), channel_id=1, replica_groups={{0,6,16,22,32,38,48,54,67,69,83,85,99,101,115,117,130,132,146,148,162,1..., dimensions={0} | all-to-all | bytes 1310720 | tf_op jit(solution)/shard_map/all_to_all | solution.py:403
  43.0 2.6 %collective-permute-start.2 = (bf16[512,640]{1,0:T(8,128)(2,1)S(1)}, bf16[512,640]{1,0:T(8,128)(2,1)S(1)}, u32[]{:S(2)}, u32[]{:S(2)}) collective-permute-start(bf16[512,640]{1,0:T(8,128)(2,1)S(1)} %bitcast.2), channel_id=1, source_target_pairs={{0,3},{8,9},{1,0},{9,10},{2,1},{10,11},{3,2},{11,8},{4,7},{12,13},... | collective-permute-start | bytes 1966088 | tf_op jit(solution)/shard_map/ppermute | solution.py:406
  45.6 6.7 %collective-permute-start.3 = (bf16[512,640]{1,0:T(8,128)(2,1)S(1)}, bf16[512,640]{1,0:T(8,128)(2,1)S(1)}, u32[]{:S(2)}, u32[]{:S(2)}) collective-permute-start(bf16[512,640]{1,0:T(8,128)(2,1)S(1)} %bitcast.3), channel_id=1, source_target_pairs={{0,72},{8,448},{1,73},{9,449},{2,74},{10,450},{3,75},{11,451},{4,7... | collective-permute-start | bytes 1966088 | tf_op jit(solution)/shard_map/ppermute | solution.py:407
  52.3 2.9 %collective-permute-start = (bf16[512,640]{1,0:T(8,128)(2,1)S(1)}, bf16[512,640]{1,0:T(8,128)(2,1)S(1)}, u32[]{:S(2)}, u32[]{:S(2)}) collective-permute-start(bf16[512,640]{1,0:T(8,128)(2,1)S(1)} %bitcast.4), channel_id=1, source_target_pairs={{0,52},{8,12},{1,53},{9,13},{2,54},{10,14},{3,55},{11,15},{4,0},{1... | collective-permute-start | bytes 1966088 | tf_op jit(solution)/shard_map/ppermute | solution.py:408
  55.2 0.0 copy-done.2
  55.2 1.9 %collective-permute-start.1 = (bf16[64,1664]{1,0:T(8,128)(2,1)S(1)}, bf16[64,1664]{1,0:T(8,128)(2,1)S(1)}, u32[]{:S(2)}, u32[]{:S(2)}) collective-permute-start(bf16[64,1664]{1,0:T(8,128)(2,1)S(1)} %copy-done.2), channel_id=1, source_target_pairs={{0,8},{8,0},{1,9},{9,1},{2,10},{10,2},{3,11},{11,3},{4,12},{12,4},... | collective-permute-start | bytes 638984 | tf_op jit(solution)/shard_map/ppermute | solution.py:409
  57.2 0.0 copy-done
  57.2 1.4 %first.1 = (bf16[512,640]{1,0:T(8,128)(2,1)S(1)}, f32[512,128]{1,0:T(8,128)S(1)}, f32[512,512]{1,0:T(8,128)S(1)}, f32[512,128]{1,0:T(8,128)S(1)}, f32[512,128]{1,0:T(8,128)S(1)}) custom-call(bf16[64,1664]{1,0:T(8,128)(2,1)S(1)} %copy-done.2, bf16[8,128,512]{2,1,0:T(8,128)(2,1)S(1)} %copy-done, bf16[512,640]{1,0:T(8,128)(2,1)S(1)} %bitcast.5), custom_call_target="tpu_custom_call" | custom-call | tf_op jit(solution)/shard_map/first/pallas_call | solution.py:412
  58.6 0.0 collective-permute-done.1.sibling_ref
  58.6 0.0 collective-permute-done.2.one_ref
  58.6 2.0 %collective-permute-done.3.two_ref = bf16[512,640]{1,0:T(8,128)(2,1)S(1)} collective-permute-done((bf16[512,640]{1,0:T(8,128)(2,1)S(1)}, bf16[512,640]{1,0:T(8,128)(2,1)S(1)}, u32[]{:S(2)}, u32[]{:S(2)}) %collective-permute-start.3) | collective-permute-done | bytes 655392 | tf_op jit(solution)/shard_map/ppermute | solution.py:407
  60.6 4.8 %middle.1 = (f32[512,512]{1,0:T(8,128)S(1)}, f32[512,128]{1,0:T(8,128)S(1)}, f32[512,128]{1,0:T(8,128)S(1)}, bf16[512,640]{1,0:T(8,128)(2,1)S(1)}, f32[512,128]{...) custom-call(bf16[512,640]{1,0:T(8,128)(2,1)S(1)} %get-tuple-element.25.query_ref, ...), custom_call_target="tpu_custom_call" | custom-call | tf_op jit(solution)/shard_map/middle/pallas_call | solution.py:415
  65.4 0.0 collective-permute-done.keys_ref
  65.5 1.2 %sibling_rows.1 = bf16[512,640]{1,0:T(8,128)(2,1)S(1)} custom-call(bf16[512,640]{1,0:T(8,128)(2,1)S(1)} %get-tuple-element.36.query_ref, f32[512,128]{1,0:T(8,128)S(1)} %get-tuple-element.37.place_ref, bf16[512,640]{1,0:T(8,128)(2,1)S(1)} %collective-permute-done.keys_ref, f32[512,512]{1,0:T(8,128)S(1)} %get-tuple-element.38.old_acc_ref, ...), custom_call_target="tpu_custom_call" | custom-call | tf_op jit(solution)/shard_map/sibling_rows/pallas_call | solution.py:419
  66.7 3.2 %collective-permute-start.4 = (bf16[512,640]{1,0:T(8,128)(2,1)S(1)}, bf16[512,640]{1,0:T(8,128)(2,1)S(1)}, u32[]{:S(2)}, u32[]{:S(2)}) collective-permute-start(bf16[512,640]{1,0:T(8,128)(2,1)S(1)} %sibling_rows.1), channel_id=1, source_target_pairs={{0,8},{8,0},{1,9},{9,1},{2,10},{10,2},{3,11},{11,3},{4,12},{12,4},... | collective-permute-start | bytes 1966088 | tf_op jit(solution)/shard_map/ppermute | solution.py:422
  69.9 0.0 copy-start.1
  69.9 1.2 %own_rows.1 = (f32[512,512]{1,0:T(8,128)S(1)}, f32[512,128]{1,0:T(8,128)S(1)}, f32[512,128]{1,0:T(8,128)S(1)}) custom-call(bf16[512,640]{1,0:T(8,128)(2,1)S(1)} %get-tuple-element.25.query_ref, f32[512,128]{1,0:T(8,128)S(1)} %get-tuple-element.26.place_ref, bf16[512,640]{1,0:T(8,128)(2,1)S(1)} %collective-permute-done.keys_ref, ...), custom_call_target="tpu_custom_call" | custom-call | tf_op jit(solution)/shard_map/own_rows/pallas_call | solution.py:423
  71.1 0.4 collective-permute-done.4.got_ref
  71.6 0.0 copy-done.1
  71.6 1.1 %merge.1 = bf16[64,1024]{1,0:T(8,128)(2,1)} custom-call(f32[512,512]{1,0:T(8,128)S(1)} %get-tuple-element.33.acc_ref, f32[512,128]{1,0:T(8,128)S(1)} %get-tuple-element.34.top_ref, f32[512,128]{1,0:T(8,128)S(1)} %get-tuple-element.35.sum_ref, bf16[512,640]{1,0:T(8,128)(2,1)S(1)} %collective-permute-done.4.got_ref, bf16[8,512,128]{2,1,0:T(8,128)(2,1)S(1)} %copy-done.1), custom_call_target="tpu_custom_call" | custom-call | tf_op jit(solution)/shard_map/merge/pallas_call | solution.py:424
Async XLA Ops:
  0.0 57.2 %copy-start = (bf16[8,128,512]{2,1,0:T(8,128)(2,1)S(1)}, bf16[8,128,512]{2,1,0:T(8,128)(2,1)}, u32[]{:S(2)}) copy-start(bf16[8,128,512]{2,1,0:T(8,128)(2,1)} %key_up_ref.3) | copy-start | bytes 3145732
  2.0 53.2 %copy-start.2 = (bf16[64,1664]{1,0:T(8,128)(2,1)S(1)}, bf16[64,1664]{1,0:T(8,128)(2,1)}, u32[]{:S(2)}) copy-start(bf16[64,1664]{1,0:T(8,128)(2,1)} %get-tuple-element.23.own_ref) | copy-start | bytes 638980
  43.0 15.6 %collective-permute-start.2 = (bf16[512,640]{1,0:T(8,128)(2,1)S(1)}, bf16[512,640]{1,0:T(8,128)(2,1)S(1)}, u32[]{:S(2)}, u32[]{:S(2)}) collective-permute-start(bf16[512,640]{1,0:T(8,128)(2,1)S(1)} %bitcast.2), channel_id=1, source_target_pairs={{0,3},{8,9},{1,0},{9,10},{2,1},{10,11},{3,2},{11,8},{4,7},{12,13},... | collective-permute-start | bytes 1966088 | tf_op jit(solution)/shard_map/ppermute | solution.py:406
  45.6 15.0 %collective-permute-start.3 = (bf16[512,640]{1,0:T(8,128)(2,1)S(1)}, bf16[512,640]{1,0:T(8,128)(2,1)S(1)}, u32[]{:S(2)}, u32[]{:S(2)}) collective-permute-start(bf16[512,640]{1,0:T(8,128)(2,1)S(1)} %bitcast.3), channel_id=1, source_target_pairs={{0,72},{8,448},{1,73},{9,449},{2,74},{10,450},{3,75},{11,451},{4,7... | collective-permute-start | bytes 1966088 | tf_op jit(solution)/shard_map/ppermute | solution.py:407
  52.3 13.1 %collective-permute-start = (bf16[512,640]{1,0:T(8,128)(2,1)S(1)}, bf16[512,640]{1,0:T(8,128)(2,1)S(1)}, u32[]{:S(2)}, u32[]{:S(2)}) collective-permute-start(bf16[512,640]{1,0:T(8,128)(2,1)S(1)} %bitcast.4), channel_id=1, source_target_pairs={{0,52},{8,12},{1,53},{9,13},{2,54},{10,14},{3,55},{11,15},{4,0},{1... | collective-permute-start | bytes 1966088 | tf_op jit(solution)/shard_map/ppermute | solution.py:408
  55.2 3.4 %collective-permute-start.1 = (bf16[64,1664]{1,0:T(8,128)(2,1)S(1)}, bf16[64,1664]{1,0:T(8,128)(2,1)S(1)}, u32[]{:S(2)}, u32[]{:S(2)}) collective-permute-start(bf16[64,1664]{1,0:T(8,128)(2,1)S(1)} %copy-done.2), channel_id=1, source_target_pairs={{0,8},{8,0},{1,9},{9,1},{2,10},{10,2},{3,11},{11,3},{4,12},{12,4},... | collective-permute-start | bytes 638984 | tf_op jit(solution)/shard_map/ppermute | solution.py:409
  66.7 4.9 %collective-permute-start.4 = (bf16[512,640]{1,0:T(8,128)(2,1)S(1)}, bf16[512,640]{1,0:T(8,128)(2,1)S(1)}, u32[]{:S(2)}, u32[]{:S(2)}) collective-permute-start(bf16[512,640]{1,0:T(8,128)(2,1)S(1)} %sibling_rows.1), channel_id=1, source_target_pairs={{0,8},{8,0},{1,9},{9,1},{2,10},{10,2},{3,11},{11,3},{4,12},{12,4},... | collective-permute-start | bytes 1966088 | tf_op jit(solution)/shard_map/ppermute | solution.py:422
  69.9 1.7 %copy-start.1 = (bf16[8,512,128]{2,1,0:T(8,128)(2,1)S(1)}, bf16[8,512,128]{2,1,0:T(8,128)(2,1)}, u32[]{:S(2)}) copy-start(bf16[8,512,128]{2,1,0:T(8,128)(2,1)} %value_up_ref.1) | copy-start | bytes 3145732

commit v10 on v9

--- a/solution.py
+++ b/solution.py
@@ -241,36 +241,11 @@
     attend(query_ref, place_ref, [keys_ref], None, keep(acc_ref, top_ref, sum_ref))
 
 
-def middle_kernel(
-    query_ref,
-    place_ref,
-    sibling_ref,
-    key_up_ref,
-    keys_ref,
-    one_ref,
-    two_ref,
-    old_acc_ref,
-    old_top_ref,
-    old_sum_ref,
-    acc_ref,
-    top_ref,
-    sum_ref,
-    sibling_query_ref,
-    sibling_place_ref,
-    sibling_acc_ref,
-    sibling_top_ref,
-    sibling_sum_ref,
-):
-    project(sibling_ref, key_up_ref, sibling_query_ref, sibling_place_ref)
-    old = (old_acc_ref, old_top_ref, old_sum_ref)
-    attend(query_ref, place_ref, [one_ref, two_ref], old, keep(acc_ref, top_ref, sum_ref))
-    attend(
-        sibling_query_ref,
-        sibling_place_ref,
-        [keys_ref, one_ref, two_ref],
-        None,
-        keep(sibling_acc_ref, sibling_top_ref, sibling_sum_ref),
-    )
+def middle_kernel(one_ref, two_ref, *refs):
+    for side in range(2):
+        query_ref, place_ref, *old = refs[side * 5 : side * 5 + 5]
+        new = refs[10 + side * 3 : 13 + side * 3]
+        attend(query_ref, place_ref, [one_ref, two_ref], old, keep(*new))
 
 
 def send_kernel(
@@ -409,18 +384,15 @@
     sibling = lax.ppermute(joined, AXES, sibling_pairs)
     state = (shape((ROWS, LATENT), f32), shape((ROWS, 128), f32), shape((ROWS, 128), f32))
     rows = (shape((ROWS, WIDE), bf16), shape((ROWS, 128), f32))
-    queries, places, *carry = call(first_kernel, [VMEM] * 3, (*rows, *state), "first")(
-        joined, key_up, own_keys
-    )
-    *carry, acc, top, total = call(middle_kernel, [VMEM] * 10, (*state, *rows, *state), "middle")(
-        queries, places, sibling, key_up, own_keys, one, two, *carry
-    )
-    *carry, sibling_queries, sibling_places = carry
+    first = call(first_kernel, [VMEM] * 3, (*rows, *state), "first")
+    here = first(joined, key_up, own_keys)
+    there = first(sibling, key_up, own_keys)
+    carry = call(middle_kernel, [VMEM] * 12, (*state, *state), "middle")(one, two, *here, *there)
     send = call(send_kernel, [VMEM] * 6, shape((ROWS, WIDE), bf16), "sibling_rows")(
-        sibling_queries, sibling_places, three, acc, top, total
+        *there[:2], three, *carry[3:]
     )
     got = lax.ppermute(send, AXES, sibling_pairs)
-    own = call(own_kernel, [VMEM] * 6, state, "own_rows")(queries, places, three, *carry)
+    own = call(own_kernel, [VMEM] * 6, state, "own_rows")(*here[:2], three, *carry[:3])
     return call(
         merge_kernel, [VMEM] * 5, shape((TOK, HEADS_HERE * VDIM), bf16), "merge", 16
     )(*own, got, value_up)

time: 73 us -> 71 us (0.973)
  starting transfers between devices: 17.3 us -> 15.2 us
    ppermute x1, waiting for transfers between devices: 1.99 us -> 0.01 us  [shards(): two = lax.ppermute(own_keys, AXES, y_pairs)]
    ppermute x1, starting transfers between devices: 6.73 us -> 4.98 us  [shards(): two = lax.ppermute(own_keys, AXES, y_pairs)]
    ppermute x1, waiting for transfers between devices: 0.01 us -> 1.47 us  [shards(): one = lax.ppermute(own_keys, AXES, x_pairs)]
    ppermute x1, starting transfers between devices: 3.17 us -> 1.92 us  [shards(): got = lax.ppermute(send, AXES, sibling_pairs)]
    ppermute x1, starting transfers between devices: 2.61 us -> 3.7 us  [shards(): one = lax.ppermute(own_keys, AXES, x_pairs)]
    ppermute x1, starting transfers between devices: 2.88 us -> 1.92 us  [shards(): three = lax.ppermute(own_keys, AXES, z_pairs)]
    pallas_call x2 -> x3, Pallas kernels: 6.21 us -> 6.57 us  [the longest x1 3.82 us: shards(): call(middle_kernel, [VMEM] * 12, (*state, *state), 'middle')]
  transfers between devices with their start and end apart: 5 -> 5, of which waited for: 2 -> 2; matrix products, arithmetic and copies ran while one was open for 0% -> 0% of each run, Pallas kernels for 10% -> 11%
where the time goes in v10:
time: 71 us; the launch traced here: 70.7 us
  blocking collectives  41 us (58%)
  starting transfers between devices  15.2 us (21%)
  Pallas kernels  12.1 us (17%)
  waiting for transfers between devices  2.28 us (3%)
    all_to_all x1, blocking collectives, shards(): lax.all_to_all(sent, AXES, 0, 0, tiled=True, axis_index_groups=colours())  41 us
    ppermute x1, starting transfers between devices, shards(): two = lax.ppermute(own_keys, AXES, y_pairs)  4.98 us
    pallas_call x1, Pallas kernels, shards(): call(middle_kernel, [VMEM] * 12, (*state, *state), 'middle')  3.82 us
    ppermute x1, starting transfers between devices, shards(): one = lax.ppermute(own_keys, AXES, x_pairs)  3.7 us
    ppermute x1, starting transfers between devices, shards(): sibling = lax.ppermute(joined, AXES, sibling_pairs)  2.63 us
    pallas_call x1, Pallas kernels, shards(): call(prep_kernel, [HBM] * 5, (shape((64, 8, WIDE), bf16), shape((TOK, JOI...  1.99 us
    ppermute x1, starting transfers between devices, shards(): got = lax.ppermute(send, AXES, sibling_pairs)  1.92 us
    ppermute x1, starting transfers between devices, shards(): three = lax.ppermute(own_keys, AXES, z_pairs)  1.92 us
  transfers between devices with their start and end apart: 5, of which 2 were waited for; matrix products, arithmetic and copies ran while one was open for 0% of the time, Pallas kernels for 11%

profile of v10, /device:TPU:1, one launch (start us, length us, event | category | flops | bytes accessed | tf_op | source)
XLA Modules:
  0.0 70.7 jit_solution(12917239646255711179)
XLA Ops:
  0.0 0.0 copy-start
  0.0 2.0 %prep.1 = (bf16[64,8,640]{2,1,0:T(8,128)(2,1)}, bf16[64,1664]{1,0:T(8,128)(2,1)}) custom-call(s32[128]{0:T(128)} %span_hbm.1, bf16[8,576]{1,0:T(8,128)(2,1)} %compressed_hbm.1, f32[1,512]{1,0:T(1,128)} %bitcast.7, bf16[64,1024]{1,0:T(8,128)(2,1)} %nope_hbm.1, bf16[64,512]{1,0:T(8,128)(2,1)} %rope_hbm.1), custom_call_target="tpu_custom_call" | custom-call | tf_op jit(solution)/shard_map/prep/pallas_call | solution.py:365
  2.0 0.0 copy-start.2
  2.0 41.0 %all_to_all.5 = bf16[64,8,640]{2,1,0:T(8,128)(2,1)S(1)} all-to-all(bf16[64,8,640]{2,1,0:T(8,128)(2,1)} %get-tuple-element.27), channel_id=1, replica_groups={{0,6,16,22,32,38,48,54,67,69,83,85,99,101,115,117,130,132,146,148,162,1..., dimensions={0} | all-to-all | bytes 1310720 | tf_op jit(solution)/shard_map/all_to_all | solution.py:378
  43.0 5.0 %collective-permute-start.2 = (bf16[512,640]{1,0:T(8,128)(2,1)S(1)}, bf16[512,640]{1,0:T(8,128)(2,1)S(1)}, u32[]{:S(2)}, u32[]{:S(2)}) collective-permute-start(bf16[512,640]{1,0:T(8,128)(2,1)S(1)} %bitcast.2), channel_id=1, source_target_pairs={{0,72},{8,448},{1,73},{9,449},{2,74},{10,450},{3,75},{11,451},{4,7... | collective-permute-start | bytes 1966088 | tf_op jit(solution)/shard_map/ppermute | solution.py:382
  48.0 3.7 %collective-permute-start.1 = (bf16[512,640]{1,0:T(8,128)(2,1)S(1)}, bf16[512,640]{1,0:T(8,128)(2,1)S(1)}, u32[]{:S(2)}, u32[]{:S(2)}) collective-permute-start(bf16[512,640]{1,0:T(8,128)(2,1)S(1)} %bitcast.3), channel_id=1, source_target_pairs={{0,3},{8,9},{1,0},{9,10},{2,1},{10,11},{3,2},{11,8},{4,7},{12,13},... | collective-permute-start | bytes 1966088 | tf_op jit(solution)/shard_map/ppermute | solution.py:381
  51.7 1.9 %collective-permute-start = (bf16[512,640]{1,0:T(8,128)(2,1)S(1)}, bf16[512,640]{1,0:T(8,128)(2,1)S(1)}, u32[]{:S(2)}, u32[]{:S(2)}) collective-permute-start(bf16[512,640]{1,0:T(8,128)(2,1)S(1)} %bitcast.4), channel_id=1, source_target_pairs={{0,52},{8,12},{1,53},{9,13},{2,54},{10,14},{3,55},{11,15},{4,0},{1... | collective-permute-start | bytes 1966088 | tf_op jit(solution)/shard_map/ppermute | solution.py:383
  53.6 0.0 copy-done.2
  53.6 2.6 %collective-permute-start.3 = (bf16[64,1664]{1,0:T(8,128)(2,1)S(1)}, bf16[64,1664]{1,0:T(8,128)(2,1)S(1)}, u32[]{:S(2)}, u32[]{:S(2)}) collective-permute-start(bf16[64,1664]{1,0:T(8,128)(2,1)S(1)} %copy-done.2), channel_id=1, source_target_pairs={{0,8},{8,0},{1,9},{9,1},{2,10},{10,2},{3,11},{11,3},{4,12},{12,4},... | collective-permute-start | bytes 638984 | tf_op jit(solution)/shard_map/ppermute | solution.py:384
  56.3 0.0 copy-done
  56.3 1.4 %first.2 = (bf16[512,640]{1,0:T(8,128)(2,1)S(1)}, f32[512,128]{1,0:T(8,128)S(1)}, f32[512,512]{1,0:T(8,128)S(1)}, f32[512,128]{1,0:T(8,128)S(1)}, f32[512,128]{1,0:T(8,128)S(1)}) custom-call(bf16[64,1664]{1,0:T(8,128)(2,1)S(1)} %copy-done.2, bf16[8,128,512]{2,1,0:T(8,128)(2,1)S(1)} %copy-done, bf16[512,640]{1,0:T(8,128)(2,1)S(1)} %bitcast.5), custom_call_target="tpu_custom_call" | custom-call | tf_op jit(solution)/shard_map/first/pallas_call | solution.py:388
  57.7 0.0 collective-permute-done.3.own_ref
  57.7 1.4 %first.3 = (bf16[512,640]{1,0:T(8,128)(2,1)S(1)}, f32[512,128]{1,0:T(8,128)S(1)}, f32[512,512]{1,0:T(8,128)S(1)}, f32[512,128]{1,0:T(8,128)S(1)}, f32[512,128]{1,0:T(8,128)S(1)}) custom-call(bf16[64,1664]{1,0:T(8,128)(2,1)S(1)} %collective-permute-done.3.own_ref, bf16[8,128,512]{2,1,0:T(8,128)(2,1)S(1)} %copy-done, bf16[512,640]{1,0:T(8,128)(2,1)S(1)} %bitcast.6), custom_call_target="tpu_custom_call" | custom-call | tf_op jit(solution)/shard_map/first/pallas_call | solution.py:389
  59.0 0.0 collective-permute-done.2.two_ref
  59.1 1.5 %collective-permute-done.1.one_ref = bf16[512,640]{1,0:T(8,128)(2,1)S(1)} collective-permute-done((bf16[512,640]{1,0:T(8,128)(2,1)S(1)}, bf16[512,640]{1,0:T(8,128)(2,1)S(1)}, u32[]{:S(2)}, u32[]{:S(2)}) %collective-permute-start.1) | collective-permute-done | bytes 655392 | tf_op jit(solution)/shard_map/ppermute | solution.py:381
  60.5 3.8 %middle.1 = (f32[512,512]{1,0:T(8,128)S(1)}, f32[512,128]{1,0:T(8,128)S(1)}, f32[512,128]{1,0:T(8,128)S(1)}, f32[512,512]{1,0:T(8,128)S(1)}, f32[512,128]{1,0:T(8,128)S(1)}, /*index=5*/f32[512,128]{1,0:T(8,128)S(1)}) custom-call(bf16[512,640]{1,0:T(8,128)(2,1)S(1)} %collective-permute-done.1.one_ref, bf16[512,640]{1,0:T(8,128)(2,1)S(1)} %collective-permute-done.2.two_ref, ...), custom_call_target="tpu_custom_call" | custom-call | tf_op jit(solution)/shard_map/middle/pallas_call | solution.py:390
  64.4 0.0 collective-permute-done.keys_ref
  64.4 1.2 %sibling_rows.1 = bf16[512,640]{1,0:T(8,128)(2,1)S(1)} custom-call(bf16[512,640]{1,0:T(8,128)(2,1)S(1)} %get-tuple-element.33.refs_5_.query_ref, f32[512,128]{1,0:T(8,128)S(1)} %get-tuple-element.34.refs_6_.place_ref, bf16[512,640]{1,0:T(8,128)(2,1)S(1)} %collective-permute-done.keys_ref, f32[512,512]{1,0:T(8,128)S(1)} %get-tuple-element.44.old_acc_ref, ...), custom_call_target="tpu_custom_call" | custom-call | tf_op jit(solution)/shard_map/sibling_rows/pallas_call | solution.py:391
  65.6 1.9 %collective-permute-start.4 = (bf16[512,640]{1,0:T(8,128)(2,1)S(1)}, bf16[512,640]{1,0:T(8,128)(2,1)S(1)}, u32[]{:S(2)}, u32[]{:S(2)}) collective-permute-start(bf16[512,640]{1,0:T(8,128)(2,1)S(1)} %sibling_rows.1), channel_id=1, source_target_pairs={{0,8},{8,0},{1,9},{9,1},{2,10},{10,2},{3,11},{11,3},{4,12},{12,4},... | collective-permute-start | bytes 1966088 | tf_op jit(solution)/shard_map/ppermute | solution.py:394
  67.5 0.0 copy-start.1
  67.5 1.2 %own_rows.1 = (f32[512,512]{1,0:T(8,128)S(1)}, f32[512,128]{1,0:T(8,128)S(1)}, f32[512,128]{1,0:T(8,128)S(1)}) custom-call(bf16[512,640]{1,0:T(8,128)(2,1)S(1)} %get-tuple-element.28.refs_0_.query_ref, f32[512,128]{1,0:T(8,128)S(1)} %get-tuple-element.29.refs_1_.place_ref, bf16[512,640]{1,0:T(8,128)(2,1)S(1)} %collective-permute-done.keys_ref, ...), custom_call_target="tpu_custom_call" | custom-call | tf_op jit(solution)/shard_map/own_rows/pallas_call | solution.py:395
  68.8 0.8 %collective-permute-done.4.got_ref = bf16[512,640]{1,0:T(8,128)(2,1)S(1)} collective-permute-done((bf16[512,640]{1,0:T(8,128)(2,1)S(1)}, bf16[512,640]{1,0:T(8,128)(2,1)S(1)}, u32[]{:S(2)}, u32[]{:S(2)}) %collective-permute-start.4) | collective-permute-done | bytes 655392 | tf_op jit(solution)/shard_map/ppermute | solution.py:394
  69.6 0.0 copy-done.1
  69.6 1.1 %merge.1 = bf16[64,1024]{1,0:T(8,128)(2,1)} custom-call(f32[512,512]{1,0:T(8,128)S(1)} %get-tuple-element.41.acc_ref, f32[512,128]{1,0:T(8,128)S(1)} %get-tuple-element.42.top_ref, f32[512,128]{1,0:T(8,128)S(1)} %get-tuple-element.43.sum_ref, bf16[512,640]{1,0:T(8,128)(2,1)S(1)} %collective-permute-done.4.got_ref, bf16[8,512,128]{2,1,0:T(8,128)(2,1)S(1)} %copy-done.1), custom_call_target="tpu_custom_call" | custom-call | tf_op jit(solution)/shard_map/merge/pallas_call | solution.py:396
Async XLA Ops:
  0.0 56.3 %copy-start = (bf16[8,128,512]{2,1,0:T(8,128)(2,1)S(1)}, bf16[8,128,512]{2,1,0:T(8,128)(2,1)}, u32[]{:S(2)}) copy-start(bf16[8,128,512]{2,1,0:T(8,128)(2,1)} %key_up_ref.3) | copy-start | bytes 3145732
  2.0 51.6 %copy-start.2 = (bf16[64,1664]{1,0:T(8,128)(2,1)S(1)}, bf16[64,1664]{1,0:T(8,128)(2,1)}, u32[]{:S(2)}) copy-start(bf16[64,1664]{1,0:T(8,128)(2,1)} %get-tuple-element.26.own_ref) | copy-start | bytes 638980
  43.0 16.1 %collective-permute-start.2 = (bf16[512,640]{1,0:T(8,128)(2,1)S(1)}, bf16[512,640]{1,0:T(8,128)(2,1)S(1)}, u32[]{:S(2)}, u32[]{:S(2)}) collective-permute-start(bf16[512,640]{1,0:T(8,128)(2,1)S(1)} %bitcast.2), channel_id=1, source_target_pairs={{0,72},{8,448},{1,73},{9,449},{2,74},{10,450},{3,75},{11,451},{4,7... | collective-permute-start | bytes 1966088 | tf_op jit(solution)/shard_map/ppermute | solution.py:382
  48.0 12.5 %collective-permute-start.1 = (bf16[512,640]{1,0:T(8,128)(2,1)S(1)}, bf16[512,640]{1,0:T(8,128)(2,1)S(1)}, u32[]{:S(2)}, u32[]{:S(2)}) collective-permute-start(bf16[512,640]{1,0:T(8,128)(2,1)S(1)} %bitcast.3), channel_id=1, source_target_pairs={{0,3},{8,9},{1,0},{9,10},{2,1},{10,11},{3,2},{11,8},{4,7},{12,13},... | collective-permute-start | bytes 1966088 | tf_op jit(solution)/shard_map/ppermute | solution.py:381
  51.7 12.7 %collective-permute-start = (bf16[512,640]{1,0:T(8,128)(2,1)S(1)}, bf16[512,640]{1,0:T(8,128)(2,1)S(1)}, u32[]{:S(2)}, u32[]{:S(2)}) collective-permute-start(bf16[512,640]{1,0:T(8,128)(2,1)S(1)} %bitcast.4), channel_id=1, source_target_pairs={{0,52},{8,12},{1,53},{9,13},{2,54},{10,14},{3,55},{11,15},{4,0},{1... | collective-permute-start | bytes 1966088 | tf_op jit(solution)/shard_map/ppermute | solution.py:383
  53.6 4.0 %collective-permute-start.3 = (bf16[64,1664]{1,0:T(8,128)(2,1)S(1)}, bf16[64,1664]{1,0:T(8,128)(2,1)S(1)}, u32[]{:S(2)}, u32[]{:S(2)}) collective-permute-start(bf16[64,1664]{1,0:T(8,128)(2,1)S(1)} %copy-done.2), channel_id=1, source_target_pairs={{0,8},{8,0},{1,9},{9,1},{2,10},{10,2},{3,11},{11,3},{4,12},{12,4},... | collective-permute-start | bytes 638984 | tf_op jit(solution)/shard_map/ppermute | solution.py:384
  65.6 4.0 %collective-permute-start.4 = (bf16[512,640]{1,0:T(8,128)(2,1)S(1)}, bf16[512,640]{1,0:T(8,128)(2,1)S(1)}, u32[]{:S(2)}, u32[]{:S(2)}) collective-permute-start(bf16[512,640]{1,0:T(8,128)(2,1)S(1)} %sibling_rows.1), channel_id=1, source_target_pairs={{0,8},{8,0},{1,9},{9,1},{2,10},{10,2},{3,11},{11,3},{4,12},{12,4},... | collective-permute-start | bytes 1966088 | tf_op jit(solution)/shard_map/ppermute | solution.py:394
  67.5 2.1 %copy-start.1 = (bf16[8,512,128]{2,1,0:T(8,128)(2,1)S(1)}, bf16[8,512,128]{2,1,0:T(8,128)(2,1)}, u32[]{:S(2)}) copy-start(bf16[8,512,128]{2,1,0:T(8,128)(2,1)} %value_up_ref.1) | copy-start | bytes 3145732

commit v11 on v10

--- a/solution.py
+++ b/solution.py
@@ -241,11 +241,11 @@
     attend(query_ref, place_ref, [keys_ref], None, keep(acc_ref, top_ref, sum_ref))
 
 
-def middle_kernel(one_ref, two_ref, *refs):
+def middle_kernel(keys_ref, *refs):
     for side in range(2):
         query_ref, place_ref, *old = refs[side * 5 : side * 5 + 5]
         new = refs[10 + side * 3 : 13 + side * 3]
-        attend(query_ref, place_ref, [one_ref, two_ref], old, keep(*new))
+        attend(query_ref, place_ref, [keys_ref], old, keep(*new))
 
 
 def send_kernel(
@@ -387,7 +387,9 @@
     first = call(first_kernel, [VMEM] * 3, (*rows, *state), "first")
     here = first(joined, key_up, own_keys)
     there = first(sibling, key_up, own_keys)
-    carry = call(middle_kernel, [VMEM] * 12, (*state, *state), "middle")(one, two, *here, *there)
+    middle = call(middle_kernel, [VMEM] * 11, (*state, *state), "middle")
+    carry = middle(two, *here, *there)
+    carry = middle(one, *here[:2], *carry[:3], *there[:2], *carry[3:])
     send = call(send_kernel, [VMEM] * 6, shape((ROWS, WIDE), bf16), "sibling_rows")(
         *there[:2], three, *carry[3:]
     )

time: 71 us -> 70.9 us (level)
  waiting for transfers between devices: 2.28 us -> 1.25 us
  Pallas kernels: 12.1 us -> 12.9 us
    ppermute x1, waiting for transfers between devices: 1.47 us -> 0.01 us  [shards(): one = lax.ppermute(own_keys, AXES, x_pairs)]
    pallas_call x1 -> x2, Pallas kernels: 3.82 us -> 4.6 us  [the longest x1 2.3 us: shards(): carry = middle(one, *here[:2], *carry[:3], *there[:2], *carry[3:])]
  transfers between devices with their start and end apart: 5 -> 5, of which waited for: 2 -> 2; matrix products, arithmetic and copies ran while one was open for 0% -> 0% of each run, Pallas kernels for 11% -> 12%
where the time goes in v11:
time: 70.9 us; the launch traced here: 70.6 us
  blocking collectives  41 us (58%)
  starting transfers between devices  15.3 us (22%)
  Pallas kernels  12.9 us (18%)
  waiting for transfers between devices  1.25 us (2%)
    all_to_all x1, blocking collectives, shards(): lax.all_to_all(sent, AXES, 0, 0, tiled=True, axis_index_groups=colours())  41 us
    ppermute x1, starting transfers between devices, shards(): two = lax.ppermute(own_keys, AXES, y_pairs)  4.98 us
    ppermute x1, starting transfers between devices, shards(): one = lax.ppermute(own_keys, AXES, x_pairs)  3.7 us
    ppermute x1, starting transfers between devices, shards(): sibling = lax.ppermute(joined, AXES, sibling_pairs)  2.63 us
    pallas_call x1, Pallas kernels, shards(): carry = middle(one, *here[:2], *carry[:3], *there[:2], *carry[3:])  2.3 us
    pallas_call x1, Pallas kernels, shards(): carry = middle(two, *here, *there)  2.3 us
    ppermute x1, starting transfers between devices, shards(): got = lax.ppermute(send, AXES, sibling_pairs)  2.04 us
    pallas_call x1, Pallas kernels, shards(): call(prep_kernel, [HBM] * 5, (shape((64, 8, WIDE), bf16), shape((TOK, JOI...  1.99 us
  transfers between devices with their start and end apart: 5, of which 2 were waited for; matrix products, arithmetic and copies ran while one was open for 0% of the time, Pallas kernels for 12%

profile of v11, /device:TPU:1, one launch (start us, length us, event | category | flops | bytes accessed | tf_op | source)
XLA Modules:
  0.0 70.6 jit_solution(3152122892700717204)
XLA Ops:
  0.0 2.0 %prep.1 = (bf16[64,8,640]{2,1,0:T(8,128)(2,1)}, bf16[64,1664]{1,0:T(8,128)(2,1)}) custom-call(s32[128]{0:T(128)} %span_hbm.1, bf16[8,576]{1,0:T(8,128)(2,1)} %compressed_hbm.1, f32[1,512]{1,0:T(1,128)} %bitcast.7, bf16[64,1024]{1,0:T(8,128)(2,1)} %nope_hbm.1, bf16[64,512]{1,0:T(8,128)(2,1)} %rope_hbm.1), custom_call_target="tpu_custom_call" | custom-call | tf_op jit(solution)/shard_map/prep/pallas_call | solution.py:365
  2.0 0.0 copy-start.2
  2.0 41.0 %all_to_all.5 = bf16[64,8,640]{2,1,0:T(8,128)(2,1)S(1)} all-to-all(bf16[64,8,640]{2,1,0:T(8,128)(2,1)} %get-tuple-element.33), channel_id=1, replica_groups={{0,6,16,22,32,38,48,54,67,69,83,85,99,101,115,117,130,132,146,148,162,1..., dimensions={0} | all-to-all | bytes 1310720 | tf_op jit(solution)/shard_map/all_to_all | solution.py:378
  43.0 5.0 %collective-permute-start.2 = (bf16[512,640]{1,0:T(8,128)(2,1)S(1)}, bf16[512,640]{1,0:T(8,128)(2,1)S(1)}, u32[]{:S(2)}, u32[]{:S(2)}) collective-permute-start(bf16[512,640]{1,0:T(8,128)(2,1)S(1)} %bitcast.2), channel_id=1, source_target_pairs={{0,72},{8,448},{1,73},{9,449},{2,74},{10,450},{3,75},{11,451},{4,7... | collective-permute-start | bytes 1966088 | tf_op jit(solution)/shard_map/ppermute | solution.py:382
  48.0 3.7 %collective-permute-start.1 = (bf16[512,640]{1,0:T(8,128)(2,1)S(1)}, bf16[512,640]{1,0:T(8,128)(2,1)S(1)}, u32[]{:S(2)}, u32[]{:S(2)}) collective-permute-start(bf16[512,640]{1,0:T(8,128)(2,1)S(1)} %bitcast.3), channel_id=1, source_target_pairs={{0,3},{8,9},{1,0},{9,10},{2,1},{10,11},{3,2},{11,8},{4,7},{12,13},... | collective-permute-start | bytes 1966088 | tf_op jit(solution)/shard_map/ppermute | solution.py:381
  51.7 1.9 %collective-permute-start = (bf16[512,640]{1,0:T(8,128)(2,1)S(1)}, bf16[512,640]{1,0:T(8,128)(2,1)S(1)}, u32[]{:S(2)}, u32[]{:S(2)}) collective-permute-start(bf16[512,640]{1,0:T(8,128)(2,1)S(1)} %bitcast.4), channel_id=1, source_target_pairs={{0,52},{8,12},{1,53},{9,13},{2,54},{10,14},{3,55},{11,15},{4,0},{1... | collective-permute-start | bytes 1966088 | tf_op jit(solution)/shard_map/ppermute | solution.py:383
  53.6 0.0 copy-done.2
  53.6 2.6 %collective-permute-start.3 = (bf16[64,1664]{1,0:T(8,128)(2,1)S(1)}, bf16[64,1664]{1,0:T(8,128)(2,1)S(1)}, u32[]{:S(2)}, u32[]{:S(2)}) collective-permute-start(bf16[64,1664]{1,0:T(8,128)(2,1)S(1)} %copy-done.2), channel_id=1, source_target_pairs={{0,8},{8,0},{1,9},{9,1},{2,10},{10,2},{3,11},{11,3},{4,12},{12,4},... | collective-permute-start | bytes 638984 | tf_op jit(solution)/shard_map/ppermute | solution.py:384
  56.3 0.0 copy-done
  56.3 1.4 %first.2 = (bf16[512,640]{1,0:T(8,128)(2,1)S(1)}, f32[512,128]{1,0:T(8,128)S(1)}, f32[512,512]{1,0:T(8,128)S(1)}, f32[512,128]{1,0:T(8,128)S(1)}, f32[512,128]{1,0:T(8,128)S(1)}) custom-call(bf16[64,1664]{1,0:T(8,128)(2,1)S(1)} %copy-done.2, bf16[8,128,512]{2,1,0:T(8,128)(2,1)S(1)} %copy-done, bf16[512,640]{1,0:T(8,128)(2,1)S(1)} %bitcast.5), custom_call_target="tpu_custom_call" | custom-call | tf_op jit(solution)/shard_map/first/pallas_call | solution.py:388
  57.6 0.0 collective-permute-done.3.own_ref
  57.7 1.4 %first.3 = (bf16[512,640]{1,0:T(8,128)(2,1)S(1)}, f32[512,128]{1,0:T(8,128)S(1)}, f32[512,512]{1,0:T(8,128)S(1)}, f32[512,128]{1,0:T(8,128)S(1)}, f32[512,128]{1,0:T(8,128)S(1)}) custom-call(bf16[64,1664]{1,0:T(8,128)(2,1)S(1)} %collective-permute-done.3.own_ref, bf16[8,128,512]{2,1,0:T(8,128)(2,1)S(1)} %copy-done, bf16[512,640]{1,0:T(8,128)(2,1)S(1)} %bitcast.6), custom_call_target="tpu_custom_call" | custom-call | tf_op jit(solution)/shard_map/first/pallas_call | solution.py:389
  59.0 0.0 collective-permute-done.2.keys_ref
  59.0 2.3 %middle.2 = (f32[512,512]{1,0:T(8,128)S(1)}, f32[512,128]{1,0:T(8,128)S(1)}, f32[512,128]{1,0:T(8,128)S(1)}, f32[512,512]{1,0:T(8,128)S(1)}, f32[512,128]{1,0:T(8,128)S(1)}, /*index=5*/f32[512,128]{1,0:T(8,128)S(1)}) custom-call(bf16[512,640]{1,0:T(8,128)(2,1)S(1)} %collective-permute-done.2.keys_ref, ...), custom_call_target="tpu_custom_call" | custom-call | tf_op jit(solution)/shard_map/middle/pallas_call | solution.py:391
  61.4 0.0 collective-permute-done.1.keys_ref
  61.4 2.3 %middle.3 = (f32[512,512]{1,0:T(8,128)S(1)}, f32[512,128]{1,0:T(8,128)S(1)}, f32[512,128]{1,0:T(8,128)S(1)}, f32[512,512]{1,0:T(8,128)S(1)}, f32[512,128]{1,0:T(8,128)S(1)}, /*index=5*/f32[512,128]{1,0:T(8,128)S(1)}) custom-call(bf16[512,640]{1,0:T(8,128)(2,1)S(1)} %collective-permute-done.1.keys_ref, ...), custom_call_target="tpu_custom_call" | custom-call | tf_op jit(solution)/shard_map/middle/pallas_call | solution.py:392
  63.7 0.6 collective-permute-done.keys_ref
  64.2 1.2 %sibling_rows.1 = bf16[512,640]{1,0:T(8,128)(2,1)S(1)} custom-call(bf16[512,640]{1,0:T(8,128)(2,1)S(1)} %get-tuple-element.39.refs_5_.query_ref, f32[512,128]{1,0:T(8,128)S(1)} %get-tuple-element.40.refs_6_.place_ref, bf16[512,640]{1,0:T(8,128)(2,1)S(1)} %collective-permute-done.keys_ref, f32[512,512]{1,0:T(8,128)S(1)} %get-tuple-element.56.old_acc_ref, ...), custom_call_target="tpu_custom_call" | custom-call | tf_op jit(solution)/shard_map/sibling_rows/pallas_call | solution.py:393
  65.4 2.0 %collective-permute-start.4 = (bf16[512,640]{1,0:T(8,128)(2,1)S(1)}, bf16[512,640]{1,0:T(8,128)(2,1)S(1)}, u32[]{:S(2)}, u32[]{:S(2)}) collective-permute-start(bf16[512,640]{1,0:T(8,128)(2,1)S(1)} %sibling_rows.1), channel_id=1, source_target_pairs={{0,8},{8,0},{1,9},{9,1},{2,10},{10,2},{3,11},{11,3},{4,12},{12,4},... | collective-permute-start | bytes 1966088 | tf_op jit(solution)/shard_map/ppermute | solution.py:396
  67.5 0.0 copy-start.1
  67.5 1.2 %own_rows.1 = (f32[512,512]{1,0:T(8,128)S(1)}, f32[512,128]{1,0:T(8,128)S(1)}, f32[512,128]{1,0:T(8,128)S(1)}) custom-call(bf16[512,640]{1,0:T(8,128)(2,1)S(1)} %get-tuple-element.34.refs_0_.query_ref, f32[512,128]{1,0:T(8,128)S(1)} %get-tuple-element.35.refs_1_.place_ref, bf16[512,640]{1,0:T(8,128)(2,1)S(1)} %collective-permute-done.keys_ref, ...), custom_call_target="tpu_custom_call" | custom-call | tf_op jit(solution)/shard_map/own_rows/pallas_call | solution.py:397
  68.8 0.7 collective-permute-done.4.got_ref
  69.4 0.0 copy-done.1
  69.4 1.1 %merge.1 = bf16[64,1024]{1,0:T(8,128)(2,1)} custom-call(f32[512,512]{1,0:T(8,128)S(1)} %get-tuple-element.53.acc_ref, f32[512,128]{1,0:T(8,128)S(1)} %get-tuple-element.54.top_ref, f32[512,128]{1,0:T(8,128)S(1)} %get-tuple-element.55.sum_ref, bf16[512,640]{1,0:T(8,128)(2,1)S(1)} %collective-permute-done.4.got_ref, bf16[8,512,128]{2,1,0:T(8,128)(2,1)S(1)} %copy-done.1), custom_call_target="tpu_custom_call" | custom-call | tf_op jit(solution)/shard_map/merge/pallas_call | solution.py:398
  (1 shorter events, 0.0 us)
Async XLA Ops:
  0.0 56.3 %copy-start = (bf16[8,128,512]{2,1,0:T(8,128)(2,1)S(1)}, bf16[8,128,512]{2,1,0:T(8,128)(2,1)}, u32[]{:S(2)}) copy-start(bf16[8,128,512]{2,1,0:T(8,128)(2,1)} %key_up_ref.3) | copy-start | bytes 3145732
  2.0 51.6 %copy-start.2 = (bf16[64,1664]{1,0:T(8,128)(2,1)S(1)}, bf16[64,1664]{1,0:T(8,128)(2,1)}, u32[]{:S(2)}) copy-start(bf16[64,1664]{1,0:T(8,128)(2,1)} %get-tuple-element.32.own_ref) | copy-start | bytes 638980
  43.0 16.1 %collective-permute-start.2 = (bf16[512,640]{1,0:T(8,128)(2,1)S(1)}, bf16[512,640]{1,0:T(8,128)(2,1)S(1)}, u32[]{:S(2)}, u32[]{:S(2)}) collective-permute-start(bf16[512,640]{1,0:T(8,128)(2,1)S(1)} %bitcast.2), channel_id=1, source_target_pairs={{0,72},{8,448},{1,73},{9,449},{2,74},{10,450},{3,75},{11,451},{4,7... | collective-permute-start | bytes 1966088 | tf_op jit(solution)/shard_map/ppermute | solution.py:382
  48.0 13.4 %collective-permute-start.1 = (bf16[512,640]{1,0:T(8,128)(2,1)S(1)}, bf16[512,640]{1,0:T(8,128)(2,1)S(1)}, u32[]{:S(2)}, u32[]{:S(2)}) collective-permute-start(bf16[512,640]{1,0:T(8,128)(2,1)S(1)} %bitcast.3), channel_id=1, source_target_pairs={{0,3},{8,9},{1,0},{9,10},{2,1},{10,11},{3,2},{11,8},{4,7},{12,13},... | collective-permute-start | bytes 1966088 | tf_op jit(solution)/shard_map/ppermute | solution.py:381
  51.7 12.5 %collective-permute-start = (bf16[512,640]{1,0:T(8,128)(2,1)S(1)}, bf16[512,640]{1,0:T(8,128)(2,1)S(1)}, u32[]{:S(2)}, u32[]{:S(2)}) collective-permute-start(bf16[512,640]{1,0:T(8,128)(2,1)S(1)} %bitcast.4), channel_id=1, source_target_pairs={{0,52},{8,12},{1,53},{9,13},{2,54},{10,14},{3,55},{11,15},{4,0},{1... | collective-permute-start | bytes 1966088 | tf_op jit(solution)/shard_map/ppermute | solution.py:383
  53.6 4.0 %collective-permute-start.3 = (bf16[64,1664]{1,0:T(8,128)(2,1)S(1)}, bf16[64,1664]{1,0:T(8,128)(2,1)S(1)}, u32[]{:S(2)}, u32[]{:S(2)}) collective-permute-start(bf16[64,1664]{1,0:T(8,128)(2,1)S(1)} %copy-done.2), channel_id=1, source_target_pairs={{0,8},{8,0},{1,9},{9,1},{2,10},{10,2},{3,11},{11,3},{4,12},{12,4},... | collective-permute-start | bytes 638984 | tf_op jit(solution)/shard_map/ppermute | solution.py:384
  65.4 4.0 %collective-permute-start.4 = (bf16[512,640]{1,0:T(8,128)(2,1)S(1)}, bf16[512,640]{1,0:T(8,128)(2,1)S(1)}, u32[]{:S(2)}, u32[]{:S(2)}) collective-permute-start(bf16[512,640]{1,0:T(8,128)(2,1)S(1)} %sibling_rows.1), channel_id=1, source_target_pairs={{0,8},{8,0},{1,9},{9,1},{2,10},{10,2},{3,11},{11,3},{4,12},{12,4},... | collective-permute-start | bytes 1966088 | tf_op jit(solution)/shard_map/ppermute | solution.py:396
  67.5 1.9 %copy-start.1 = (bf16[8,512,128]{2,1,0:T(8,128)(2,1)S(1)}, bf16[8,512,128]{2,1,0:T(8,128)(2,1)}, u32[]{:S(2)}) copy-start(bf16[8,512,128]{2,1,0:T(8,128)(2,1)} %value_up_ref.1) | copy-start | bytes 3145732

commit v12 on v11

--- a/solution.py
+++ b/solution.py
@@ -378,9 +378,9 @@
     own_keys = lax.all_to_all(
         sent, AXES, 0, 0, tiled=True, axis_index_groups=colours()
     ).reshape(512, WIDE)
-    one = lax.ppermute(own_keys, AXES, x_pairs)
+    one = lax.ppermute(own_keys, AXES, z_pairs)
     two = lax.ppermute(own_keys, AXES, y_pairs)
-    three = lax.ppermute(own_keys, AXES, z_pairs)
+    three = lax.ppermute(own_keys, AXES, x_pairs)
     sibling = lax.ppermute(joined, AXES, sibling_pairs)
     state = (shape((ROWS, LATENT), f32), shape((ROWS, 128), f32), shape((ROWS, 128), f32))
     rows = (shape((ROWS, WIDE), bf16), shape((ROWS, 128), f32))

time: 70.9 us -> 70.4 us (level)
  no operation moved by 1% of the time
where the time goes in v12:
time: 70.4 us; the launch traced here: 70.1 us
  blocking collectives  41 us (58%)
  starting transfers between devices  15.2 us (22%)
  Pallas kernels  12.9 us (18%)
  waiting for transfers between devices  0.88 us (1%)
    all_to_all x1, blocking collectives, shards(): lax.all_to_all(sent, AXES, 0, 0, tiled=True, axis_index_groups=colours())  41 us
    ppermute x1, starting transfers between devices, shards(): two = lax.ppermute(own_keys, AXES, y_pairs)  4.98 us
    ppermute x1, starting transfers between devices, shards(): one = lax.ppermute(own_keys, AXES, z_pairs)  3.21 us
    ppermute x1, starting transfers between devices, shards(): sibling = lax.ppermute(joined, AXES, sibling_pairs)  2.63 us
    ppermute x1, starting transfers between devices, shards(): three = lax.ppermute(own_keys, AXES, x_pairs)  2.41 us
    pallas_call x1, Pallas kernels, shards(): carry = middle(one, *here[:2], *carry[:3], *there[:2], *carry[3:])  2.3 us
    pallas_call x1, Pallas kernels, shards(): carry = middle(two, *here, *there)  2.3 us
    pallas_call x1, Pallas kernels, shards(): call(prep_kernel, [HBM] * 5, (shape((64, 8, WIDE), bf16), shape((TOK, JOI...  1.99 us
  transfers between devices with their start and end apart: 5, of which 2 were waited for; matrix products, arithmetic and copies ran while one was open for 0% of the time, Pallas kernels for 12%

profile of v12, /device:TPU:1, one launch (start us, length us, event | category | flops | bytes accessed | tf_op | source)
XLA Modules:
  0.0 70.1 jit_solution(6193538633912706884)
XLA Ops:
  0.0 2.0 %prep.1 = (bf16[64,8,640]{2,1,0:T(8,128)(2,1)}, bf16[64,1664]{1,0:T(8,128)(2,1)}) custom-call(s32[128]{0:T(128)} %span_hbm.1, bf16[8,576]{1,0:T(8,128)(2,1)} %compressed_hbm.1, f32[1,512]{1,0:T(1,128)} %bitcast.7, bf16[64,1024]{1,0:T(8,128)(2,1)} %nope_hbm.1, bf16[64,512]{1,0:T(8,128)(2,1)} %rope_hbm.1), custom_call_target="tpu_custom_call" | custom-call | tf_op jit(solution)/shard_map/prep/pallas_call | solution.py:365
  2.0 0.0 copy-start.2
  2.0 41.0 %all_to_all.5 = bf16[64,8,640]{2,1,0:T(8,128)(2,1)S(1)} all-to-all(bf16[64,8,640]{2,1,0:T(8,128)(2,1)} %get-tuple-element.33), channel_id=1, replica_groups={{0,6,16,22,32,38,48,54,67,69,83,85,99,101,115,117,130,132,146,148,162,1..., dimensions={0} | all-to-all | bytes 1310720 | tf_op jit(solution)/shard_map/all_to_all | solution.py:378
  43.0 5.0 %collective-permute-start.2 = (bf16[512,640]{1,0:T(8,128)(2,1)S(1)}, bf16[512,640]{1,0:T(8,128)(2,1)S(1)}, u32[]{:S(2)}, u32[]{:S(2)}) collective-permute-start(bf16[512,640]{1,0:T(8,128)(2,1)S(1)} %bitcast.2), channel_id=1, source_target_pairs={{0,72},{8,448},{1,73},{9,449},{2,74},{10,450},{3,75},{11,451},{4,7... | collective-permute-start | bytes 1966088 | tf_op jit(solution)/shard_map/ppermute | solution.py:382
  48.0 3.2 %collective-permute-start.1 = (bf16[512,640]{1,0:T(8,128)(2,1)S(1)}, bf16[512,640]{1,0:T(8,128)(2,1)S(1)}, u32[]{:S(2)}, u32[]{:S(2)}) collective-permute-start(bf16[512,640]{1,0:T(8,128)(2,1)S(1)} %bitcast.3), channel_id=1, source_target_pairs={{0,52},{8,12},{1,53},{9,13},{2,54},{10,14},{3,55},{11,15},{4,0},{1... | collective-permute-start | bytes 1966088 | tf_op jit(solution)/shard_map/ppermute | solution.py:381
  51.2 2.4 %collective-permute-start = (bf16[512,640]{1,0:T(8,128)(2,1)S(1)}, bf16[512,640]{1,0:T(8,128)(2,1)S(1)}, u32[]{:S(2)}, u32[]{:S(2)}) collective-permute-start(bf16[512,640]{1,0:T(8,128)(2,1)S(1)} %bitcast.4), channel_id=1, source_target_pairs={{0,3},{8,9},{1,0},{9,10},{2,1},{10,11},{3,2},{11,8},{4,7},{12,13},... | collective-permute-start | bytes 1966088 | tf_op jit(solution)/shard_map/ppermute | solution.py:383
  53.6 0.0 copy-done.2
  53.6 2.6 %collective-permute-start.3 = (bf16[64,1664]{1,0:T(8,128)(2,1)S(1)}, bf16[64,1664]{1,0:T(8,128)(2,1)S(1)}, u32[]{:S(2)}, u32[]{:S(2)}) collective-permute-start(bf16[64,1664]{1,0:T(8,128)(2,1)S(1)} %copy-done.2), channel_id=1, source_target_pairs={{0,8},{8,0},{1,9},{9,1},{2,10},{10,2},{3,11},{11,3},{4,12},{12,4},... | collective-permute-start | bytes 638984 | tf_op jit(solution)/shard_map/ppermute | solution.py:384
  56.3 0.0 copy-done
  56.3 1.4 %first.2 = (bf16[512,640]{1,0:T(8,128)(2,1)S(1)}, f32[512,128]{1,0:T(8,128)S(1)}, f32[512,512]{1,0:T(8,128)S(1)}, f32[512,128]{1,0:T(8,128)S(1)}, f32[512,128]{1,0:T(8,128)S(1)}) custom-call(bf16[64,1664]{1,0:T(8,128)(2,1)S(1)} %copy-done.2, bf16[8,128,512]{2,1,0:T(8,128)(2,1)S(1)} %copy-done, bf16[512,640]{1,0:T(8,128)(2,1)S(1)} %bitcast.5), custom_call_target="tpu_custom_call" | custom-call | tf_op jit(solution)/shard_map/first/pallas_call | solution.py:388
  57.6 0.0 collective-permute-done.3.own_ref
  57.7 1.4 %first.3 = (bf16[512,640]{1,0:T(8,128)(2,1)S(1)}, f32[512,128]{1,0:T(8,128)S(1)}, f32[512,512]{1,0:T(8,128)S(1)}, f32[512,128]{1,0:T(8,128)S(1)}, f32[512,128]{1,0:T(8,128)S(1)}) custom-call(bf16[64,1664]{1,0:T(8,128)(2,1)S(1)} %collective-permute-done.3.own_ref, bf16[8,128,512]{2,1,0:T(8,128)(2,1)S(1)} %copy-done, bf16[512,640]{1,0:T(8,128)(2,1)S(1)} %bitcast.6), custom_call_target="tpu_custom_call" | custom-call | tf_op jit(solution)/shard_map/first/pallas_call | solution.py:389
  59.0 0.0 collective-permute-done.2.keys_ref
  59.0 2.3 %middle.2 = (f32[512,512]{1,0:T(8,128)S(1)}, f32[512,128]{1,0:T(8,128)S(1)}, f32[512,128]{1,0:T(8,128)S(1)}, f32[512,512]{1,0:T(8,128)S(1)}, f32[512,128]{1,0:T(8,128)S(1)}, /*index=5*/f32[512,128]{1,0:T(8,128)S(1)}) custom-call(bf16[512,640]{1,0:T(8,128)(2,1)S(1)} %collective-permute-done.2.keys_ref, ...), custom_call_target="tpu_custom_call" | custom-call | tf_op jit(solution)/shard_map/middle/pallas_call | solution.py:391
  61.4 0.0 collective-permute-done.1.keys_ref
  61.4 2.3 %middle.3 = (f32[512,512]{1,0:T(8,128)S(1)}, f32[512,128]{1,0:T(8,128)S(1)}, f32[512,128]{1,0:T(8,128)S(1)}, f32[512,512]{1,0:T(8,128)S(1)}, f32[512,128]{1,0:T(8,128)S(1)}, /*index=5*/f32[512,128]{1,0:T(8,128)S(1)}) custom-call(bf16[512,640]{1,0:T(8,128)(2,1)S(1)} %collective-permute-done.1.keys_ref, ...), custom_call_target="tpu_custom_call" | custom-call | tf_op jit(solution)/shard_map/middle/pallas_call | solution.py:392
  63.7 0.1 collective-permute-done.keys_ref
  63.7 1.2 %sibling_rows.1 = bf16[512,640]{1,0:T(8,128)(2,1)S(1)} custom-call(bf16[512,640]{1,0:T(8,128)(2,1)S(1)} %get-tuple-element.39.refs_5_.query_ref, f32[512,128]{1,0:T(8,128)S(1)} %get-tuple-element.40.refs_6_.place_ref, bf16[512,640]{1,0:T(8,128)(2,1)S(1)} %collective-permute-done.keys_ref, f32[512,512]{1,0:T(8,128)S(1)} %get-tuple-element.56.old_acc_ref, ...), custom_call_target="tpu_custom_call" | custom-call | tf_op jit(solution)/shard_map/sibling_rows/pallas_call | solution.py:393
  65.0 1.9 %collective-permute-start.4 = (bf16[512,640]{1,0:T(8,128)(2,1)S(1)}, bf16[512,640]{1,0:T(8,128)(2,1)S(1)}, u32[]{:S(2)}, u32[]{:S(2)}) collective-permute-start(bf16[512,640]{1,0:T(8,128)(2,1)S(1)} %sibling_rows.1), channel_id=1, source_target_pairs={{0,8},{8,0},{1,9},{9,1},{2,10},{10,2},{3,11},{11,3},{4,12},{12,4},... | collective-permute-start | bytes 1966088 | tf_op jit(solution)/shard_map/ppermute | solution.py:396
  66.9 0.0 copy-start.1
  66.9 1.2 %own_rows.1 = (f32[512,512]{1,0:T(8,128)S(1)}, f32[512,128]{1,0:T(8,128)S(1)}, f32[512,128]{1,0:T(8,128)S(1)}) custom-call(bf16[512,640]{1,0:T(8,128)(2,1)S(1)} %get-tuple-element.34.refs_0_.query_ref, f32[512,128]{1,0:T(8,128)S(1)} %get-tuple-element.35.refs_1_.place_ref, bf16[512,640]{1,0:T(8,128)(2,1)S(1)} %collective-permute-done.keys_ref, ...), custom_call_target="tpu_custom_call" | custom-call | tf_op jit(solution)/shard_map/own_rows/pallas_call | solution.py:397
  68.1 0.8 %collective-permute-done.4.got_ref = bf16[512,640]{1,0:T(8,128)(2,1)S(1)} collective-permute-done((bf16[512,640]{1,0:T(8,128)(2,1)S(1)}, bf16[512,640]{1,0:T(8,128)(2,1)S(1)}, u32[]{:S(2)}, u32[]{:S(2)}) %collective-permute-start.4) | collective-permute-done | bytes 655392 | tf_op jit(solution)/shard_map/ppermute | solution.py:396
  68.9 0.0 copy-done.1
  69.0 1.1 %merge.1 = bf16[64,1024]{1,0:T(8,128)(2,1)} custom-call(f32[512,512]{1,0:T(8,128)S(1)} %get-tuple-element.53.acc_ref, f32[512,128]{1,0:T(8,128)S(1)} %get-tuple-element.54.top_ref, f32[512,128]{1,0:T(8,128)S(1)} %get-tuple-element.55.sum_ref, bf16[512,640]{1,0:T(8,128)(2,1)S(1)} %collective-permute-done.4.got_ref, bf16[8,512,128]{2,1,0:T(8,128)(2,1)S(1)} %copy-done.1), custom_call_target="tpu_custom_call" | custom-call | tf_op jit(solution)/shard_map/merge/pallas_call | solution.py:398
  (1 shorter events, 0.0 us)
Async XLA Ops:
  0.0 56.3 %copy-start = (bf16[8,128,512]{2,1,0:T(8,128)(2,1)S(1)}, bf16[8,128,512]{2,1,0:T(8,128)(2,1)}, u32[]{:S(2)}) copy-start(bf16[8,128,512]{2,1,0:T(8,128)(2,1)} %key_up_ref.3) | copy-start | bytes 3145732
  2.0 51.6 %copy-start.2 = (bf16[64,1664]{1,0:T(8,128)(2,1)S(1)}, bf16[64,1664]{1,0:T(8,128)(2,1)}, u32[]{:S(2)}) copy-start(bf16[64,1664]{1,0:T(8,128)(2,1)} %get-tuple-element.32.own_ref) | copy-start | bytes 638980
  43.0 16.1 %collective-permute-start.2 = (bf16[512,640]{1,0:T(8,128)(2,1)S(1)}, bf16[512,640]{1,0:T(8,128)(2,1)S(1)}, u32[]{:S(2)}, u32[]{:S(2)}) collective-permute-start(bf16[512,640]{1,0:T(8,128)(2,1)S(1)} %bitcast.2), channel_id=1, source_target_pairs={{0,72},{8,448},{1,73},{9,449},{2,74},{10,450},{3,75},{11,451},{4,7... | collective-permute-start | bytes 1966088 | tf_op jit(solution)/shard_map/ppermute | solution.py:382
  48.0 13.4 %collective-permute-start.1 = (bf16[512,640]{1,0:T(8,128)(2,1)S(1)}, bf16[512,640]{1,0:T(8,128)(2,1)S(1)}, u32[]{:S(2)}, u32[]{:S(2)}) collective-permute-start(bf16[512,640]{1,0:T(8,128)(2,1)S(1)} %bitcast.3), channel_id=1, source_target_pairs={{0,52},{8,12},{1,53},{9,13},{2,54},{10,14},{3,55},{11,15},{4,0},{1... | collective-permute-start | bytes 1966088 | tf_op jit(solution)/shard_map/ppermute | solution.py:381
  51.2 12.5 %collective-permute-start = (bf16[512,640]{1,0:T(8,128)(2,1)S(1)}, bf16[512,640]{1,0:T(8,128)(2,1)S(1)}, u32[]{:S(2)}, u32[]{:S(2)}) collective-permute-start(bf16[512,640]{1,0:T(8,128)(2,1)S(1)} %bitcast.4), channel_id=1, source_target_pairs={{0,3},{8,9},{1,0},{9,10},{2,1},{10,11},{3,2},{11,8},{4,7},{12,13},... | collective-permute-start | bytes 1966088 | tf_op jit(solution)/shard_map/ppermute | solution.py:383
  53.6 4.0 %collective-permute-start.3 = (bf16[64,1664]{1,0:T(8,128)(2,1)S(1)}, bf16[64,1664]{1,0:T(8,128)(2,1)S(1)}, u32[]{:S(2)}, u32[]{:S(2)}) collective-permute-start(bf16[64,1664]{1,0:T(8,128)(2,1)S(1)} %copy-done.2), channel_id=1, source_target_pairs={{0,8},{8,0},{1,9},{9,1},{2,10},{10,2},{3,11},{11,3},{4,12},{12,4},... | collective-permute-start | bytes 638984 | tf_op jit(solution)/shard_map/ppermute | solution.py:384
  65.0 4.0 %collective-permute-start.4 = (bf16[512,640]{1,0:T(8,128)(2,1)S(1)}, bf16[512,640]{1,0:T(8,128)(2,1)S(1)}, u32[]{:S(2)}, u32[]{:S(2)}) collective-permute-start(bf16[512,640]{1,0:T(8,128)(2,1)S(1)} %sibling_rows.1), channel_id=1, source_target_pairs={{0,8},{8,0},{1,9},{9,1},{2,10},{10,2},{3,11},{11,3},{4,12},{12,4},... | collective-permute-start | bytes 1966088 | tf_op jit(solution)/shard_map/ppermute | solution.py:396
  66.9 2.1 %copy-start.1 = (bf16[8,512,128]{2,1,0:T(8,128)(2,1)S(1)}, bf16[8,512,128]{2,1,0:T(8,128)(2,1)}, u32[]{:S(2)}) copy-start(bf16[8,512,128]{2,1,0:T(8,128)(2,1)} %value_up_ref.1) | copy-start | bytes 3145732
